TPU v7x, 32 devices: a whole 2x2x4 slice. The times are simulated.
32 devices in a mesh: res: 8 (over z, y), nbr: 4 (over x, core).
Axes of the slice: x: 2, y: 2, z: 4, core: 2. Of those that a mesh axis runs over, the one named last changes fastest.
Arguments:
- nodes: float32 [1024, 512], P(('res', 'nbr')), may hold values from -6 to 6
- edges: float32 [1024, 60, 192], P('res', 'nbr'), may hold values from -6 to 6
- protein_ids: int32 [1024], P(('res', 'nbr')), may hold values from 0 to 5, as said below
- time_index: int32 [6], replicated, may hold values from 0 to 127
- neighbors: int32 [1024, 60], P('res', 'nbr'), may hold values from 0 to 1023, as said below
- edge_mask: int32 [1024, 60], P('res', 'nbr'), may hold values from 0 to 1, as said below
- time_table: float32 [128, 512], P('res', 'nbr'), may hold values from -3 to 3
- msg_in: float32 [2, 1216, 512], P(None, 'res', 'nbr'), may hold values from -0.15625 to 0.15625
- msg_mid: float32 [2, 512, 512], P(None, 'res', 'nbr'), may hold values from -0.25 to 0.25
- msg_out: float32 [2, 512, 512], P(None, 'res', 'nbr'), may hold values from -0.5 to 0.5
- ffn_in: float32 [2, 512, 2048], P(None, 'res', 'nbr'), may hold values from -0.25 to 0.25
- ffn_out: float32 [2, 2048, 512], P(None, 'nbr', 'res'), may hold values from -0.125 to 0.125
- edge_in: float32 [2, 1216, 192], P(None, 'res', 'nbr'), may hold values from -0.15625 to 0.15625
- edge_hidden: float32 [2, 2, 192, 192], P(None, None, 'res', 'nbr'), may hold values from -0.4375 to 0.4375
- node_gains: float32 [2, 2, 512], replicated, may hold values from 0.25 to 1.75
- node_biases: float32 [2, 6, 512], replicated, may hold values from -1 to 1
- ffn_bias: float32 [2, 2048], replicated, may hold values from -1 to 1
- edge_gains: float32 [2, 192], replicated, may hold values from 0.25 to 1.75
- edge_biases: float32 [2, 4, 192], replicated, may hold values from -1 to 1
- d_nodes: float32 [1024, 512], P(('res', 'nbr')), may hold values from -6 to 6
- d_edges: float32 [1024, 60, 192], P('res', 'nbr'), may hold values from -6 to 6
Outputs:
- nodes_out: float32 [1024, 512], P(('res', 'nbr'))
- edges_out: float32 [1024, 60, 192], P('res', 'nbr')
- g_nodes: float32 [1024, 512], P(('res', 'nbr'))
- g_edges: float32 [1024, 60, 192], P('res', 'nbr')
- g_time_table: float32 [128, 512], P('res', 'nbr')
- g_msg_in: float32 [2, 1216, 512], P(None, 'res', 'nbr')
- g_msg_mid: float32 [2, 512, 512], P(None, 'res', 'nbr')
- g_msg_out: float32 [2, 512, 512], P(None, 'res', 'nbr')
- g_ffn_in: float32 [2, 512, 2048], P(None, 'res', 'nbr')
- g_ffn_out: float32 [2, 2048, 512], P(None, 'nbr', 'res')
- g_edge_in: float32 [2, 1216, 192], P(None, 'res', 'nbr')
- g_edge_hidden: float32 [2, 2, 192, 192], P(None, None, 'res', 'nbr')
- g_node_gains: float32 [2, 2, 512], replicated
- g_node_biases: float32 [2, 6, 512], replicated
- g_ffn_bias: float32 [2, 2048], replicated
- g_edge_gains: float32 [2, 192], replicated
- g_edge_biases: float32 [2, 4, 192], replicated
Inputs may be any that keep to these rules, and one draw needn't show every extreme that they name: `protein_ids`: protein numbers never fall along the residues and each protein covers a run of one or more residues; one protein covers residues of every index of res. `neighbors`: every neighbour lies in the same protein as its residue and at most 128 positions from it. `edge_mask`: slot 0 of every residue is used.
All inputs are finite; a program needn't handle non-finite values.
Results may differ from a plain program's by a relative error of at most 0.02.
Values may be sent and summed in bfloat16 or wider, within the bound.
A program may use at most 256 MiB of HBM per device.

v0:
```python
import jax
import jax.numpy as jnp
from jax import lax
from jax.sharding import PartitionSpec as P

NORM_EPS = 1e-05


def padded(cells, sides, width):
    for axis, dim in sides:
        count = lax.axis_size(axis)
        ends = count - 1
        head = lax.slice_in_dim(cells, 0, width, axis=dim)
        tail = lax.slice_in_dim(cells, cells.shape[dim] - width, cells.shape[dim], axis=dim)
        cells = jnp.concatenate(
            [
                lax.ppermute(tail, axis, [(i, (i + 1) % count) for i in range(ends)]),
                cells,
                lax.ppermute(head, axis, [((i + 1) % count, i) for i in range(ends)]),
            ],
            axis=dim,
        )
    return cells


def split_up(value, dim, count):
    before, after = (value.shape[:dim], value.shape[dim + 1 :])
    return jnp.moveaxis(value.reshape(*before, count, -1, *after), dim, 0)


def summed_on_arrival(value, axis, dim):
    blocks = split_up(value, dim, lax.axis_size(axis))
    arrived = lax.all_to_all(blocks, axis, split_axis=0, concat_axis=0, tiled=True)
    return arrived.astype(jnp.float32).sum(axis=0)


def in_one_piece(arrays, axis, dim, along):
    widths = [a.shape[along] for a in arrays]
    both = jnp.concatenate(arrays, axis=along)
    result = summed_on_arrival(both, axis, dim)
    return tuple(jnp.split(result, [sum(widths[:k]) for k in range(1, len(widths))], axis=along))


def layer_norm(value, gain, shift):
    centre = jnp.mean(value, axis=-1, keepdims=True)
    offset = value - centre
    spread_sq = jnp.mean(offset * offset, axis=-1, keepdims=True)
    return offset * lax.rsqrt(spread_sq + NORM_EPS) * gain + shift


def norm_back(value, gain, shift, grad):
    unused, pullback = jax.vjp(layer_norm, value, gain, shift)
    return pullback(grad)


def gelu_grad(pre_value, grad):
    return jax.vjp(jax.nn.gelu, pre_value)[1](grad)[0]


def matmul_nn(left, right):
    return jnp.dot(left, right, preferred_element_type=jnp.float32)


def matmul_tn(left, right):
    return lax.dot_general(
        left, right, (((0,), (0,)), ((), ())), preferred_element_type=jnp.float32
    )


def matmul_nt(left, right):
    return lax.dot_general(
        left, right, (((1,), (1,)), ((), ())), preferred_element_type=jnp.float32
    )


def mlp_forward(inputs, first, bias_one, middle, bias_two, last, bias_three):
    pre_one = matmul_nn(inputs, first) + bias_one
    act_one = jax.nn.gelu(pre_one).astype(jnp.bfloat16)
    pre_two = matmul_nn(act_one, middle) + bias_two
    act_two = jax.nn.gelu(pre_two).astype(jnp.bfloat16)
    result = matmul_nn(act_two, last) + bias_three
    return (result, (inputs, pre_one, act_one, pre_two, act_two))


def mlp_backward(stored, first, middle, last, grad_out):
    inputs, pre_one, act_one, pre_two, act_two = stored
    g_last = matmul_tn(act_two, grad_out)
    g_bias_three = jnp.sum(grad_out.astype(jnp.float32), axis=0)
    grad_two = gelu_grad(pre_two, matmul_nt(grad_out, last)).astype(jnp.bfloat16)
    g_middle = matmul_tn(act_one, grad_two)
    g_bias_two = jnp.sum(grad_two.astype(jnp.float32), axis=0)
    grad_one = gelu_grad(pre_one, matmul_nt(grad_two, middle)).astype(jnp.bfloat16)
    g_first = matmul_tn(inputs, grad_one)
    g_bias_one = jnp.sum(grad_one.astype(jnp.float32), axis=0)
    g_inputs = matmul_nt(grad_one, first)
    return (g_inputs, g_first, g_bias_one, g_middle, g_bias_two, g_last, g_bias_three)


def collect(residue_low):
    return lax.all_gather(residue_low, "nbr", axis=0, tiled=True)


def combine(partial_rows):
    return lax.psum_scatter(
        partial_rows.astype(jnp.bfloat16), "nbr", scatter_dimension=0, tiled=True
    ).astype(jnp.float32)


def spread(states_low):
    block_rows = collect(states_low)
    extended = padded(block_rows, (("res", 0),), block_rows.shape[0])
    return (block_rows, extended)


def edge_inputs(block_rows, extended, local_index, edges_low):
    row_count, slot_count = local_index.shape
    node_width = block_rows.shape[1]
    mine = jnp.broadcast_to(block_rows[:, None, :], (row_count, slot_count, node_width))
    other = jnp.take(extended, local_index, axis=0)
    joined = jnp.concatenate([mine, other, edges_low], axis=2)
    return joined.reshape(row_count * slot_count, joined.shape[2])


def spread_back(g_inputs, local_index, node_width):
    row_count, slot_count = local_index.shape
    pieces = g_inputs.reshape(row_count, slot_count, g_inputs.shape[1])
    g_own = jnp.sum(pieces[:, :, :node_width], axis=1)
    g_other = pieces[:, :, node_width : 2 * node_width].reshape(row_count * slot_count, node_width)
    table = (
        jnp.zeros((3 * row_count, node_width), jnp.float32).at[local_index.reshape(-1)].add(g_other)
    )
    outer = jnp.concatenate([table[:row_count], table[2 * row_count :]], axis=0)
    moved = padded(outer.astype(jnp.bfloat16), (("res", 0),), row_count).astype(outer.dtype)
    g_block = table[row_count : 2 * row_count] + g_own + moved[:row_count] + moved[3 * row_count :]
    return (combine(g_block), pieces[:, :, 2 * node_width :])


def per_device(
    nodes,
    edges,
    protein_ids,
    time_index,
    neighbors,
    edge_mask,
    time_table,
    msg_in,
    msg_mid,
    msg_out,
    ffn_in,
    ffn_out,
    edge_in,
    edge_hidden,
    node_gains,
    node_biases,
    ffn_bias,
    edge_gains,
    edge_biases,
    d_nodes,
    d_edges,
):
    node_width = nodes.shape[1]
    row_count, slot_count = neighbors.shape
    layer_total = msg_in.shape[0]
    cols = (
        lax.all_gather(msg_in.astype(jnp.bfloat16), "nbr", axis=2, tiled=True),
        lax.all_gather(msg_mid.astype(jnp.bfloat16), "nbr", axis=2, tiled=True),
        lax.all_gather(msg_out.astype(jnp.bfloat16), "nbr", axis=2, tiled=True),
        lax.all_gather(edge_in.astype(jnp.bfloat16), "nbr", axis=2, tiled=True),
        lax.all_gather(edge_hidden.astype(jnp.bfloat16), "nbr", axis=3, tiled=True),
        lax.all_gather(time_table.astype(jnp.bfloat16), "nbr", axis=1, tiled=True),
    )
    w_first, w_middle, w_last, e_first, e_hidden, table_low = (
        lax.all_gather(cols[0], "res", axis=1, tiled=True),
        lax.all_gather(cols[1], "res", axis=1, tiled=True),
        lax.all_gather(cols[2], "res", axis=1, tiled=True),
        lax.all_gather(cols[3], "res", axis=1, tiled=True),
        lax.all_gather(cols[4], "res", axis=2, tiled=True),
        lax.all_gather(cols[5], "res", axis=0, tiled=True),
    )
    ffn_first = ffn_in.astype(jnp.bfloat16)
    ffn_second = ffn_out.astype(jnp.bfloat16)
    ffn_first, ffn_second = (
        lax.all_gather(ffn_first, "nbr", axis=2, tiled=True),
        lax.all_gather(ffn_second, "nbr", axis=1, tiled=True),
    )
    ffn_first, ffn_second = (
        lax.all_gather(ffn_first, "res", axis=1, tiled=True),
        lax.all_gather(ffn_second, "res", axis=2, tiled=True),
    )
    protein_count = time_index.shape[0]
    matches = protein_ids[:, None] == jnp.arange(protein_count, dtype=jnp.int32)[None, :]
    step_rows = jnp.sum(jnp.where(matches, time_index[None, :], 0), axis=1)
    step_onehot = (
        step_rows[:, None] == jnp.arange(table_low.shape[0], dtype=jnp.int32)[None, :]
    ).astype(jnp.bfloat16)
    state = nodes + matmul_nn(step_onehot, table_low)
    edge_state = edges
    base_row = lax.axis_index("res") * row_count - row_count
    local_index = neighbors - base_row
    slot_used = edge_mask > 0
    ones_float = edge_mask.astype(jnp.float32)
    count_part = jnp.sum(ones_float, axis=1)
    stored = []
    for layer_at in range(layer_total):
        biases_now = node_biases[layer_at]
        edge_bias_now = edge_biases[layer_at]
        states_low = state.astype(jnp.bfloat16)
        edges_low = edge_state.astype(jnp.bfloat16)
        block_rows, extended = spread(states_low)
        msg_inputs = edge_inputs(block_rows, extended, local_index, edges_low)
        message, msg_saved = mlp_forward(
            msg_inputs,
            w_first[layer_at],
            biases_now[0],
            w_middle[layer_at],
            biases_now[1],
            w_last[layer_at],
            biases_now[2],
        )
        masked = jnp.sum(
            message.reshape(row_count, slot_count, node_width) * ones_float[:, :, None], axis=1
        )
        totals, counts = (
            lax.psum_scatter(masked, "nbr", scatter_dimension=0, tiled=True),
            lax.psum_scatter(count_part, "nbr", scatter_dimension=0, tiled=True),
        )
        merged = state + totals / counts[:, None]
        hidden_one = layer_norm(merged, node_gains[layer_at, 0], biases_now[4])
        one_low = hidden_one.astype(jnp.bfloat16)
        ffn_rows_low = one_low
        ffn_bias_now = ffn_bias[layer_at]
        pre_ffn = matmul_nn(ffn_rows_low, ffn_first[layer_at]) + ffn_bias_now
        act_ffn = jax.nn.gelu(pre_ffn).astype(jnp.bfloat16)
        branch_part = matmul_nn(act_ffn, ffn_second[layer_at])
        joined = hidden_one + branch_part + biases_now[3]
        hidden_two = layer_norm(joined, node_gains[layer_at, 1], biases_now[5])
        two_low = hidden_two.astype(jnp.bfloat16)
        block_two, extended_two = spread(two_low)
        upd_inputs = edge_inputs(block_two, extended_two, local_index, edges_low)
        update, edge_saved = mlp_forward(
            upd_inputs,
            e_first[layer_at],
            edge_bias_now[0],
            e_hidden[layer_at, 0],
            edge_bias_now[1],
            e_hidden[layer_at, 1],
            edge_bias_now[2],
        )
        edge_sum = edge_state + update.reshape(row_count, slot_count, update.shape[1])
        new_edges = layer_norm(edge_sum, edge_gains[layer_at], edge_bias_now[3])
        stored.append(
            (
                msg_saved,
                merged,
                counts,
                ffn_rows_low,
                pre_ffn,
                act_ffn,
                joined,
                edge_saved,
                edge_sum,
            )
        )
        state = hidden_two
        edge_state = new_edges
    g_state = d_nodes
    g_edge_state = d_edges
    grads_held = [None] * layer_total
    for layer_at in range(layer_total - 1, -1, -1):
        msg_saved, merged, counts, ffn_rows_low, pre_ffn, act_ffn, joined, edge_saved, edge_sum = (
            stored[layer_at]
        )
        biases_now = node_biases[layer_at]
        edge_bias_now = edge_biases[layer_at]
        g_sum, g_edge_gain, g_edge_shift = norm_back(
            edge_sum, edge_gains[layer_at], edge_bias_now[3], g_edge_state
        )
        g_update = g_sum.reshape(row_count * slot_count, g_sum.shape[2]).astype(jnp.bfloat16)
        upd_grads = mlp_backward(
            edge_saved, e_first[layer_at], e_hidden[layer_at, 0], e_hidden[layer_at, 1], g_update
        )
        g_nodes_two, g_edges_two = spread_back(upd_grads[0], local_index, node_width)
        g_edges_prev = g_sum + g_edges_two
        g_two = g_state + g_nodes_two
        g_joined, g_gain_two, g_shift_two = norm_back(
            joined, node_gains[layer_at, 1], biases_now[5], g_two
        )
        g_branch = g_joined.astype(jnp.bfloat16)
        g_bias_five = jnp.sum(g_branch.astype(jnp.float32), axis=0)
        g_second = matmul_tn(act_ffn, g_branch)
        g_pre = gelu_grad(pre_ffn, matmul_nt(g_branch, ffn_second[layer_at])).astype(jnp.bfloat16)
        g_first_ffn = matmul_tn(ffn_rows_low, g_pre)
        g_pre_sum = jnp.sum(g_pre.astype(jnp.float32), axis=0)
        g_back = matmul_nt(g_pre, ffn_first[layer_at])
        g_hidden_one = g_joined + g_back
        g_merged, g_gain_one, g_shift_one = norm_back(
            merged, node_gains[layer_at, 0], biases_now[4], g_hidden_one
        )
        g_totals = (g_merged / counts[:, None]).astype(jnp.bfloat16)
        g_totals_all = collect(g_totals)
        g_message = jnp.where(
            slot_used[:, :, None], g_totals_all[:, None, :], jnp.zeros((), jnp.bfloat16)
        )
        g_message = g_message.reshape(row_count * slot_count, node_width)
        msg_grads = mlp_backward(
            msg_saved, w_first[layer_at], w_middle[layer_at], w_last[layer_at], g_message
        )
        g_nodes_one, g_edges_one = spread_back(msg_grads[0], local_index, node_width)
        g_state = g_merged + g_nodes_one
        g_edge_state = g_edges_prev + g_edges_one
        grads_held[layer_at] = (
            msg_grads[1],
            msg_grads[3],
            msg_grads[5],
            g_first_ffn,
            g_second,
            upd_grads[1],
            jnp.stack([upd_grads[3], upd_grads[5]]),
            jnp.stack([g_gain_one, g_gain_two]),
            jnp.stack(
                [msg_grads[2], msg_grads[4], msg_grads[6], g_bias_five, g_shift_one, g_shift_two]
            ),
            g_pre_sum,
            g_edge_gain,
            jnp.stack([upd_grads[2], upd_grads[4], upd_grads[6], g_edge_shift]),
        )
    stacked = [
        jnp.stack([grads_held[layer_at][member] for layer_at in range(layer_total)])
        for member in range(12)
    ]
    g_table_full = lax.dot_general(
        step_onehot.astype(jnp.float32),
        g_state,
        (((0,), (0,)), ((), ())),
        precision=lax.Precision.HIGHEST,
        preferred_element_type=jnp.float32,
    )
    col_sums = (
        lax.psum_scatter(
            stacked[0].astype(jnp.bfloat16), "nbr", scatter_dimension=2, tiled=True
        ).astype(jnp.float32),
        lax.psum_scatter(
            stacked[1].astype(jnp.bfloat16), "nbr", scatter_dimension=2, tiled=True
        ).astype(jnp.float32),
        lax.psum_scatter(
            stacked[2].astype(jnp.bfloat16), "nbr", scatter_dimension=2, tiled=True
        ).astype(jnp.float32),
        lax.psum_scatter(
            stacked[5].astype(jnp.bfloat16), "nbr", scatter_dimension=2, tiled=True
        ).astype(jnp.float32),
        lax.psum_scatter(
            stacked[6].astype(jnp.bfloat16), "nbr", scatter_dimension=3, tiled=True
        ).astype(jnp.float32),
        lax.psum_scatter(
            g_table_full.astype(jnp.bfloat16), "nbr", scatter_dimension=1, tiled=True
        ).astype(jnp.float32),
    )
    g_msg_in, g_msg_mid, g_msg_out, g_edge_in, g_edge_hidden, g_time_table = (
        summed_on_arrival(col_sums[0].astype(jnp.bfloat16), "res", 1),
        *in_one_piece(
            (col_sums[1].astype(jnp.bfloat16), col_sums[2].astype(jnp.bfloat16)), "res", 1, 0
        ),
        summed_on_arrival(col_sums[3].astype(jnp.bfloat16), "res", 1),
        summed_on_arrival(col_sums[4].astype(jnp.bfloat16), "res", 2),
        summed_on_arrival(col_sums[5].astype(jnp.bfloat16), "res", 0),
    )
    g_ffn_first = stacked[3]
    g_ffn_second = stacked[4]
    g_ffn_first, g_ffn_second = (
        lax.psum_scatter(
            g_ffn_first.astype(jnp.bfloat16), "nbr", scatter_dimension=2, tiled=True
        ).astype(jnp.float32),
        lax.psum_scatter(
            g_ffn_second.astype(jnp.bfloat16), "nbr", scatter_dimension=1, tiled=True
        ).astype(jnp.float32),
    )
    g_ffn_in, g_ffn_out = (
        summed_on_arrival(g_ffn_first.astype(jnp.bfloat16), "res", 1),
        summed_on_arrival(g_ffn_second.astype(jnp.bfloat16), "res", 2),
    )
    g_node_gains, g_node_biases, g_ffn_bias, g_edge_gains, g_edge_biases = lax.psum(
        (stacked[7], stacked[8], stacked[9], stacked[10], stacked[11]), ("res", "nbr")
    )
    return (
        state,
        edge_state,
        g_state,
        g_edge_state,
        g_time_table,
        g_msg_in,
        g_msg_mid,
        g_msg_out,
        g_ffn_in,
        g_ffn_out,
        g_edge_in,
        g_edge_hidden,
        g_node_gains,
        g_node_biases,
        g_ffn_bias,
        g_edge_gains,
        g_edge_biases,
    )


def solution(mesh):
    return jax.shard_map(
        per_device,
        mesh=mesh,
        in_specs=(
            P(("res", "nbr"), None),
            P("res", "nbr", None),
            P(("res", "nbr")),
            P(),
            P("res", "nbr"),
            P("res", "nbr"),
            P("res", "nbr"),
            P(None, "res", "nbr"),
            P(None, "res", "nbr"),
            P(None, "res", "nbr"),
            P(None, "res", "nbr"),
            P(None, "nbr", "res"),
            P(None, "res", "nbr"),
            P(None, None, "res", "nbr"),
            P(),
            P(),
            P(),
            P(),
            P(),
            P(("res", "nbr"), None),
            P("res", "nbr", None),
        ),
        out_specs=(
            P(("res", "nbr"), None),
            P("res", "nbr", None),
            P(("res", "nbr"), None),
            P("res", "nbr", None),
            P("res", "nbr"),
            P(None, "res", "nbr"),
            P(None, "res", "nbr"),
            P(None, "res", "nbr"),
            P(None, "res", "nbr"),
            P(None, "nbr", "res"),
            P(None, "res", "nbr"),
            P(None, None, "res", "nbr"),
            P(),
            P(),
            P(),
            P(),
            P(),
        ),
        check_vma=False,
    )
```

profile of v0, /device:TPU:0, one launch (start us, length us, event | category | flops | bytes accessed | tf_op | source)
XLA Modules:
  0.0 1277.7 jit_solution(15188559198505584720)
XLA Ops:
  29.0 31.4 %all_gather.65 = bf16[128,512]{1,0:T(8,128)(2,1)S(1)} all-gather(bf16[16,512]{1,0:T(8,128)(2,1)S(1)} %all_gather.64), channel_id=1, replica_groups=mesh['res'=8,'nbr'=4] {'res'}, dimensions={0}, use_global_device_ids=true | all-gather | bytes 147456 | tf_op jit(solution)/shard_map/all_gather | solution.py:178
  118.9 35.4 %all-gather.10.cloned.1.call-done = bf16[2,512,512]{2,1,0:T(8,128)(2,1)} async-done(((bf16[2,64,512]{2,1,0:T(8,128)(2,1)}), bf16[2,512,512]{2,1,0:T(8,128)(2,1)}) %all-gather.10.cloned.1.call-update) | async-done | bytes 1048592 | tf_op jit(solution)/shard_map/all_gather | solution.py:175
  177.1 8.2 all_gather.75
  201.1 36.9 %all_gather.79 = bf16[2,1216,192]{2,0,1:T(2,128)(2,1)S(1)} all-gather(bf16[2,152,192]{2,0,1:T(2,128)(2,1)S(1)} %copy.287), channel_id=1, replica_groups=mesh['res'=8,'nbr'=4] {'res'}, dimensions={1}, use_global_device_ids=true | all-gather | bytes 1050624 | tf_op jit(solution)/shard_map/all_gather | solution.py:176
  242.6 31.4 %all-gather.12.cloned.1.call-done = bf16[2,512,2048]{2,1,0:T(8,128)(2,1)} async-done(((bf16[2,64,2048]{2,1,0:T(8,128)(2,1)}), bf16[2,512,2048]{2,1,0:T(8,128)(2,1)}) %all-gather.12.cloned.1.call-update) | async-done | bytes 4194320 | tf_op jit(solution)/shard_map/all_gather | solution.py:187
  276.1 71.8 %all-gather.14.cloned.1.call-done = bf16[2,2048,512]{1,2,0:T(8,128)(2,1)} async-done(((bf16[2,2048,64]{1,2,0:T(8,128)(2,1)}), bf16[2,2048,512]{1,2,0:T(8,128)(2,1)}) %all-gather.14.cloned.1.call-update) | async-done | bytes 4194320 | tf_op jit(solution)/shard_map/all_gather | solution.py:188
  371.0 33.0 %all_gather.81 = bf16[2,2,192,192]{3,2,1,0:T(8,128)(2,1)} all-gather(bf16[2,2,24,192]{3,2,1,0:T(8,128)(2,1)S(1)} %copy.290), channel_id=1, replica_groups=mesh['res'=8,'nbr'=4] {'res'}, dimensions={2}, use_global_device_ids=true | all-gather | bytes 331776 | tf_op jit(solution)/shard_map/all_gather | solution.py:177
  419.5 8.1 reshape.480
  450.4 8.0 reshape.482
  480.3 18.2 %reduce-scatter.24.cloned.1.call-done = f32[32,512]{1,0:T(8,128)} async-done(((f32[128,512]{1,0:T(8,128)}), f32[32,512]{1,0:T(8,128)}) %reduce-scatter.24.cloned.1.call-update) | async-done | bytes 65552 | tf_op jit(solution)/shard_map/reduce_scatter | solution.py:224
  539.2 8.0 reshape.484
  603.8 14.1 %scatter_custom_fusion = f32[384,512]{1,0:T(8,128)} fusion(s32[1920]{0:T(1024)} %fusion.171, f32[1920,512]{1,0:T(8,128)} %reshape.534, f32[]{:T(128)} %constant.87.clone.1), kind=kCustom, calls=%fused_computation.260 | custom fusion | flops 983040 | bytes 786944 | tf_op jit(solution)/shard_map/scatter-add | solution.py:130
  635.9 16.8 %reduce-scatter.26.cloned.1.call-done = bf16[32,512]{1,0:T(8,128)(2,1)} async-done(((bf16[128,512]{1,0:T(8,128)(2,1)}), bf16[32,512]{1,0:T(8,128)(2,1)}) %reduce-scatter.26.cloned.1.call-update) | async-done | bytes 32784 | tf_op jit(solution)/shard_map/reduce_scatter | solution.py:104
  711.3 13.8 %scatter_custom_fusion.1 = f32[384,512]{1,0:T(8,128)S(1)} fusion(s32[1920]{0:T(1024)} %fusion.171, f32[1920,512]{1,0:T(8,128)} %reshape.542, f32[]{:T(128)} %constant.87.clone.1), kind=kCustom, calls=%fused_computation.258 | custom fusion | flops 983040 | bytes 786944 | tf_op jit(solution)/shard_map/scatter-add | solution.py:130
  767.7 14.1 %scatter_custom_fusion.2 = f32[384,512]{1,0:T(8,128)} fusion(s32[1920]{0:T(1024)} %fusion.171, f32[1920,512]{1,0:T(8,128)} %reshape.550, f32[]{:T(128)} %constant.87.clone.1), kind=kCustom, calls=%fused_computation.256 | custom fusion | flops 983040 | bytes 786944 | tf_op jit(solution)/shard_map/scatter-add | solution.py:130
  800.1 12.4 reduce-scatter.28.cloned.1.call-done
  812.5 21.9 %reduce-scatter.30.cloned.1.call-done = bf16[32,512]{1,0:T(8,128)(2,1)} async-done(((bf16[128,512]{1,0:T(8,128)(2,1)}), bf16[32,512]{1,0:T(8,128)(2,1)}) %reduce-scatter.30.cloned.1.call-update) | async-done | bytes 32784 | tf_op jit(solution)/shard_map/reduce_scatter | solution.py:104
  888.5 13.6 %scatter_custom_fusion.3 = f32[384,512]{1,0:T(8,128)S(1)} fusion(s32[1920]{0:T(1024)} %fusion.171, f32[1920,512]{1,0:T(8,128)} %reshape.558, f32[]{:T(128)} %constant.87.clone.1), kind=kCustom, calls=%fused_computation.254 | custom fusion | flops 983040 | bytes 786944 | tf_op jit(solution)/shard_map/scatter-add | solution.py:130
  920.4 15.1 %reduce-scatter.32.cloned.1.call-done = bf16[32,512]{1,0:T(8,128)(2,1)} async-done(((bf16[128,512]{1,0:T(8,128)(2,1)}), bf16[32,512]{1,0:T(8,128)(2,1)}) %reduce-scatter.32.cloned.1.call-update) | async-done | bytes 32784 | tf_op jit(solution)/shard_map/reduce_scatter | solution.py:104
  1048.9 25.9 %reduce-scatter.46.cloned.1.call-done = bf16[128,1024]{1,0:T(8,128)(2,1)} async-done(((bf16[512,1024]{1,0:T(8,128)(2,1)}), bf16[128,1024]{1,0:T(8,128)(2,1)}) %reduce-scatter.46.cloned.1.call-update) | async-done | bytes 262160
  1082.9 28.4 %reduce-scatter.42.cloned.1.call-done = bf16[128,2432]{1,0:T(8,128)(2,1)} async-done(((bf16[512,2432]{1,0:T(8,128)(2,1)}), bf16[128,2432]{1,0:T(8,128)(2,1)}) %reduce-scatter.42.cloned.1.call-update) | async-done | bytes 622608
  1121.2 37.0 %reduce-scatter.36.cloned.1.call-done = bf16[2,512,512]{2,1,0:T(8,128)(2,1)} async-done(((bf16[2,2048,512]{2,1,0:T(8,128)(2,1)}), bf16[2,512,512]{2,1,0:T(8,128)(2,1)}) %reduce-scatter.36.cloned.1.call-update) | async-done | bytes 1048592 | tf_op jit(solution)/shard_map/reduce_scatter | solution.py:373
  1169.8 35.6 %reduce-scatter.34.cloned.1.call-done = bf16[2,512,512]{2,1,0:T(8,128)(2,1)} async-done(((bf16[2,512,2048]{2,1,0:T(8,128)(2,1)}), bf16[2,512,512]{2,1,0:T(8,128)(2,1)}) %reduce-scatter.34.cloned.1.call-update) | async-done | bytes 1048592 | tf_op jit(solution)/shard_map/reduce_scatter | solution.py:370
  1213.4 45.8 %all-reduce.2 = (f32[2,2,512]{2,1,0:T(2,128)}, f32[2,6,512]{2,1,0:T(8,128)S(1)}, f32[2,2048]{1,0:T(2,128)}, f32[2,192]{1,0:T(2,128)}, f32[2,4,192]{2,1,0:T(4,128)}) all-reduce(f32[2,2,512]{2,1,0:T(2,128)S(1)} %pad_maximum_fusion.30, f32[2,6,512]{2,1,0:T(8,128)S(1)} %pad_maximum_fusion.28, ...), channel_id=1, replica_groups=mesh['res'=8,'nbr'=4] {'res','nbr'}, use_global_device_ids=true, to_apply=%region_62.64 | all-reduce | flops 14208 | bytes 113664 | tf_op jit(solution)/shard_map/psum | solution.py:381
  (764 shorter events, 674.1 us)
Async XLA Ops:
  7.2 98.4 %all-gather.6.cloned.1.call-start = ((), (), s32[]{:S(2)}) async-start(), calls=%async_computation.20 | async-start | bytes 2801664 | tf_op jit(solution)/shard_map/all_gather | solution.py:173
  16.3 96.8 %all-gather.8.cloned.1.call-start = ((), (), s32[]{:S(2)}) async-start(), calls=%async_computation.21 | async-start | bytes 1179648 | tf_op jit(solution)/shard_map/all_gather | solution.py:174
  23.1 131.2 %all-gather.10.cloned.1.call-start = ((), (), s32[]{:S(2)}) async-start(), calls=%async_computation.22 | async-start | bytes 1179648 | tf_op jit(solution)/shard_map/all_gather | solution.py:175
  80.8 160.5 %reduce-scatter.22.cloned.1.call-start = ((), (), s32[]{:S(2)}) async-start(), calls=%async_computation.23 | async-start | bytes 327680 | tf_op jit(solution)/shard_map/reduce_scatter | solution.py:224
  169.3 104.7 %all-gather.12.cloned.1.call-start = ((), (), s32[]{:S(2)}) async-start(), calls=%async_computation.24 | async-start | bytes 4718592 | tf_op jit(solution)/shard_map/all_gather | solution.py:187
  177.0 170.9 %all-gather.14.cloned.1.call-start = ((), (), s32[]{:S(2)}) async-start(), calls=%async_computation.25 | async-start | bytes 4718592 | tf_op jit(solution)/shard_map/all_gather | solution.py:188
  185.3 313.2 %reduce-scatter.24.cloned.1.call-start = ((), (), s32[]{:S(2)}) async-start(), calls=%async_computation.26 | async-start | bytes 327680 | tf_op jit(solution)/shard_map/reduce_scatter | solution.py:224
  356.7 47.3 %collective-permute-start.3 = (bf16[128,512]{1,0:T(8,128)(2,1)S(1)}, bf16[128,512]{1,0:T(8,128)(2,1)S(1)}, u32[]{:S(2)}, u32[]{:S(2)}) collective-permute-start(bf16[128,512]{1,0:T(8,128)(2,1)S(1)} %all_gather.77), channel_id=1, source_target_pairs={{4,0},{8,4},{12,8},{16,12},{20,16},{24,20},{28,24},{5,1},{9,5},{13... | collective-permute-start | bytes 393224 | tf_op jit(solution)/shard_map/ppermute | solution.py:19
  358.0 46.0 %collective-permute-start.2 = (bf16[128,512]{1,0:T(8,128)(2,1)S(1)}, bf16[128,512]{1,0:T(8,128)(2,1)S(1)}, u32[]{:S(2)}, u32[]{:S(2)}) collective-permute-start(bf16[128,512]{1,0:T(8,128)(2,1)S(1)} %all_gather.77), channel_id=1, source_target_pairs={{0,4},{4,8},{8,12},{12,16},{16,20},{20,24},{24,28},{1,5},{5,9},{9,... | collective-permute-start | bytes 393224 | tf_op jit(solution)/shard_map/ppermute | solution.py:17
  480.2 172.5 %reduce-scatter.26.cloned.1.call-start = ((), (), s32[]{:S(2)}) async-start(), calls=%async_computation.27 | async-start | bytes 163840 | tf_op jit(solution)/shard_map/reduce_scatter | solution.py:104
  633.0 179.5 %reduce-scatter.28.cloned.1.call-start = ((), (), s32[]{:S(2)}) async-start(), calls=%async_computation.28 | async-start | bytes 163840 | tf_op jit(solution)/shard_map/reduce_scatter | solution.py:104
  726.7 62.9 %collective-permute-start.8 = (bf16[128,512]{1,0:T(8,128)(2,1)}, bf16[128,512]{1,0:T(8,128)(2,1)}, u32[]{:S(2)}, u32[]{:S(2)}) collective-permute-start(bf16[128,512]{1,0:T(8,128)(2,1)} %get-tuple-element.192), channel_id=1, source_target_pairs={{0,4},{4,8},{8,12},{12,16},{16,20},{20,24},{24,28},{1,5},{5,9},{9,... | collective-permute-start | bytes 393224 | tf_op jit(solution)/shard_map/ppermute | solution.py:17
  730.7 58.9 %collective-permute-start.9 = (bf16[128,512]{1,0:T(8,128)(2,1)}, bf16[128,512]{1,0:T(8,128)(2,1)}, u32[]{:S(2)}, u32[]{:S(2)}) collective-permute-start(bf16[128,512]{1,0:T(8,128)(2,1)} %get-tuple-element.193), channel_id=1, source_target_pairs={{4,0},{8,4},{12,8},{16,12},{20,16},{24,20},{28,24},{5,1},{9,5},{13... | collective-permute-start | bytes 393224 | tf_op jit(solution)/shard_map/ppermute | solution.py:19
  797.1 138.3 %reduce-scatter.32.cloned.1.call-start = ((), (), s32[]{:S(2)}) async-start(), calls=%async_computation.30 | async-start | bytes 163840 | tf_op jit(solution)/shard_map/reduce_scatter | solution.py:104
  916.4 98.0 %all-reduce.5.cloned.1.call-start = ((), (), s32[]{:S(2)}) async-start(), calls=%async_computation.38 | async-start | bytes 786432
  920.3 101.7 %reduce-scatter.40.cloned.1.call-start = ((), (), s32[]{:S(2)}) async-start(), calls=%async_computation.34 | async-start | bytes 163840
  937.5 94.9 %reduce-scatter.38.cloned.1.call-start = ((), (), s32[]{:S(2)}) async-start(), calls=%async_computation.33 | async-start | bytes 1228800 | tf_op jit(solution)/shard_map/reduce_scatter | solution.py:348
  938.6 108.9 %reduce-scatter.44.cloned.1.call-start = ((), (), s32[]{:S(2)}) async-start(), calls=%async_computation.36 | async-start | bytes 1310720
  950.0 124.8 %reduce-scatter.46.cloned.1.call-start = ((), (), s32[]{:S(2)}) async-start(), calls=%async_computation.37 | async-start | bytes 1310720
  976.3 135.0 %reduce-scatter.42.cloned.1.call-start = ((), (), s32[]{:S(2)}) async-start(), calls=%async_computation.35 | async-start | bytes 3112960
  1003.7 154.5 %reduce-scatter.36.cloned.1.call-start = ((), (), s32[]{:S(2)}) async-start(), calls=%async_computation.32 | async-start | bytes 5242880 | tf_op jit(solution)/shard_map/reduce_scatter | solution.py:373
  1008.7 196.7 %reduce-scatter.34.cloned.1.call-start = ((), (), s32[]{:S(2)}) async-start(), calls=%async_computation.31 | async-start | bytes 5242880 | tf_op jit(solution)/shard_map/reduce_scatter | solution.py:370
  1161.0 46.8 %all-to-all-start.4 = ((bf16[8,2,512,64]{2,3,1,0:T(8,128)(2,1)}), bf16[8,2,512,64]{2,3,1,0:T(8,128)(2,1)S(1)}, u32[]{:S(2)}, u32[]{:S(2)}) async-start(bf16[8,2,512,64]{2,3,1,0:T(8,128)(2,1)} %copy.323), calls=%async_computation.12 | async-start | bytes 2097152 | tf_op jit(solution)/shard_map/all_to_all | solution.py:33
  1207.8 61.1 %all-to-all-start.3 = ((bf16[8,2,64,512]{3,2,1,0:T(8,128)(2,1)}), bf16[8,2,64,512]{3,2,1,0:T(8,128)(2,1)}, u32[]{:S(2)}, u32[]{:S(2)}) async-start(bf16[8,2,64,512]{3,2,1,0:T(8,128)(2,1)} %bitcast.312), calls=%async_computation.10 | async-start | bytes 2097152 | tf_op jit(solution)/shard_map/all_to_all | solution.py:33
  (210 other events, 3501.9 us)
Sparse Core Ops, SparseCore 0:
  16.4 55.5 all-gather.5
  74.1 38.9 all-gather.7
  115.3 38.9 all-gather.9
  169.4 18.7 reduce-scatter.21
  190.4 83.4 all-gather.11
  276.2 71.6 all-gather.13
  480.4 18.0 reduce-scatter.23
  633.0 19.6 reduce-scatter.25
  791.4 21.0 reduce-scatter.27
  814.8 19.5 reduce-scatter.29
  916.5 18.9 reduce-scatter.31
  937.6 32.6 all-reduce.4
  973.4 19.5 reduce-scatter.39
  995.5 24.5 reduce-scatter.37
  1022.6 24.8 reduce-scatter.43
  1049.9 24.9 reduce-scatter.45
  1077.4 33.8 reduce-scatter.41
  1113.7 44.4 reduce-scatter.35
  1160.9 44.4 reduce-scatter.33
where the time goes:
time: 1290 us; the launch traced here: 1280 us
  waiting for transfers between devices  372 us (29%)
  local copies, waits for them, and re-layouts  256 us (20%)
  blocking collectives  233 us (18%)
  matrix products  164 us (13%)
  other arithmetic  159 us (12%)
  starting transfers between devices  75.6 us (6%)
  between operations  18.4 us (1%)
    all_gather x1, waiting for transfers between devices, per_device(): lax.all_gather(ffn_second, 'res', axis=2, tiled=True)  71.8 us
    reduce_scatter x4, waiting for transfers between devices, combine(): lax.psum_scatter(partial_rows.astype(jnp.bfloat16), 'nbr', scatter_dimens...  66.2 us
    dot_general x16, matrix products, matmul_nt(): lax.dot_general(left, right, (((1,), (1,)), ((), ())), preferred_element_...  62.2 us
    unnamed x412, local copies, waits for them, and re-layouts  60.7 us
    unnamed x24, waiting for transfers between devices  59.9 us
    scatter-add x4, other arithmetic, spread_back(): jnp.zeros((3 * row_count, node_width), jnp.float32)  55.7 us
    dot_general x17, matrix products, matmul_nn(): return jnp.dot(left, right, preferred_element_type=jnp.float32)  52.7 us
    dot_general x16, matrix products, matmul_tn(): lax.dot_general(left, right, (((0,), (0,)), ((), ())), preferred_element_...  48.5 us
  transfers between devices with their start and end apart: 40, of which 19 were waited for; matrix products, arithmetic and copies ran while one was open for 19% of the time, Pallas kernels for 0%

commit v1 on v0

v1 whole, which is shorter than its diff:
```python
import functools

import jax
import jax.numpy as jnp
from jax import lax
from jax.experimental import pallas as pl
from jax.experimental.pallas import tpu as pltpu
from jax.sharding import PartitionSpec as P

NORM_EPS = 1e-05
F32 = jnp.float32
BF16 = jnp.bfloat16
MESH = pl.DeviceIdType.MESH
LANES = 128
CHUNK = 5
TANH_A = 0.7978845608028654
TANH_B = 0.044715
B1, B2, B3, B5, SH1, SH2, GN1, GN2, FB, C1, C2, C3, C4, GE = range(14)
VECTORS = 14


def nn(left, right):
    return jnp.dot(left, right, preferred_element_type=F32)


def nt(left, right):
    return lax.dot_general(left, right, (((1,), (1,)), ((), ())), preferred_element_type=F32)


def tn(left, right):
    return lax.dot_general(left, right, (((0,), (0,)), ((), ())), preferred_element_type=F32)


def gelu_pair(z):
    sq = z * z
    half = 0.5 + 0.5 * jnp.tanh(z * (TANH_A + (TANH_A * TANH_B) * sq))
    value = z * half
    slope = half + (value * (1.0 - half)) * (2.0 * TANH_A + (6.0 * TANH_A * TANH_B) * sq)
    return value.astype(BF16), slope.astype(BF16)


def norm_parts(value):
    scale = 1.0 / value.shape[0]
    centre = jnp.sum(value, axis=0, keepdims=True) * scale
    offset = value - centre
    spread = jnp.sum(offset * offset, axis=0, keepdims=True) * scale
    rstd = lax.rsqrt(spread + NORM_EPS)
    return offset * rstd, rstd


def norm_back(hat, rstd, gain, grad):
    scale = 1.0 / hat.shape[0]
    weighted = grad * gain
    first = jnp.sum(weighted, axis=0, keepdims=True) * scale
    second = jnp.sum(weighted * hat, axis=0, keepdims=True) * scale
    return rstd * (weighted - first - hat * second)


def whole_kernel(
    res_total,
    nbr_total,
    h0_ref,
    dh_ref,
    idx_ref,
    mask_ref,
    cnt_ref,
    edges_ref,
    dedges_ref,
    vec_ref,
    w_in,
    w_et,
    w_mid,
    w_midt,
    w_out,
    f_in,
    f_outt,
    e_int,
    e_e,
    e_hid,
    e_hidt,
    nodes_out,
    edges_out,
    g_nodes,
    g_edges,
    g_in,
    g_mid,
    g_out,
    g_fin,
    g_foutt,
    g_eint,
    g_ehid,
    g_vec,
    onehot,
    eb,
    u1,
    s1,
    s2,
    w1,
    t1,
    w2,
    t2,
    psum,
    proj,
    proj_e,
    own,
    own_e,
    state,
    ext,
    joined_a,
    joined_c,
    h1b,
    act,
    slope_f,
    ubar,
    acc_mid,
    acc_e,
    acc_z,
    acc_zs,
    acc_b2,
    acc_h2,
    acc_h3,
    acc_ee,
    acc_t,
    acc_ts,
    acc_c,
    zbuf,
    vrow,
    dcur,
    g_part,
    halo_send,
    halo_recv,
    ar_part,
    ar_one,
    ar_two,
    ar_three,
    ar_tot,
    send_sem,
    recv_sem,
):
    r = lax.axis_index("res")
    n = lax.axis_index("nbr")
    core = lax.rem(n, 2)
    buddy = n + 1 - 2 * core
    across = lax.rem(n + 2, 4)
    slots = idx_ref.shape[0]
    chunks = slots // CHUNK
    width = h0_ref.shape[0]
    ew = edges_ref.shape[1]
    half_rows = width // 2
    has_prev = r > 0
    has_next = r < res_total - 1
    sem_at = [0]
    ar_at = [0]

    def next_sem():
        at = sem_at[0]
        sem_at[0] = at + 1
        return send_sem.at[at], recv_sem.at[at]

    def remote(src, dst, device):
        ss, rs = next_sem()
        return pltpu.make_async_remote_copy(
            src_ref=src, dst_ref=dst, send_sem=ss, recv_sem=rs, device_id=device, device_id_type=MESH
        )

    def vec(layer, which, rows=None):
        at = layer * VECTORS + which
        return vec_ref[0 : (width if rows is None else rows), at : at + 1]

    def put_vec(layer, which, value):
        at = layer * VECTORS + which
        g_vec[0 : value.shape[0], at : at + 1] = jnp.sum(value, axis=1, keepdims=True)

    zero_tile = jnp.zeros((width, LANES), BF16)
    for b in range(3):
        ext[b, 0] = zero_tile
        ext[b, 2] = zero_tile
        halo_recv[b, 0] = zero_tile
        halo_recv[b, 1] = zero_tile
    barrier = pltpu.get_barrier_semaphore()
    pl.semaphore_signal(barrier, inc=1, device_id=(r, buddy), device_id_type=MESH)
    pl.semaphore_signal(barrier, inc=1, device_id=(r, across), device_id_type=MESH)

    @pl.when(has_prev)
    def _():
        pl.semaphore_signal(barrier, inc=1, device_id=(r - 1, n), device_id_type=MESH)

    @pl.when(has_next)
    def _():
        pl.semaphore_signal(barrier, inc=1, device_id=(r + 1, n), device_id_type=MESH)

    peers = 2 + jnp.minimum(r, 1) + jnp.minimum(res_total - 1 - r, 1)
    pl.semaphore_wait(barrier, peers)

    def two_way(to_prev, at_prev, to_next, at_next):
        up = remote(to_prev, at_prev, (r - 1, n))
        down = remote(to_next, at_next, (r + 1, n))

        @pl.when(has_prev)
        def _():
            up.start()

        @pl.when(has_next)
        def _():
            down.start()

        @pl.when(has_prev)
        def _():
            up.wait_send()
            down.wait_recv()

        @pl.when(has_next)
        def _():
            down.wait_send()
            up.wait_recv()

    def all_reduce(value):
        at = ar_at[0] % 2
        ar_at[0] += 1
        mine = pl.multiple_of(core * half_rows, half_rows)
        theirs = pl.multiple_of(half_rows - mine, half_rows)
        ar_part[at] = value
        one = remote(ar_part.at[at, pl.ds(theirs, half_rows)], ar_one.at[at], (r, buddy))
        one.start()
        one.wait()
        ar_two[at] = ar_part[at, pl.ds(mine, half_rows)] + ar_one[at]
        two = remote(ar_two.at[at], ar_three.at[at], (r, across))
        two.start()
        two.wait()
        ar_tot[at, pl.ds(mine, half_rows)] = ar_two[at] + ar_three[at]
        span = ar_tot.at[at, pl.ds(mine, half_rows)]
        three = remote(span, span, (r, buddy))
        three.start()
        three.wait()
        return ar_tot.at[at]

    def extended(b):
        return jnp.concatenate([ext[b, 0], ext[b, 1], ext[b, 2]], axis=1)

    def halo(b, value):
        ext[b, 1] = value
        two_way(ext.at[b, 1], ext.at[b, 2], ext.at[b, 1], ext.at[b, 0])

    def halo_back(b, g_ext, g_own):
        halo_send[0] = g_ext[:, :LANES].astype(BF16)
        halo_send[1] = g_ext[:, 2 * LANES :].astype(BF16)
        g_part[...] = g_ext[:, LANES : 2 * LANES] + g_own
        two_way(halo_send.at[0], halo_recv.at[b, 1], halo_send.at[1], halo_recv.at[b, 0])
        total = g_part[...] + halo_recv[b, 0].astype(F32) + halo_recv[b, 1].astype(F32)
        return all_reduce(total)

    cells = lax.broadcasted_iota(jnp.int32, (3 * LANES, LANES), 0)

    def make_onehot(s, _):
        onehot[s] = jnp.where(cells == idx_ref[pl.ds(s, 1), :], 1.0, 0.0).astype(BF16)
        eb[0, s] = edges_ref[s].astype(BF16)
        return 0

    lax.fori_loop(0, slots, make_onehot, 0)
    counts = cnt_ref[...]
    inv_counts = 1.0 / counts

    def prepare_message(layer):
        proj[:, : 3 * LANES] = tn(w_in[layer, width : 2 * width, :], extended(layer)).astype(BF16)
        proj[:, 3 * LANES :] = w_et[layer]
        own[...] = tn(w_in[layer, :width, :], ext[layer, 1]) + vec(layer, B1)
        ubar[layer] = jnp.zeros((width, LANES), F32)

    def prepare_edge(layer):
        proj_e[:, : 3 * LANES] = nn(e_int[layer, :, width : 2 * width], extended(layer + 1)).astype(BF16)
        proj_e[:, 3 * LANES :] = e_int[layer, :, 2 * width :]
        own_e[...] = nn(e_int[layer, :, :width], ext[layer + 1, 1]) + vec(layer, C1, ew)

    def lanes_of(ref, base, *lead):
        return jnp.concatenate([ref[(*lead, base + j)] for j in range(CHUNK)], axis=1)

    def edge_at(layer, base):
        return base if layer == 0 else slots

    def message_forward(layer, base):
        rows = jnp.concatenate([lanes_of(onehot, base), lanes_of(eb, base, layer)], axis=0)
        zbuf[...] = nn(proj[...], rows)
        for j in range(CHUNK):
            z = zbuf[:, j * LANES : (j + 1) * LANES] + own[...]
            u1[layer, base + j], s1[layer, base + j] = gelu_pair(z)
        zbuf[...] = nn(w_midt[layer], lanes_of(u1, base, layer))
        for j in range(CHUNK):
            z = zbuf[:, j * LANES : (j + 1) * LANES] + vec(layer, B2)
            u2, s2[layer, base + j] = gelu_pair(z)
            ubar[layer] += u2.astype(F32) * mask_ref[pl.ds(base + j, 1), :]

    def edge_forward(layer, base, edge_ref, save):
        rows = jnp.concatenate([lanes_of(onehot, base), lanes_of(eb, base, layer)], axis=0)
        z = nn(proj_e[...], rows)
        for j in range(CHUNK):
            zj = z[:, j * LANES : (j + 1) * LANES] + own_e[...]
            w1[edge_at(layer, base) + j], t1[edge_at(layer, base) + j] = gelu_pair(zj)
        z = nn(e_hidt[layer, 0], lanes_of(w1, edge_at(layer, base)))
        for j in range(CHUNK):
            zj = z[:, j * LANES : (j + 1) * LANES] + vec(layer, C2, ew)
            w2[edge_at(layer, base) + j], t2[edge_at(layer, base) + j] = gelu_pair(zj)
        z = nn(e_hidt[layer, 1], lanes_of(w2, edge_at(layer, base)))
        for j in range(CHUNK):
            p = edge_ref[base + j] + z[:, j * LANES : (j + 1) * LANES] + vec(layer, C3, ew)
            hat, rstd = norm_parts(p)
            save(j, hat, rstd, p, hat * vec(layer, GE, ew) + vec(layer, C4, ew))

    def node_update(layer):
        total = all_reduce(ubar[layer])[...]
        high = total.astype(BF16)
        low = (total - high.astype(F32)).astype(BF16)
        sums = tn(w_out[layer], high) + tn(w_out[layer], low) + counts * vec(layer, B3)
        merged = state[layer] + sums * inv_counts
        joined_a[layer] = merged
        hat, _ = norm_parts(merged)
        hidden = hat * vec(layer, GN1) + vec(layer, SH1)
        h1b[layer] = hidden.astype(BF16)
        pre = tn(f_in[layer], h1b[layer]) + vec(layer, FB)
        act[layer], slope_f[layer] = gelu_pair(pre)
        branch = all_reduce(nn(f_outt[layer], act[layer]))[...]
        joined = hidden + (branch + vec(layer, B5))
        joined_c[layer] = joined
        hat, _ = norm_parts(joined)
        state[layer + 1] = hat * vec(layer, GN2) + vec(layer, SH2)
        halo(layer + 1, state[layer + 1].astype(BF16))

    def clear_edge():
        acc_h2[...] = jnp.zeros_like(acc_h2)
        acc_h3[...] = jnp.zeros_like(acc_h3)
        acc_ee[...] = jnp.zeros_like(acc_ee)
        acc_t[...] = jnp.zeros_like(acc_t)
        acc_ts[...] = jnp.zeros_like(acc_ts)
        acc_c[...] = jnp.zeros_like(acc_c)

    def clear_message():
        acc_mid[...] = jnp.zeros_like(acc_mid)
        acc_e[...] = jnp.zeros_like(acc_e)
        acc_z[...] = jnp.zeros_like(acc_z)
        acc_zs[...] = jnp.zeros_like(acc_zs)
        acc_b2[...] = jnp.zeros_like(acc_b2)

    def edge_backward(layer, base, parts):
        lows = []
        for j in range(CHUNK):
            hat, rstd, grad = parts(j)
            acc_c[0] += grad * hat
            acc_c[1] += grad
            dp = norm_back(hat, rstd, vec(layer, GE, ew), grad)
            g_edges[base + j] = dp
            low = dp.astype(BF16)
            acc_c[2] += low.astype(F32)
            lows.append(low)
        out = jnp.concatenate(lows, axis=1)
        acc_h3[...] += nt(lanes_of(w2, edge_at(layer, base)), out)
        grad_two = (nn(e_hid[layer, 1], out) * lanes_of(t2, edge_at(layer, base)).astype(F32)).astype(BF16)
        for j in range(CHUNK):
            acc_c[3] += grad_two[:, j * LANES : (j + 1) * LANES].astype(F32)
        acc_h2[...] += nt(lanes_of(w1, edge_at(layer, base)), grad_two)
        grad_one = (nn(e_hid[layer, 0], grad_two) * lanes_of(t1, edge_at(layer, base)).astype(F32)).astype(BF16)
        for j in range(CHUNK):
            acc_ts[...] += grad_one[:, j * LANES : (j + 1) * LANES].astype(F32)
        acc_t[...] += nt(grad_one, lanes_of(onehot, base))
        acc_ee[...] += nt(grad_one, lanes_of(eb, base, layer))
        back = nn(e_e[layer], grad_one)
        for j in range(CHUNK):
            g_edges[base + j] += back[:, j * LANES : (j + 1) * LANES]

    def edge_finish(layer):
        put_vec(layer, GE, acc_c[0])
        put_vec(layer, C4, acc_c[1])
        put_vec(layer, C3, acc_c[2])
        put_vec(layer, C2, acc_c[3])
        put_vec(layer, C1, acc_ts[...])
        g_ehid[layer, 0] = acc_h2[...].astype(BF16)
        g_ehid[layer, 1] = acc_h3[...].astype(BF16)
        table = acc_t[...].astype(BF16)
        sums = acc_ts[...].astype(BF16)
        g_eint[layer, :, :width] = nt(sums, ext[layer + 1, 1]).astype(BF16)
        g_eint[layer, :, width : 2 * width] = nt(table, extended(layer + 1)).astype(BF16)
        g_eint[layer, :, 2 * width :] = acc_ee[...].astype(BF16)
        g_ext = tn(e_int[layer, :, width : 2 * width], table)
        g_own = tn(e_int[layer, :, :width], sums)
        return g_ext, g_own

    def message_backward(layer, base, add_edge):
        grads = []
        for j in range(CHUNK):
            s = base + j
            dz = (vrow[...] * mask_ref[pl.ds(s, 1), :] * s2[layer, s].astype(F32)).astype(BF16)
            acc_b2[...] += dz.astype(F32)
            grads.append(dz)
        grad_two = jnp.concatenate(grads, axis=1)
        acc_mid[...] += nt(lanes_of(u1, base, layer), grad_two)
        zbuf[...] = nn(w_mid[layer], grad_two)
        grads = []
        for j in range(CHUNK):
            s = base + j
            dz = (zbuf[:, j * LANES : (j + 1) * LANES] * s1[layer, s].astype(F32)).astype(BF16)
            acc_zs[...] += dz.astype(F32)
            grads.append(dz)
        grad_one = jnp.concatenate(grads, axis=1)
        acc_z[...] += nt(grad_one, lanes_of(onehot, base))
        acc_e[...] += nt(lanes_of(eb, base, layer), grad_one)
        back = nn(w_in[layer, 2 * width :, :], grad_one)
        for j in range(CHUNK):
            add_edge(base + j, back[:, j * LANES : (j + 1) * LANES])

    def message_finish(layer):
        put_vec(layer, B2, acc_b2[...])
        put_vec(layer, B1, acc_zs[...])
        g_mid[layer] = acc_mid[...].astype(BF16)
        table = acc_z[...].astype(BF16)
        sums = acc_zs[...].astype(BF16)
        g_in[layer, :width] = nt(ext[layer, 1], sums).astype(BF16)
        g_in[layer, width : 2 * width] = nt(extended(layer), table).astype(BF16)
        g_in[layer, 2 * width :] = acc_e[...].astype(BF16)
        g_ext = nn(w_in[layer, width : 2 * width, :], table)
        g_own = nn(w_in[layer, :width, :], sums)
        return g_ext, g_own

    def node_back(layer):
        grad = dcur[...]
        hat, rstd = norm_parts(joined_c[layer])
        put_vec(layer, GN2, grad * hat)
        put_vec(layer, SH2, grad)
        dc = norm_back(hat, rstd, vec(layer, GN2), grad)
        dy = dc.astype(BF16)
        put_vec(layer, B5, dy.astype(F32))
        df = (tn(f_outt[layer], dy) * slope_f[layer].astype(F32)).astype(BF16)
        put_vec(layer, FB, df.astype(F32))
        total = all_reduce(nn(f_in[layer], df))
        g_foutt[layer] = nt(dy, act[layer]).astype(BF16)
        g_fin[layer] = nt(h1b[layer], df).astype(BF16)
        grad = dc + total[...]
        hat, rstd = norm_parts(joined_a[layer])
        put_vec(layer, GN1, grad * hat)
        put_vec(layer, SH1, grad)
        da = norm_back(hat, rstd, vec(layer, GN1), grad)
        dcur[...] = da
        ds = (da * inv_counts).astype(BF16)
        put_vec(layer, B3, ds.astype(F32) * counts)
        g_out[layer] = nt(ubar[layer].astype(BF16), ds).astype(BF16)
        vrow[...] = nn(w_out[layer], ds)

    state[0] = h0_ref[...]
    halo(0, state[0].astype(BF16))
    prepare_message(0)

    def loop_a(i, _):
        message_forward(0, i * CHUNK)
        return 0

    lax.fori_loop(0, chunks, loop_a, 0)
    node_update(0)
    prepare_edge(0)
    prepare_message(1)

    def loop_b(i, _):
        base = i * CHUNK

        def save(j, hat, rstd, p, value):
            psum[base + j] = p
            edges_out[base + j] = value
            eb[1, base + j] = value.astype(BF16)

        edge_forward(0, base, edges_ref, save)
        message_forward(1, base)
        return 0

    lax.fori_loop(0, chunks, loop_b, 0)
    node_update(1)
    nodes_out[...] = state[2].T
    prepare_edge(1)
    clear_edge()

    def loop_c(i, _):
        base = i * CHUNK
        kept = {}

        def save(j, hat, rstd, p, value):
            edges_out[base + j] = value
            kept[j] = (hat, rstd)

        edge_forward(1, base, edges_out, save)
        edge_backward(1, base, lambda j: (*kept[j], dedges_ref[base + j]))
        return 0

    lax.fori_loop(0, chunks, loop_c, 0)
    g_ext, g_own = edge_finish(1)
    dcur[...] = dh_ref[...] + halo_back(0, g_ext, g_own)[...]
    node_back(1)
    clear_message()
    clear_edge()

    def loop_d(i, _):
        base = i * CHUNK

        def add_edge(s, value):
            g_edges[s] += value

        message_backward(1, base, add_edge)
        edge_backward(0, base, lambda j: (*norm_parts(psum[base + j]), g_edges[base + j]))
        return 0

    lax.fori_loop(0, chunks, loop_d, 0)
    m_ext, m_own = message_finish(1)
    e_ext, e_own = edge_finish(0)
    dcur[...] += halo_back(1, m_ext + e_ext, m_own + e_own)[...]
    node_back(0)
    clear_message()

    def loop_e(i, _):
        base = i * CHUNK

        def add_edge(s, value):
            g_edges[s] = g_edges[s] + value

        message_backward(0, base, add_edge)
        return 0

    lax.fori_loop(0, chunks, loop_e, 0)
    m_ext, m_own = message_finish(0)
    final = dcur[...] + halo_back(2, m_ext, m_own)[...]
    g_nodes[...] = final.T


def vmem(shape, dtype):
    return pltpu.VMEM(shape, dtype)


def run_whole(h0, dh, idx, mask, counts, edges, d_edges, vectors, weights, res_total, nbr_total):
    width, lanes = h0.shape
    slots, ew, _ = edges.shape
    w_in, f_in = weights[0], weights[5]
    layers, rows_in, _ = w_in.shape
    ff = f_in.shape[2]
    out_shape = (
        jax.ShapeDtypeStruct((lanes, width), F32),
        jax.ShapeDtypeStruct((slots, ew, lanes), F32),
        jax.ShapeDtypeStruct((lanes, width), F32),
        jax.ShapeDtypeStruct((slots, ew, lanes), F32),
        jax.ShapeDtypeStruct((layers, rows_in, width), BF16),
        jax.ShapeDtypeStruct((layers, width, width), BF16),
        jax.ShapeDtypeStruct((layers, width, width), BF16),
        jax.ShapeDtypeStruct((layers, width, ff), BF16),
        jax.ShapeDtypeStruct((layers, width, ff), BF16),
        jax.ShapeDtypeStruct((layers, ew, rows_in), BF16),
        jax.ShapeDtypeStruct((layers, 2, ew, ew), BF16),
        jax.ShapeDtypeStruct((width, 32), F32),
    )
    per_slot = lambda rows: vmem((layers, slots, rows, lanes), BF16)
    scratch = [
        vmem((slots, 3 * lanes, lanes), BF16),
        per_slot(ew),
        per_slot(width),
        per_slot(width),
        per_slot(width),
        vmem((slots + CHUNK, ew, lanes), BF16),
        vmem((slots + CHUNK, ew, lanes), BF16),
        vmem((slots + CHUNK, ew, lanes), BF16),
        vmem((slots + CHUNK, ew, lanes), BF16),
        vmem((slots, ew, lanes), F32),
        vmem((width, 3 * lanes + ew), BF16),
        vmem((ew, 3 * lanes + ew), BF16),
        vmem((width, lanes), F32),
        vmem((ew, lanes), F32),
        vmem((3, width, lanes), F32),
        vmem((3, 3, width, lanes), BF16),
        vmem((layers, width, lanes), F32),
        vmem((layers, width, lanes), F32),
        vmem((layers, width, lanes), BF16),
        vmem((layers, ff, lanes), BF16),
        vmem((layers, ff, lanes), BF16),
        vmem((layers, width, lanes), F32),
        vmem((width, width), F32),
        vmem((ew, width), F32),
        vmem((width, 3 * lanes), F32),
        vmem((width, lanes), F32),
        vmem((width, lanes), F32),
        vmem((ew, ew), F32),
        vmem((ew, ew), F32),
        vmem((ew, ew), F32),
        vmem((ew, 3 * lanes), F32),
        vmem((ew, lanes), F32),
        vmem((4, ew, lanes), F32),
        vmem((width, CHUNK * lanes), F32),
        vmem((width, lanes), F32),
        vmem((width, lanes), F32),
        vmem((width, lanes), F32),
        vmem((2, width, lanes), BF16),
        vmem((3, 2, width, lanes), BF16),
        vmem((2, width, lanes), F32),
        vmem((2, width // 2, lanes), F32),
        vmem((2, width // 2, lanes), F32),
        vmem((2, width // 2, lanes), F32),
        vmem((2, width, lanes), F32),
        pltpu.SemaphoreType.DMA((48,)),
        pltpu.SemaphoreType.DMA((48,)),
    ]
    operands = (h0, dh, idx, mask, counts, edges, d_edges, vectors, *weights)
    return pl.pallas_call(
        functools.partial(whole_kernel, res_total, nbr_total),
        out_shape=out_shape,
        in_specs=[pl.BlockSpec(memory_space=pltpu.VMEM)] * len(operands),
        out_specs=[pl.BlockSpec(memory_space=pltpu.VMEM)] * len(out_shape),
        scratch_shapes=scratch,
        compiler_params=pltpu.CompilerParams(
            collective_id=1, has_side_effects=True, vmem_limit_bytes=62 * 1024 * 1024
        ),
    )(*operands)


def gather_all(value, res_dim, nbr_dim):
    value = lax.all_gather(value, "res", axis=res_dim, tiled=True)
    return lax.all_gather(value, "nbr", axis=nbr_dim, tiled=True)


def scatter_sum(value, res_dim, nbr_dim):
    value = lax.psum_scatter(value, "res", scatter_dimension=res_dim, tiled=True)
    return lax.psum_scatter(value, "nbr", scatter_dimension=nbr_dim, tiled=True).astype(F32)


def per_device(
    nodes,
    edges,
    protein_ids,
    time_index,
    neighbors,
    edge_mask,
    time_table,
    msg_in,
    msg_mid,
    msg_out,
    ffn_in,
    ffn_out,
    edge_in,
    edge_hidden,
    node_gains,
    node_biases,
    ffn_bias,
    edge_gains,
    edge_biases,
    d_nodes,
    d_edges,
):
    res_total, nbr_total = lax.axis_size("res"), lax.axis_size("nbr")
    width = nodes.shape[1]
    ew = edges.shape[2]
    row_count, slot_count = neighbors.shape
    own_rows = nodes.shape[0]
    layers = msg_in.shape[0]
    n_at = lax.axis_index("nbr")
    ff = ffn_bias.shape[1] // nbr_total

    low = lambda a: a.astype(BF16)
    table_low = gather_all(low(time_table), 0, 1)
    w_in = gather_all(low(msg_in), 1, 2)
    w_mid = gather_all(low(msg_mid), 1, 2)
    w_out = gather_all(low(msg_out), 1, 2)
    e_in = gather_all(low(edge_in), 1, 2)
    e_hid = gather_all(low(edge_hidden), 2, 3)
    f_in = lax.all_gather(low(ffn_in), "res", axis=1, tiled=True)
    f_outt = lax.all_gather(jnp.swapaxes(low(ffn_out), 1, 2), "res", axis=1, tiled=True)
    weights = (
        w_in,
        jnp.swapaxes(w_in[:, 2 * width :], 1, 2),
        w_mid,
        jnp.swapaxes(w_mid, 1, 2),
        w_out,
        f_in,
        f_outt,
        jnp.swapaxes(e_in, 1, 2),
        e_in[:, 2 * width :],
        e_hid,
        jnp.swapaxes(e_hid, 2, 3),
    )
    matches = protein_ids[:, None] == jnp.arange(time_index.shape[0], dtype=jnp.int32)[None, :]
    step_rows = jnp.sum(jnp.where(matches, time_index[None, :], 0), axis=1)
    step_onehot = (
        step_rows[:, None] == jnp.arange(table_low.shape[0], dtype=jnp.int32)[None, :]
    ).astype(BF16)
    state = nodes + jnp.dot(step_onehot, table_low, preferred_element_type=F32)
    mask_rows = edge_mask.astype(F32).T
    count_row = jnp.sum(mask_rows, axis=0)
    count_block = jnp.zeros((8, width), F32).at[0, :row_count].set(count_row)
    packed = lax.all_gather(jnp.concatenate([state, d_nodes, count_block], axis=0), "nbr", axis=0)
    h0 = packed[:, :own_rows].reshape(row_count, width).T
    dh = packed[:, own_rows : 2 * own_rows].reshape(row_count, width).T
    counts = jnp.sum(packed[:, 2 * own_rows, :row_count], axis=0)[None, :]
    base_row = lax.axis_index("res") * row_count - row_count
    idx = (neighbors - base_row).T

    pad_edge = lambda a: jnp.pad(a, ((0, 0), (0, 0), (0, width - ew)))
    own_bias = lax.dynamic_slice_in_dim(ffn_bias, n_at * ff, ff, axis=1)
    table = jnp.concatenate(
        [
            node_biases,
            node_gains,
            jnp.pad(own_bias, ((0, 0), (0, width - ff)))[:, None],
            pad_edge(edge_biases),
            pad_edge(edge_gains[:, None]),
        ],
        axis=1,
    )
    vectors = jnp.pad(table.reshape(layers * VECTORS, width), ((0, 32 - layers * VECTORS), (0, 0))).T

    results = run_whole(
        h0,
        dh,
        idx,
        mask_rows,
        counts,
        jnp.transpose(edges, (1, 2, 0)),
        jnp.transpose(d_edges, (1, 2, 0)),
        vectors,
        weights,
        res_total,
        nbr_total,
    )
    nodes_all, edges_t, g_nodes_all, g_edges_t, g_in, g_mid, g_out, g_fin, g_foutt, g_eint, g_ehid, g_vec = results
    mine = lambda a: lax.dynamic_slice_in_dim(a, n_at * own_rows, own_rows, axis=0)
    g_nodes = mine(g_nodes_all)
    g_table_full = lax.dot_general(
        step_onehot.astype(F32),
        g_nodes,
        (((0,), (0,)), ((), ())),
        precision=lax.Precision.HIGHEST,
        preferred_element_type=F32,
    )
    g_rows = g_vec.T[: layers * VECTORS].reshape(layers, VECTORS, width)
    shared = g_rows[:, B3 : GN2 + 1] * (1.0 / nbr_total)
    g_bias_ffn = lax.dynamic_update_slice_in_dim(
        jnp.zeros_like(ffn_bias), g_rows[:, FB, :ff], n_at * ff, axis=1
    )
    g_node_biases, g_node_gains, g_ffn_bias, g_edge_biases, g_edge_gains = lax.psum(
        (
            jnp.concatenate([g_rows[:, : B3], shared[:, : SH2 + 1 - B3]], axis=1),
            shared[:, GN1 - B3 :],
            g_bias_ffn,
            g_rows[:, C1 : C4 + 1, :ew],
            g_rows[:, GE, :ew],
        ),
        ("res", "nbr"),
    )
    return (
        mine(nodes_all),
        jnp.transpose(edges_t, (2, 0, 1)),
        g_nodes,
        jnp.transpose(g_edges_t, (2, 0, 1)),
        scatter_sum(low(g_table_full), 0, 1),
        scatter_sum(g_in, 1, 2),
        scatter_sum(g_mid, 1, 2),
        scatter_sum(g_out, 1, 2),
        lax.psum_scatter(g_fin, "res", scatter_dimension=1, tiled=True).astype(F32),
        jnp.swapaxes(
            lax.psum_scatter(g_foutt, "res", scatter_dimension=1, tiled=True), 1, 2
        ).astype(F32),
        jnp.swapaxes(scatter_sum(g_eint, 2, 1), 1, 2),
        scatter_sum(g_ehid, 2, 3),
        g_node_gains,
        g_node_biases,
        g_ffn_bias,
        g_edge_gains,
        g_edge_biases,
    )


def solution(mesh):
    return jax.shard_map(
        per_device,
        mesh=mesh,
        in_specs=(
            P(("res", "nbr"), None),
            P("res", "nbr", None),
            P(("res", "nbr")),
            P(),
            P("res", "nbr"),
            P("res", "nbr"),
            P("res", "nbr"),
            P(None, "res", "nbr"),
            P(None, "res", "nbr"),
            P(None, "res", "nbr"),
            P(None, "res", "nbr"),
            P(None, "nbr", "res"),
            P(None, "res", "nbr"),
            P(None, None, "res", "nbr"),
            P(),
            P(),
            P(),
            P(),
            P(),
            P(("res", "nbr"), None),
            P("res", "nbr", None),
        ),
        out_specs=(
            P(("res", "nbr"), None),
            P("res", "nbr", None),
            P(("res", "nbr"), None),
            P("res", "nbr", None),
            P("res", "nbr"),
            P(None, "res", "nbr"),
            P(None, "res", "nbr"),
            P(None, "res", "nbr"),
            P(None, "res", "nbr"),
            P(None, "nbr", "res"),
            P(None, "res", "nbr"),
            P(None, None, "res", "nbr"),
            P(),
            P(),
            P(),
            P(),
            P(),
        ),
        check_vma=False,
    )
```

time: 1290 us -> 1120 us (0.87); the launches traced: 1280 us -> 1120 us
  waiting for transfers between devices: 372 us -> 607 us
  local copies, waits for them, and re-layouts: 256 us -> 62.6 us
  Pallas kernels: 0 us -> 164 us
  matrix products: 164 us -> 1.23 us
  other arithmetic: 159 us -> 10.6 us
  starting transfers between devices: 75.6 us -> 1.04 us
  blocking collectives: 233 us -> 260 us
    unnamed x24 -> x28, waiting for transfers between devices: 59.9 us -> 306 us
    pallas_call x0 -> x1, Pallas kernels: none -> 164 us  [run_whole(): pl.pallas_call(functools.partial(whole_kernel, res_total, nbr_total), out...]
    dot_general x50 -> x2, matrix products: 164 us -> 1.23 us  [the longest x1 1.03 us: per_device(): lax.dot_general(step_onehot.astype(F32), g_nodes, (((0,), (0,)), ((), ())...]
    reduce_scatter x9 -> x5, waiting for transfers between devices: 157 us -> 301 us  [the longest x3 172 us: scatter_sum(): lax.psum_scatter(value, 'res', scatter_dimension=res_dim, tiled=True)]
    all_gather x5, waiting for transfers between devices: 139 us -> 0.01 us  [the longest x3 0.01 us: gather_all(): return lax.all_gather(value, 'nbr', axis=nbr_dim, tiled=True)]
    reshape x20 -> x5, local copies, waits for them, and re-layouts: 76.2 us -> 1.82 us  [the longest x1 0.84 us: per_device(): h0 = packed[:, :own_rows].reshape(row_count, width).T]
    scatter-add x4 -> x0, other arithmetic: 55.7 us -> none  [spread_back(): jnp.zeros((3 * row_count, node_width), jnp.float32)]
    ppermute x14 -> x0, starting transfers between devices: 39.7 us -> none  [the longest x7 30.6 us: padded(): lax.ppermute(tail, axis, [(i, (i + 1) % count) for i in range(ends)])]
  transfers between devices with their start and end apart: 40 -> 19, of which waited for: 19 -> 12; matrix products, arithmetic and copies ran while one was open for 19% -> 6% of each run, Pallas kernels for 0% -> 0%
where the time goes in v1:
time: 1120 us
  waiting for transfers between devices  607 us (54%)
  blocking collectives  260 us (23%)
  Pallas kernels  164 us (15%)
  local copies, waits for them, and re-layouts  62.6 us (6%)
  between operations  15.9 us (1%)
    unnamed x28, waiting for transfers between devices  306 us
    all_gather x6, blocking collectives, gather_all(): value = lax.all_gather(value, 'res', axis=res_dim, tiled=True)  190 us
    reduce_scatter x3, waiting for transfers between devices, scatter_sum(): lax.psum_scatter(value, 'res', scatter_dimension=res_dim, tiled=True)  172 us
    pallas_call x1, Pallas kernels, run_whole(): pl.pallas_call(functools.partial(whole_kernel, res_total, nbr_total), out...  164 us
    reduce_scatter x1, waiting for transfers between devices, per_device(): lax.psum_scatter(g_fin, 'res', scatter_dimension=1, tiled=True).astype(F32)  65.6 us
    reduce_scatter x1, waiting for transfers between devices, per_device(): lax.psum_scatter(g_foutt, 'res', scatter_dimension=1, tiled=True)  64.1 us
    psum x1, blocking collectives, per_device(): lax.psum((jnp.concatenate([g_rows[:, :B3], shared[:, :SH2 + 1 - B3]], axi...  41.1 us
    unnamed x93, local copies, waits for them, and re-layouts  39.6 us
  transfers between devices with their start and end apart: 19, of which 12 were waited for; matrix products, arithmetic and copies ran while one was open for 6% of the time, Pallas kernels for 0%

profile of v1, /device:TPU:0, one launch (start us, length us, event | category | flops | bytes accessed | tf_op | source)
XLA Modules:
  0.0 1121.9 jit_solution(7762604889138812671)
XLA Ops:
  8.1 32.5 %all_gather.54 = bf16[2,512,128]{2,0,1:T(2,128)(2,1)S(1)} all-gather(bf16[2,64,128]{2,0,1:T(2,128)(2,1)S(1)} %copy.197), channel_id=1, replica_groups=mesh['res'=8,'nbr'=4] {'res'}, dimensions={1}, use_global_device_ids=true | all-gather | bytes 294912 | tf_op jit(solution)/shard_map/all_gather | solution.py:614
  42.6 31.6 %all_gather.52 = bf16[2,1216,128]{2,0,1:T(2,128)(2,1)S(1)} all-gather(bf16[2,152,128]{2,0,1:T(2,128)(2,1)S(1)} %copy.196), channel_id=1, replica_groups=mesh['res'=8,'nbr'=4] {'res'}, dimensions={1}, use_global_device_ids=true | all-gather | bytes 700416 | tf_op jit(solution)/shard_map/all_gather | solution.py:614
  76.2 32.7 %all_gather.56 = bf16[2,512,128]{2,1,0:T(8,128)(2,1)} all-gather(bf16[2,64,128]{2,1,0:T(8,128)(2,1)S(1)} %convert_element_type.67), channel_id=1, replica_groups=mesh['res'=8,'nbr'=4] {'res'}, dimensions={1}, use_global_device_ids=true | all-gather | bytes 294912 | tf_op jit(solution)/shard_map/all_gather | solution.py:614
  110.7 31.5 %all_gather.60 = bf16[2,1216,48]{2,0,1:T(2,128)(2,1)S(1)} all-gather(bf16[2,152,48]{2,0,1:T(2,128)(2,1)S(1)} %copy.153), channel_id=1, replica_groups=mesh['res'=8,'nbr'=4] {'res'}, dimensions={1}, use_global_device_ids=true | all-gather | bytes 262656 | tf_op jit(solution)/shard_map/all_gather | solution.py:614
  143.0 9.6 all_gather.61
  154.8 30.6 %all_gather.48 = bf16[128,128]{1,0:T(8,128)(2,1)S(1)} all-gather(bf16[16,128]{1,0:T(8,128)(2,1)S(1)} %convert_element_type.63), channel_id=1, replica_groups=mesh['res'=8,'nbr'=4] {'res'}, dimensions={0}, use_global_device_ids=true | all-gather | bytes 36864 | tf_op jit(solution)/shard_map/all_gather | solution.py:614
  191.2 7.8 all-gather
  201.6 30.7 %all_gather.62 = bf16[2,2,192,48]{3,1,0,2:T(2,128)(2,1)S(1)} all-gather(bf16[2,2,24,48]{3,1,0,2:T(2,128)(2,1)S(1)} %copy.198), channel_id=1, replica_groups=mesh['res'=8,'nbr'=4] {'res'}, dimensions={2}, use_global_device_ids=true | all-gather | bytes 82944 | tf_op jit(solution)/shard_map/all_gather | solution.py:614
  232.4 6.1 all_gather.63
  250.6 163.5 %shard_map.332 = (f32[128,512]{1,0:T(8,128)}, f32[15,192,128]{2,1,0:T(8,128)}, f32[128,512]{1,0:T(8,128)}, f32[15,192,128]{2,1,0:T(8,128)}, bf16[2,1216,512]{2,1...) custom-call(f32[512,128]{1,0:T(8,128)} %bitcast.76, ...), custom_call_target="tpu_custom_call" | custom-call | tf_op jit(solution)/shard_map/pallas_call | solution.py:601
  423.3 9.7 copy.169
  435.3 44.6 %reduce-scatter.27.cloned.1.call-done = bf16[16,512]{1,0:T(8,128)(2,1)} async-done(((bf16[128,512]{1,0:T(8,128)(2,1)}), bf16[16,512]{1,0:T(8,128)(2,1)}) %reduce-scatter.27.cloned.1.call-update) | async-done | bytes 16400 | tf_op jit(solution)/shard_map/reduce_scatter | solution.py:619
  482.7 59.0 %reduce-scatter.47.cloned.1.call-done = bf16[24,768]{1,0:T(8,128)(2,1)} async-done(((bf16[192,768]{1,0:T(8,128)(2,1)}), bf16[24,768]{1,0:T(8,128)(2,1)}) %reduce-scatter.47.cloned.1.call-update) | async-done | bytes 36880
  543.6 83.2 %all-reduce.10.cloned.1.call-done = bf16[2,192,1216]{1,0,2:T(2,128)(2,1)} async-done(((bf16[2,192,1216]{1,0,2:T(2,128)(2,1)}), bf16[2,192,1216]{1,0,2:T(2,128)(2,1)}) %all-reduce.10.cloned.1.call-update) | async-done | bytes 933904
  630.0 63.3 %reduce-scatter.29.cloned.1.call-done = bf16[2,64,512]{2,1,0:T(8,128)(2,1)} async-done(((bf16[2,512,512]{2,1,0:T(8,128)(2,1)}), bf16[2,64,512]{2,1,0:T(8,128)(2,1)}) %reduce-scatter.29.cloned.1.call-update) | async-done | bytes 131088 | tf_op jit(solution)/shard_map/reduce_scatter | solution.py:619
  695.2 63.9 %reduce-scatter.31.cloned.1.call-done = bf16[2,64,512]{2,1,0:T(8,128)(2,1)} async-done(((bf16[2,512,512]{2,1,0:T(8,128)(2,1)}), bf16[2,64,512]{2,1,0:T(8,128)(2,1)}) %reduce-scatter.31.cloned.1.call-update) | async-done | bytes 131088 | tf_op jit(solution)/shard_map/reduce_scatter | solution.py:619
  762.5 69.4 %reduce-scatter.39.cloned.1.call-done = bf16[152,1024]{1,0:T(8,128)(2,1)} async-done(((bf16[1216,1024]{1,0:T(8,128)(2,1)}), bf16[152,1024]{1,0:T(8,128)(2,1)}) %reduce-scatter.39.cloned.1.call-update) | async-done | bytes 311312
  835.1 41.1 %all-reduce.6 = (f32[2,2,512]{2,1,0:T(2,128)}, f32[2,6,512]{2,1,0:T(8,128)S(1)}, f32[2,2048]{1,0:T(2,128)}, f32[2,192]{1,0:T(2,128)}, f32[2,4,192]{2,1,0:T(4,128)}) all-reduce(f32[2,2,512]{2,1,0:T(2,128)S(1)} %slice.75, f32[2,6,512]{2,1,0:T(8,128)S(1)} %pad_maximum_fusion, ...), channel_id=1, replica_groups=mesh['res'=8,'nbr'=4] {'res','nbr'}, use_global_device_ids=true, to_apply=%region_17.18 | all-reduce | flops 14208 | bytes 113664 | tf_op jit(solution)/shard_map/psum | solution.py:735
  881.3 29.0 %all-reduce.12.cloned.1.call-done = bf16[2,192,152]{2,0,1:T(2,128)(2,1)} async-done(((bf16[2,192,152]{2,0,1:T(2,128)(2,1)}), bf16[2,192,152]{2,0,1:T(2,128)(2,1)}) %all-reduce.12.cloned.1.call-update) | async-done | bytes 116752
  911.7 65.6 %reduce-scatter.33.cloned.1.call-done = bf16[2,64,512]{2,1,0:T(8,128)(2,1)} async-done(((bf16[2,512,512]{2,1,0:T(8,128)(2,1)}), bf16[2,64,512]{2,1,0:T(8,128)(2,1)}) %reduce-scatter.33.cloned.1.call-update) | async-done | bytes 131088 | tf_op jit(solution)/shard_map/reduce_scatter | solution.py:754
  978.9 64.1 %reduce-scatter.35.cloned.1.call-done = bf16[2,64,512]{2,1,0:T(8,128)(2,1)} async-done(((bf16[2,512,512]{2,1,0:T(8,128)(2,1)}), bf16[2,64,512]{2,1,0:T(8,128)(2,1)}) %reduce-scatter.35.cloned.1.call-update) | async-done | bytes 131088 | tf_op jit(solution)/shard_map/reduce_scatter | solution.py:756
  1044.6 20.0 %reduce-scatter.43.cloned.1.call-done = bf16[128,128]{1,0:T(8,128)(2,1)} async-done(((bf16[512,128]{1,0:T(8,128)(2,1)}), bf16[128,128]{1,0:T(8,128)(2,1)}) %reduce-scatter.43.cloned.1.call-update) | async-done | bytes 32784
  1066.2 20.3 %reduce-scatter.45.cloned.1.call-done = bf16[128,128]{1,0:T(8,128)(2,1)} async-done(((bf16[512,128]{1,0:T(8,128)(2,1)}), bf16[128,128]{1,0:T(8,128)(2,1)}) %reduce-scatter.45.cloned.1.call-update) | async-done | bytes 32784
  1088.1 22.5 %reduce-scatter.41.cloned.1.call-done = bf16[128,304]{1,0:T(8,128)(2,1)} async-done(((bf16[512,304]{1,0:T(8,128)(2,1)}), bf16[128,304]{1,0:T(8,128)(2,1)}) %reduce-scatter.41.cloned.1.call-update) | async-done | bytes 77840
  (195 shorter events, 73.7 us)
Async XLA Ops:
  7.2 234.8 %all-gather.9.cloned.1.call-start = ((), (), s32[]{:S(2)}) async-start(), calls=%async_computation.13 | async-start | bytes 1310720 | tf_op jit(solution)/shard_map/all_gather | solution.py:615
  41.6 202.7 %all-gather.7.cloned.1.call-start = ((), (), s32[]{:S(2)}) async-start(), calls=%async_computation.12 | async-start | bytes 3276800 | tf_op jit(solution)/shard_map/all_gather | solution.py:615
  42.6 66.4 %copy-start.8 = (f32[2,64,512]{2,1,0:T(8,128)S(1)}, f32[2,64,512]{2,1,0:T(8,128)}, u32[]{:S(2)}) copy-start(f32[2,64,512]{2,1,0:T(8,128)} %param.33) | copy-start | bytes 786436
  76.1 174.5 %all-gather.11.cloned.1.call-start = ((), (), s32[]{:S(2)}) async-start(), calls=%async_computation.14 | async-start | bytes 1310720 | tf_op jit(solution)/shard_map/all_gather | solution.py:615
  108.9 141.6 %all-gather.13.cloned.1.call-start = ((), (), s32[]{:S(2)}) async-start(), calls=%async_computation.15 | async-start | bytes 1179648 | tf_op jit(solution)/shard_map/all_gather | solution.py:662
  109.7 140.9 %all-gather.15.cloned.1.call-start = ((), (), s32[]{:S(2)}) async-start(), calls=%async_computation.16 | async-start | bytes 1179648 | tf_op jit(solution)/shard_map/all_gather | solution.py:663
  110.5 369.5 %reduce-scatter.27.cloned.1.call-start = ((), (), s32[]{:S(2)}) async-start(), calls=%async_computation.17 | async-start | bytes 147456 | tf_op jit(solution)/shard_map/reduce_scatter | solution.py:619
  416.1 125.6 %reduce-scatter.47.cloned.1.call-start = ((), (), s32[]{:S(2)}) async-start(), calls=%async_computation.27 | async-start | bytes 331776
  418.9 207.9 %all-reduce.10.cloned.1.call-start = ((), (), s32[]{:S(2)}) async-start(), calls=%async_computation.29 | async-start | bytes 2490368
  421.6 271.6 %reduce-scatter.29.cloned.1.call-start = ((), (), s32[]{:S(2)}) async-start(), calls=%async_computation.18 | async-start | bytes 1179648 | tf_op jit(solution)/shard_map/reduce_scatter | solution.py:619
  422.4 336.7 %reduce-scatter.31.cloned.1.call-start = ((), (), s32[]{:S(2)}) async-start(), calls=%async_computation.19 | async-start | bytes 1179648 | tf_op jit(solution)/shard_map/reduce_scatter | solution.py:619
  423.0 408.9 %reduce-scatter.39.cloned.1.call-start = ((), (), s32[]{:S(2)}) async-start(), calls=%async_computation.23 | async-start | bytes 2801664
  435.2 46.3 %copy-start.25 = (u32[32]{0:T(128)S(1)}, u32[32]{0:T(128)}, u32[]{:S(2)}) copy-start(u32[32]{0:T(128)} %constant.67) | copy-start | bytes 388
  435.2 443.1 %reduce-scatter.37.cloned.1.call-start = ((), (), s32[]{:S(2)}) async-start(), calls=%async_computation.22 | async-start | bytes 163840
  481.4 398.3 %reduce-scatter.49.cloned.1.call-start = ((), (), s32[]{:S(2)}) async-start(), calls=%async_computation.28 | async-start | bytes 61440
  543.5 366.7 %all-reduce.12.cloned.1.call-start = ((), (), s32[]{:S(2)}) async-start(), calls=%async_computation.30 | async-start | bytes 393216
  628.7 348.6 %reduce-scatter.33.cloned.1.call-start = ((), (), s32[]{:S(2)}) async-start(), calls=%async_computation.20 | async-start | bytes 1179648 | tf_op jit(solution)/shard_map/reduce_scatter | solution.py:754
  629.3 131.7 %copy-start.24 = (u32[32]{0:T(128)S(1)}, u32[32]{0:T(128)}, u32[]{:S(2)}) copy-start(u32[32]{0:T(128)} %constant.71) | copy-start | bytes 388
  629.3 133.0 %copy-start.6 = (f32[512,32]{1,0:T(8,128)S(1)}, f32[512,32]{1,0:T(8,128)}, u32[]{:S(2)}) copy-start(f32[512,32]{1,0:T(8,128)} %get-tuple-element.52) | copy-start | bytes 196612
  629.3 413.7 %reduce-scatter.35.cloned.1.call-start = ((), (), s32[]{:S(2)}) async-start(), calls=%async_computation.21 | async-start | bytes 1179648 | tf_op jit(solution)/shard_map/reduce_scatter | solution.py:756
  629.9 434.7 %reduce-scatter.43.cloned.1.call-start = ((), (), s32[]{:S(2)}) async-start(), calls=%async_computation.25 | async-start | bytes 163840
  695.2 391.3 %reduce-scatter.45.cloned.1.call-start = ((), (), s32[]{:S(2)}) async-start(), calls=%async_computation.26 | async-start | bytes 163840
  761.0 349.6 %reduce-scatter.41.cloned.1.call-start = ((), (), s32[]{:S(2)}) async-start(), calls=%async_computation.24 | async-start | bytes 491520
  835.1 277.3 %copy-start.4 = (f32[15,192,128]{2,1,0:T(8,128)S(1)}, f32[15,192,128]{2,1,0:T(8,128)}, u32[]{:S(2)}) copy-start(f32[15,192,128]{2,1,0:T(8,128)} %get-tuple-element.42) | copy-start | bytes 4423684
  (22 other events, 386.4 us)
Sparse Core Ops, SparseCore 0:
  41.7 17.7 all-gather.8
  76.2 26.6 all-gather.6
  109.1 18.0 all-gather.10
  129.8 40.2 all-gather.12
  172.1 39.0 all-gather.14
  416.2 63.6 reduce-scatter.26
  483.8 57.8 reduce-scatter.46
  545.8 80.9 all-reduce.9
  630.6 62.5 reduce-scatter.28
  696.5 62.5 reduce-scatter.30
  763.0 68.7 reduce-scatter.38
  834.7 18.4 reduce-scatter.36
  856.3 19.3 reduce-scatter.48
  878.5 31.6 all-reduce.11
  913.9 63.3 reduce-scatter.32
  980.5 62.4 reduce-scatter.34
  1046.0 18.5 reduce-scatter.42
  1066.9 19.5 reduce-scatter.44
  1089.7 20.8 reduce-scatter.40

commit v2 on v1

v2 whole, which is shorter than its diff:
```python
import functools

import jax
import jax.numpy as jnp
from jax import lax
from jax.experimental import pallas as pl
from jax.experimental.pallas import tpu as pltpu
from jax.sharding import PartitionSpec as P

NORM_EPS = 1e-05
F32 = jnp.float32
BF16 = jnp.bfloat16
MESH = pl.DeviceIdType.MESH
LANES = 128
CHUNK = 5
TANH_A = 0.7978845608028654
TANH_B = 0.044715
B1, B2, B3, B5, SH1, SH2, GN1, GN2, FB, C1, C2, C3, C4, GE = range(14)
VECTORS = 14
VEC_ROWS = {B1: 0, B2: 1, B3: 2, B5: 3, SH1: 4, SH2: 5, GN1: 6, GN2: 7, FB: 8, C1: 12, C2: 13, C3: 14, C4: 15, GE: 16}
VEC_PER_LAYER = 20
IN0, TB, MO0, FF0, ED, IN1, MO1, FF1 = range(8)
IN, MO, FF = (IN0, IN1), (MO0, MO1), (FF0, FF1)
BY_CORE, BY_X, BY_Y, BY_Z = range(4)


def nn(left, right):
    return jnp.dot(left, right, preferred_element_type=F32)


def nt(left, right):
    return lax.dot_general(left, right, (((1,), (1,)), ((), ())), preferred_element_type=F32)


def tn(left, right):
    return lax.dot_general(left, right, (((0,), (0,)), ((), ())), preferred_element_type=F32)


def gelu_pair(z):
    sq = z * z
    half = 0.5 + 0.5 * jnp.tanh(z * (TANH_A + (TANH_A * TANH_B) * sq))
    value = z * half
    slope = half + (value * (1.0 - half)) * (2.0 * TANH_A + (6.0 * TANH_A * TANH_B) * sq)
    return value.astype(BF16), slope.astype(BF16)


def norm_parts(value):
    scale = 1.0 / value.shape[0]
    centre = jnp.sum(value, axis=0, keepdims=True) * scale
    offset = value - centre
    spread = jnp.sum(offset * offset, axis=0, keepdims=True) * scale
    rstd = lax.rsqrt(spread + NORM_EPS)
    return offset * rstd, rstd


def norm_back(hat, rstd, gain, grad):
    scale = 1.0 / hat.shape[0]
    weighted = grad * gain
    first = jnp.sum(weighted, axis=0, keepdims=True) * scale
    second = jnp.sum(weighted * hat, axis=0, keepdims=True) * scale
    return rstd * (weighted - first - hat * second)


class Refs:
    def __init__(self, names, values):
        self.__dict__.update(zip(names, values, strict=True))


def up_to(value, step):
    return (value + step - 1) // step * step


class Plan:
    def __init__(self, res_total, nbr_total, slots, width, ew, ff, layers, shards):
        self.res_total, self.nbr_total = res_total, nbr_total
        self.slots, self.width, self.ew, self.ff, self.layers = slots, width, ew, ff, layers
        self.k_in, self.k_mid, self.k_hid, self.k_time = shards
        self.fast = (res_total, nbr_total) == (8, 4) and self.k_in % 8 == 0 and self.k_mid % 16 == 0
        acts = slots * width
        self.acts = [0, 3 * acts]
        self.act_rows = acts
        edge_rows = (slots + CHUNK) * ew
        self.pool_rows = 6 * acts + 4 * edge_rows
        self.edge_at = 6 * acts
        self.edge_rows = edge_rows
        if not self.fast:
            return
        self.in_pad = up_to(self.k_in, 16)
        self.hid_pad = up_to(self.k_hid, 16)
        self.in_rows = self.in_pad
        self.mo_rows = 2 * self.k_mid
        self.ed_rows = self.in_pad + 2 * self.hid_pad
        self.tb_rows = self.k_time
        self.ff_rows = 2 * self.k_mid * (ff // LANES)
        one = 3 * acts
        sizes = {IN0: self.in_rows, MO0: self.mo_rows, ED: self.ed_rows, IN1: self.in_rows,
                 MO1: self.mo_rows, TB: self.tb_rows, FF0: self.ff_rows, FF1: self.ff_rows}
        self.sizes = sizes
        self.stage = {}
        at = 0
        for item in (IN0, TB, MO0):
            self.stage[item] = at
            at += 32 * sizes[item]
        at = one
        for item in (IN1, MO1, ED):
            self.stage[item] = at
            at += 32 * sizes[item]
        for item in (FF0, FF1):
            self.stage[item] = at
            at += 8 * sizes[item]
        top = at
        self.source, self.recv = {}, {}
        at = 0
        for item in (IN0, MO0):
            self.source[item] = at
            at += 32 * sizes[item]
        at = one
        for item in (IN1, MO1, ED):
            self.source[item] = at
            at += 32 * sizes[item]
        for stage, count in ((BY_CORE, 16), (BY_X, 8), (BY_Y, 4)):
            self.recv[ED, stage] = at
            at += count * sizes[ED]
        at = max(at, 2 * one)
        self.source[FF1] = at
        self.recv[FF1, BY_Y] = at + 8 * sizes[FF1]
        at += 12 * sizes[FF1]
        for stage, count in ((BY_CORE, 16), (BY_X, 8), (BY_Y, 4)):
            for item, twin in ((IN1, IN0), (MO1, MO0)):
                self.recv[item, stage] = self.recv[twin, stage] = at
                at += count * sizes[item]
        top = max(top, at)
        self.edge_at = top
        self.source[FF0] = top
        self.recv[FF0, BY_Y] = top + 8 * sizes[FF0]
        at = top + max(4 * edge_rows, 12 * sizes[FF0])
        self.source[TB] = at
        at += 32 * sizes[TB]
        for stage, count in ((BY_CORE, 16), (BY_X, 8), (BY_Y, 4)):
            self.recv[TB, stage] = at
            at += count * sizes[TB]
        for item in sizes:
            self.recv[item, BY_Z] = at
            at += 3 * sizes[item]
        self.pool_rows = at


def whole_kernel(plan, names, *values):
    refs = Refs(names, values)
    fast = plan.fast
    mask_ref, vec_ref = refs.mask_rows, refs.vectors
    onehot, eb, pool, psum, proj, proj_e = refs.onehot, refs.eb, refs.pool, refs.psum, refs.proj, refs.proj_e
    own, own_e, state, ext = refs.own, refs.own_e, refs.state, refs.ext
    joined_a, joined_c, h1b, act = refs.joined_a, refs.joined_c, refs.h1b, refs.act
    slope_f, ubar, ds_ref = refs.slope_f, refs.ubar, refs.ds
    acc_mid, acc_e, acc_z, acc_zs, acc_b2 = refs.acc_mid, refs.acc_e, refs.acc_z, refs.acc_zs, refs.acc_b2
    acc_h2, acc_h3, acc_ee = refs.acc_h2, refs.acc_h3, refs.acc_ee
    acc_t, acc_ts, acc_c = refs.acc_t, refs.acc_ts, refs.acc_c
    wide, vrow, dcur, g_part = refs.wide, refs.vrow, refs.dcur, refs.g_part
    halo_send, halo_recv = refs.halo_send, refs.halo_recv
    ar_part, ar_one, ar_two, ar_three = refs.ar_part, refs.ar_one, refs.ar_two, refs.ar_three
    ar_tot = refs.ar_tot
    w_in, w_et, w_mid, w_midt, w_out = refs.w_in, refs.w_et, refs.w_mid, refs.w_midt, refs.w_out
    f_in, f_outt, e_int, e_e = refs.f_in, refs.f_outt, refs.e_int, refs.e_e
    e_hid, e_hidt = refs.e_hid, refs.e_hidt
    nodes_out, edges_out, g_nodes, g_edges = refs.nodes_out, refs.edges_out, refs.g_nodes, refs.g_edges
    cnt_ref = refs.counts
    res_total = plan.res_total
    slots, width, ew, ff = plan.slots, plan.width, plan.ew, plan.ff
    r = lax.axis_index("res")
    n = lax.axis_index("nbr")
    core = lax.rem(n, 2)
    xx = n // 2
    yy = lax.rem(r, 2)
    zz = r // 2
    buddy = n + 1 - 2 * core
    across = lax.rem(n + 2, 4)
    chunks = slots // CHUNK
    half_rows = width // 2
    has_prev = r > 0
    has_next = r < res_total - 1
    sem_at = [0]
    ar_at = [0]

    greeted = [(r, buddy), (r, across)]
    z_peers = []
    if fast:
        greeted.append((r, lax.rem(buddy + 2, 4)))
        y_peer = (r + 1 - 2 * yy, n)
        z_peers = [(2 * lax.rem(zz + k, 4) + yy, n) for k in (1, 2, 3)]
        greeted += [y_peer, *z_peers]
        up_too = jnp.logical_and(yy == 0, has_prev)
        down_too = jnp.logical_and(yy == 1, has_next)
    else:
        up_too, down_too = has_prev, has_next
    barrier = pltpu.get_barrier_semaphore()
    for device in greeted:
        pl.semaphore_signal(barrier, inc=1, device_id=device, device_id_type=MESH)

    @pl.when(up_too)
    def _():
        pl.semaphore_signal(barrier, inc=1, device_id=(r - 1, n), device_id_type=MESH)

    @pl.when(down_too)
    def _():
        pl.semaphore_signal(barrier, inc=1, device_id=(r + 1, n), device_id_type=MESH)

    greetings = (len(greeted) + up_too.astype(jnp.int32) + down_too.astype(jnp.int32))

    zero_tile = jnp.zeros((width, LANES), BF16)

    @pl.when(jnp.logical_not(has_prev))
    def _():
        for b in range(3):
            ext[b, 0] = zero_tile
            halo_recv[b, 0] = zero_tile

    @pl.when(jnp.logical_not(has_next))
    def _():
        for b in range(3):
            ext[b, 2] = zero_tile
            halo_recv[b, 1] = zero_tile

    def next_sem():
        at = sem_at[0]
        sem_at[0] = at + 1
        return refs.send_sem.at[at], refs.recv_sem.at[at]

    def remote(src, dst, device):
        ss, rs = next_sem()
        return pltpu.make_async_remote_copy(
            src_ref=src, dst_ref=dst, send_sem=ss, recv_sem=rs, device_id=device, device_id_type=MESH
        )

    def start(copies):
        for copy in copies:
            copy.start()

    def wait(copies):
        for copy in copies:
            copy.wait()

    def rows_of(at, count):
        return pool.at[pl.ds(at, count)]

    def aligned(at):
        return pl.multiple_of(at, 16)

    def vec(layer, which, rows=None):
        at = layer * VECTORS + which
        return vec_ref[0 : (width if rows is None else rows), at : at + 1]

    def put_vec(layer, which, value):
        at = layer * VECTORS + which
        refs.g_vec[0 : value.shape[0], at : at + 1] = jnp.sum(value, axis=1, keepdims=True)

    load_edges = pltpu.make_async_copy(refs.edges, g_edges, refs.local_sem.at[0])
    load_edges.start()

    def two_way(to_prev, at_prev, to_next, at_next):
        up = remote(to_prev, at_prev, (r - 1, n))
        down = remote(to_next, at_next, (r + 1, n))

        def begin():
            pl.when(has_prev)(up.start)
            pl.when(has_next)(down.start)

        def finish():
            @pl.when(has_prev)
            def _():
                up.wait_send()
                down.wait_recv()

            @pl.when(has_next)
            def _():
                down.wait_send()
                up.wait_recv()

        return begin, finish

    def all_reduce(value, short=False):
        at = ar_at[0] % 2
        ar_at[0] += 1
        mine = pl.multiple_of(core * half_rows, half_rows)
        theirs = pl.multiple_of(half_rows - mine, half_rows)
        ar_part[at] = value
        one = remote(ar_part.at[at, pl.ds(theirs, half_rows)], ar_one.at[at], (r, buddy))
        one.start()
        one.wait()
        sent, got = (refs.ar_two_low, refs.ar_three_low) if short else (ar_two, ar_three)
        sent[at] = (ar_part[at, pl.ds(mine, half_rows)] + ar_one[at]).astype(sent.dtype)
        two = remote(sent.at[at], got.at[at], (r, across))
        two.start()
        two.wait()
        ar_tot[at, pl.ds(mine, half_rows)] = sent[at].astype(F32) + got[at].astype(F32)
        span = ar_tot.at[at, pl.ds(mine, half_rows)]
        three = remote(span, span, (r, buddy))
        three.start()
        three.wait()
        return ar_tot.at[at]

    def extended(b):
        return jnp.concatenate([ext[b, 0], ext[b, 1], ext[b, 2]], axis=1)

    def halo(b, value):
        ext[b, 1] = value
        begin, finish = two_way(ext.at[b, 1], ext.at[b, 2], ext.at[b, 1], ext.at[b, 0])
        begin()
        return finish

    def halo_back(b, g_ext, g_own):
        halo_send[0] = g_ext[:, :LANES].astype(BF16)
        halo_send[1] = g_ext[:, 2 * LANES :].astype(BF16)
        g_part[...] = g_ext[:, LANES : 2 * LANES] + g_own
        begin, finish = two_way(halo_send.at[0], halo_recv.at[b, 1], halo_send.at[1], halo_recv.at[b, 0])
        begin()
        finish()
        total = g_part[...] + halo_recv[b, 0].astype(F32) + halo_recv[b, 1].astype(F32)
        return all_reduce(total, short=True)

    FULL = (IN0, MO0, TB, ED, IN1, MO1)
    shard_at = ((core * 2 + xx) * 2 + yy) * 4 + zz
    short_at = yy * 4 + zz

    def my_shard(item):
        at = shard_at if item in FULL else short_at
        return aligned(plan.stage[item] + at * plan.sizes[item])

    def gather_z(item):
        size = plan.sizes[item]
        span = rows_of(my_shard(item), size)
        return [remote(span, span, peer) for peer in z_peers]

    def gather_span(item, count, device):
        size = plan.sizes[item]
        at = shard_at if item in FULL else short_at
        span = rows_of(aligned(plan.stage[item] + (at // count) * (count * size)), count * size)
        return [remote(span, span, device)]

    def gather_y(item):
        return gather_span(item, 4, y_peer)

    def gather_x(item):
        return gather_span(item, 8, (r, across))

    def gather_c(item):
        return gather_span(item, 16, (r, buddy))

    def add_rows(at, other, count):
        block = next(b for b in (512, 256, 128, 64, 32, 16) if count % b == 0)

        def step(i, _):
            to = pl.ds(aligned(at + i * block), block)
            pool[to] = (pool[to].astype(F32) + pool[pl.ds(aligned(other + i * block), block)].astype(F32)).astype(BF16)
            return 0

        lax.fori_loop(0, count // block, step, 0)

    def reduce_pairs(item, stage):
        size, source = plan.sizes[item], plan.source[item]
        if stage == BY_CORE:
            count, mine, theirs, device = 16, core, 1 - core, (r, buddy)
        elif stage == BY_X:
            count, mine, theirs, device = 8, core * 2 + xx, core * 2 + 1 - xx, (r, across)
        else:
            base = (core * 2 + xx) * 2 if item in FULL else 0
            count, mine, theirs, device = 4, base + yy, base + 1 - yy, y_peer
        arrived = plan.recv[item, stage]
        copy = remote(
            rows_of(aligned(source + theirs * (count * size)), count * size),
            rows_of(arrived, count * size),
            device,
        )
        return [copy], lambda: add_rows(aligned(source + mine * (count * size)), arrived, count * size)

    def reduce_z(item):
        size, source = plan.sizes[item], plan.source[item]
        base = ((core * 2 + xx) * 2 + yy) * 4 if item in FULL else yy * 4
        copies = []
        for k in (1, 2, 3):
            to = lax.rem(zz + k, 4)
            copies.append(
                remote(
                    rows_of(aligned(source + (base + to) * size), size),
                    rows_of(plan.recv[item, BY_Z] + (k - 1) * size, size),
                    z_peers[k - 1],
                )
            )

        def total(first, count):
            value = pool[pl.ds(aligned(source + (base + zz) * size + first), count)].astype(F32)
            for k in range(3):
                value += pool[pl.ds(plan.recv[item, BY_Z] + k * size + first, count)].astype(F32)
            return value

        return copies, total

    def blocks():
        for at in range(32):
            c, x, y, z = at // 16, at // 8 % 2, at // 4 % 2, at % 4
            yield at, 2 * z + y, 2 * x + c

    def assemble_in(layer):
        at = plan.stage[IN[layer]]
        for k, rr, nn_ in blocks():
            wide[rr * plan.k_in : (rr + 1) * plan.k_in, nn_ * LANES : (nn_ + 1) * LANES] = pool[
                at + k * plan.in_rows : at + k * plan.in_rows + plan.k_in
            ].astype(F32)
        w_in[layer] = wide[: w_in.shape[1], :width].astype(BF16)
        turned = wide[2 * width : 2 * width + 2 * LANES, :width].T
        w_et[layer] = turned[:, :ew].astype(BF16)

    def assemble_mo(layer):
        at = plan.stage[MO[layer]]
        k_mid = plan.k_mid
        for k, rr, nn_ in blocks():
            to = (layer, slice(rr * k_mid, (rr + 1) * k_mid), slice(nn_ * LANES, (nn_ + 1) * LANES))
            first = at + k * plan.mo_rows
            w_mid[to] = pool[first : first + k_mid]
            w_out[to] = pool[first + k_mid : first + 2 * k_mid]
        w_midt[layer] = w_mid[layer].astype(F32).T.astype(BF16)

    def turn_square(value):
        wide[:ew, :ew] = value
        return wide[: 2 * LANES, : 2 * LANES].T[:ew, :ew]

    def assemble_edge():
        at, cols = plan.stage[ED], ew // 4
        long = up_to(w_in.shape[1], LANES)
        for k, rr, nn_ in blocks():
            first = at + k * plan.ed_rows
            wide[rr * plan.k_in : (rr + 1) * plan.k_in, nn_ * LANES : (nn_ + 1) * LANES] = pool[
                first : first + plan.k_in
            ].astype(F32)
        for nn_ in range(4):
            turned = wide[:long, nn_ * LANES : (nn_ + 1) * LANES].T
            for layer in range(2):
                e_int[layer, nn_ * cols : (nn_ + 1) * cols] = turned[
                    layer * cols : (layer + 1) * cols, : w_in.shape[1]
                ].astype(BF16)
        for layer in range(2):
            for k, rr, nn_ in blocks():
                first = at + k * plan.ed_rows + plan.in_pad + layer * plan.hid_pad
                wide[rr * plan.k_hid : (rr + 1) * plan.k_hid, nn_ * LANES : (nn_ + 1) * LANES] = pool[
                    first : first + plan.k_hid
                ].astype(F32)
            for nn_ in range(4):
                turned = wide[: 2 * LANES, nn_ * LANES : (nn_ + 1) * LANES].T
                for m in range(2):
                    e_hidt[layer, m, nn_ * cols : (nn_ + 1) * cols] = turned[
                        m * cols : (m + 1) * cols, :ew
                    ].astype(BF16)
        for layer in range(2):
            e_e[layer] = turn_square(e_int[layer, :, 2 * width :].astype(F32)).astype(BF16)
            for m in range(2):
                e_hid[layer, m] = turn_square(e_hidt[layer, m].astype(F32)).astype(BF16)

    def assemble_ffn(layer):
        at, k_mid = plan.stage[FF[layer]], plan.k_mid
        for y in range(2):
            for z in range(4):
                rr = 2 * z + y
                for j in range(ff // LANES):
                    for m, ref in enumerate((f_in, f_outt)):
                        first = at + (y * 4 + z) * plan.ff_rows + (m * (ff // LANES) + j) * k_mid
                        ref[layer, rr * k_mid : (rr + 1) * k_mid, j * LANES : (j + 1) * LANES] = pool[
                            first : first + k_mid
                        ]

    def emit_ffn(layer, g_fin, g_foutt):
        if not fast:
            refs.g_fin[layer] = g_fin.astype(BF16)
            refs.g_foutt[layer] = g_foutt.astype(BF16)
            return
        at, k_mid = plan.source[FF[layer]], plan.k_mid
        for m, value in enumerate((g_fin.astype(BF16), g_foutt.astype(BF16))):
            for y in range(2):
                for z in range(4):
                    rr = 2 * z + y
                    for j in range(ff // LANES):
                        first = at + (y * 4 + z) * plan.ff_rows + (m * (ff // LANES) + j) * k_mid
                        pool[first : first + k_mid] = value[
                            rr * k_mid : (rr + 1) * k_mid, j * LANES : (j + 1) * LANES
                        ]

    def emit_message(layer, g_own_rows, g_other_rows, g_edge_rows, g_mid, g_out):
        if not fast:
            refs.g_in[layer, :width] = g_own_rows.astype(BF16)
            refs.g_in[layer, width : 2 * width] = g_other_rows.astype(BF16)
            refs.g_in[layer, 2 * width :] = g_edge_rows.astype(BF16)
            refs.g_mid[layer] = g_mid.astype(BF16)
            refs.g_out[layer] = g_out.astype(BF16)
            return
        wide[:width, :width] = g_own_rows
        wide[width : 2 * width, :width] = g_other_rows
        wide[2 * width : 2 * width + ew, :width] = g_edge_rows
        at = plan.source[IN[layer]]
        for k, rr, nn_ in blocks():
            first = at + k * plan.in_rows
            pool[first : first + plan.k_in] = wide[
                rr * plan.k_in : (rr + 1) * plan.k_in, nn_ * LANES : (nn_ + 1) * LANES
            ].astype(BF16)
        at, k_mid = plan.source[MO[layer]], plan.k_mid
        for m, value in enumerate((g_mid.astype(BF16), g_out.astype(BF16))):
            for k, rr, nn_ in blocks():
                first = at + k * plan.mo_rows + m * k_mid
                pool[first : first + k_mid] = value[
                    rr * k_mid : (rr + 1) * k_mid, nn_ * LANES : (nn_ + 1) * LANES
                ]

    def emit_edge_all():
        at, cols = plan.source[ED], ew // 4
        long = up_to(w_in.shape[1], LANES)
        fill = LANES - 2 * cols
        for nn_ in range(4):
            span = slice(nn_ * cols, (nn_ + 1) * cols)
            tall = jnp.concatenate(
                [refs.g_eint[0, span].astype(F32), refs.g_eint[1, span].astype(F32), jnp.zeros((fill, long), F32)],
                axis=0,
            ).T
            wide[:long, nn_ * LANES : (nn_ + 1) * LANES] = tall
        for k, rr, nn_ in blocks():
            first = at + k * plan.ed_rows
            pool[first : first + plan.k_in] = wide[
                rr * plan.k_in : (rr + 1) * plan.k_in, nn_ * LANES : (nn_ + 1) * LANES
            ].astype(BF16)
        for layer in range(2):
            for nn_ in range(4):
                span = slice(nn_ * cols, (nn_ + 1) * cols)
                tall = jnp.concatenate(
                    [refs.g_ehid[layer, m, span].astype(F32) for m in range(2)]
                    + [jnp.zeros((fill, 2 * LANES), F32)],
                    axis=0,
                ).T
                wide[: 2 * LANES, nn_ * LANES : (nn_ + 1) * LANES] = tall
            for k, rr, nn_ in blocks():
                first = at + k * plan.ed_rows + plan.in_pad + layer * plan.hid_pad
                pool[first : first + plan.k_hid] = wide[
                    rr * plan.k_hid : (rr + 1) * plan.k_hid, nn_ * LANES : (nn_ + 1) * LANES
                ].astype(BF16)

    def act_at(kind, layer, slot):
        return pl.ds(aligned(plan.acts[layer] + kind * plan.act_rows + slot * width), width)

    U1, S1, S2 = 0, 1, 2
    W1, T1, W2, T2 = 0, 1, 2, 3

    def edge_act(kind, layer, base, j):
        slot = base + j if layer == 0 else slots + j
        return pl.ds(aligned(plan.edge_at + kind * plan.edge_rows + slot * ew), ew)

    def acts(kind, layer, base):
        return jnp.concatenate([pool[act_at(kind, layer, base + j)] for j in range(CHUNK)], axis=1)

    def edge_acts(kind, layer, base):
        return jnp.concatenate([pool[edge_act(kind, layer, base, j)] for j in range(CHUNK)], axis=1)

    def lanes_of(ref, base, *lead):
        return jnp.concatenate([ref[(*lead, base + j)] for j in range(CHUNK)], axis=1)

    def make_vectors():
        refs.g_vec[...] = jnp.zeros_like(refs.g_vec)
        mask_ref[...] = refs.mask[...].astype(F32)
        for layer in range(plan.layers):
            at = layer * VECTORS
            for k in range(6):
                wide[at + k : at + k + 1, :width] = refs.node_biases[k, layer : layer + 1]
            wide[at + GN1 : at + GN2 + 1, :width] = refs.node_gains[layer]
            first = pl.multiple_of(n * ff, ff)
            wide[at + FB : at + FB + 1, :ff] = refs.ffn_bias[layer : layer + 1, pl.ds(first, ff)]
            wide[at + C1 : at + C4 + 1, :ew] = refs.edge_biases[layer]
            wide[at + GE : at + GE + 1, :ew] = refs.edge_gains[layer : layer + 1]
        vec_ref[...] = wide[:LANES, :width].T

    def make_onehot():
        cells = lax.broadcasted_iota(jnp.int32, (3 * LANES, LANES), 0) + (r - 1) * LANES

        def step(s, _):
            onehot[s] = jnp.where(cells == refs.neighbors[pl.ds(s, 1), :], 1.0, 0.0).astype(BF16)
            eb[0, s] = g_edges[s].astype(BF16)
            return 0

        load_edges.wait()
        lax.fori_loop(0, slots, step, 0)

    def prepare_message(layer):
        proj[:, : 3 * LANES] = tn(w_in[layer, width : 2 * width, :], extended(layer)).astype(BF16)
        proj[:, 3 * LANES :] = w_et[layer]
        own[...] = tn(w_in[layer, :width, :], ext[layer, 1]) + vec(layer, B1)
        ubar[layer] = jnp.zeros((width, LANES), F32)

    def prepare_edge(layer):
        proj_e[:, : 3 * LANES] = nn(e_int[layer, :, width : 2 * width], extended(layer + 1)).astype(BF16)
        proj_e[:, 3 * LANES :] = e_int[layer, :, 2 * width :]
        own_e[...] = nn(e_int[layer, :, :width], ext[layer + 1, 1]) + vec(layer, C1, ew)

    def message_forward(layer, base):
        rows = jnp.concatenate([lanes_of(onehot, base), lanes_of(eb, base, layer)], axis=0)
        wide[:width, :] = nn(proj[...], rows)
        for j in range(CHUNK):
            z = wide[:width, j * LANES : (j + 1) * LANES] + own[...]
            pool[act_at(U1, layer, base + j)], pool[act_at(S1, layer, base + j)] = gelu_pair(z)
        wide[:width, :] = nn(w_midt[layer], acts(U1, layer, base))
        for j in range(CHUNK):
            z = wide[:width, j * LANES : (j + 1) * LANES] + vec(layer, B2)
            u2, pool[act_at(S2, layer, base + j)] = gelu_pair(z)
            ubar[layer] += u2.astype(F32) * mask_ref[pl.ds(base + j, 1), :]

    def edge_forward(layer, base, edge_ref, save):
        rows = jnp.concatenate([lanes_of(onehot, base), lanes_of(eb, base, layer)], axis=0)
        z = nn(proj_e[...], rows)
        for j in range(CHUNK):
            zj = z[:, j * LANES : (j + 1) * LANES] + own_e[...]
            pool[edge_act(W1, layer, base, j)], pool[edge_act(T1, layer, base, j)] = gelu_pair(zj)
        z = nn(e_hidt[layer, 0], edge_acts(W1, layer, base))
        for j in range(CHUNK):
            zj = z[:, j * LANES : (j + 1) * LANES] + vec(layer, C2, ew)
            pool[edge_act(W2, layer, base, j)], pool[edge_act(T2, layer, base, j)] = gelu_pair(zj)
        z = nn(e_hidt[layer, 1], edge_acts(W2, layer, base))
        for j in range(CHUNK):
            p = edge_ref[base + j] + z[:, j * LANES : (j + 1) * LANES] + vec(layer, C3, ew)
            hat, rstd = norm_parts(p)
            save(j, hat, rstd, p, hat * vec(layer, GE, ew) + vec(layer, C4, ew))

    def node_update(layer, before_ffn=lambda: None):
        total = all_reduce(ubar[layer])[...]
        high = total.astype(BF16)
        low = (total - high.astype(F32)).astype(BF16)
        counts = cnt_ref[...]
        sums = tn(w_out[layer], high) + tn(w_out[layer], low) + counts * vec(layer, B3)
        merged = state[layer] + sums * (1.0 / counts)
        joined_a[layer] = merged
        hat, _ = norm_parts(merged)
        hidden = hat * vec(layer, GN1) + vec(layer, SH1)
        h1b[layer] = hidden.astype(BF16)
        before_ffn()
        pre = tn(f_in[layer], h1b[layer]) + vec(layer, FB)
        act[layer], slope_f[layer] = gelu_pair(pre)
        branch = all_reduce(nn(f_outt[layer], act[layer]))[...]
        joined = hidden + (branch + vec(layer, B5))
        joined_c[layer] = joined
        hat, _ = norm_parts(joined)
        state[layer + 1] = hat * vec(layer, GN2) + vec(layer, SH2)
        return halo(layer + 1, state[layer + 1].astype(BF16))

    def clear_edge():
        for ref in (acc_h2, acc_h3, acc_ee, acc_t, acc_ts, acc_c):
            ref[...] = jnp.zeros_like(ref)

    def clear_message():
        for ref in (acc_mid, acc_e, acc_z, acc_zs, acc_b2):
            ref[...] = jnp.zeros_like(ref)

    def edge_backward(layer, base, parts):
        lows = []
        for j in range(CHUNK):
            hat, rstd, grad = parts(j)
            acc_c[0] += grad * hat
            acc_c[1] += grad
            dp = norm_back(hat, rstd, vec(layer, GE, ew), grad)
            g_edges[base + j] = dp
            low = dp.astype(BF16)
            acc_c[2] += low.astype(F32)
            lows.append(low)
        out = jnp.concatenate(lows, axis=1)
        acc_h3[...] += nt(out, edge_acts(W2, layer, base))
        grad_two = (nn(e_hid[layer, 1], out) * edge_acts(T2, layer, base).astype(F32)).astype(BF16)
        for j in range(CHUNK):
            acc_c[3] += grad_two[:, j * LANES : (j + 1) * LANES].astype(F32)
        acc_h2[...] += nt(grad_two, edge_acts(W1, layer, base))
        grad_one = (nn(e_hid[layer, 0], grad_two) * edge_acts(T1, layer, base).astype(F32)).astype(BF16)
        for j in range(CHUNK):
            acc_ts[...] += grad_one[:, j * LANES : (j + 1) * LANES].astype(F32)
        acc_t[...] += nt(grad_one, lanes_of(onehot, base))
        acc_ee[...] += nt(grad_one, lanes_of(eb, base, layer))
        back = nn(e_e[layer], grad_one)
        for j in range(CHUNK):
            g_edges[base + j] += back[:, j * LANES : (j + 1) * LANES]

    def edge_finish(layer):
        put_vec(layer, GE, acc_c[0])
        put_vec(layer, C4, acc_c[1])
        put_vec(layer, C3, acc_c[2])
        put_vec(layer, C2, acc_c[3])
        put_vec(layer, C1, acc_ts[...])
        refs.g_ehid[layer, 0, :, :ew] = acc_h2[...].astype(BF16)
        refs.g_ehid[layer, 1, :, :ew] = acc_h3[...].astype(BF16)
        table = acc_t[...].astype(BF16)
        sums = acc_ts[...].astype(BF16)
        refs.g_eint[layer, :, :width] = nt(sums, ext[layer + 1, 1]).astype(BF16)
        refs.g_eint[layer, :, width : 2 * width] = nt(table, extended(layer + 1)).astype(BF16)
        refs.g_eint[layer, :, 2 * width : 2 * width + ew] = acc_ee[...].astype(BF16)
        g_ext = tn(e_int[layer, :, width : 2 * width], table)
        g_own = tn(e_int[layer, :, :width], sums)
        return g_ext, g_own

    def message_backward(layer, base, add_edge):
        grads = []
        for j in range(CHUNK):
            s = base + j
            slope = pool[act_at(S2, layer, s)].astype(F32)
            dz = (vrow[...] * mask_ref[pl.ds(s, 1), :] * slope).astype(BF16)
            acc_b2[...] += dz.astype(F32)
            grads.append(dz)
        grad_two = jnp.concatenate(grads, axis=1)
        acc_mid[...] += nt(acts(U1, layer, base), grad_two)
        wide[:width, :] = nn(w_mid[layer], grad_two)
        grads = []
        for j in range(CHUNK):
            slope = pool[act_at(S1, layer, base + j)].astype(F32)
            dz = (wide[:width, j * LANES : (j + 1) * LANES] * slope).astype(BF16)
            acc_zs[...] += dz.astype(F32)
            grads.append(dz)
        grad_one = jnp.concatenate(grads, axis=1)
        acc_z[...] += nt(grad_one, lanes_of(onehot, base))
        acc_e[...] += nt(lanes_of(eb, base, layer), grad_one)
        back = nn(w_in[layer, 2 * width :, :], grad_one)
        for j in range(CHUNK):
            add_edge(base + j, back[:, j * LANES : (j + 1) * LANES])

    def message_finish(layer):
        put_vec(layer, B2, acc_b2[...])
        put_vec(layer, B1, acc_zs[...])
        table = acc_z[...].astype(BF16)
        sums = acc_zs[...].astype(BF16)
        emit_message(
            layer,
            nt(ext[layer, 1], sums),
            nt(extended(layer), table),
            acc_e[...],
            acc_mid[...],
            nt(ubar[layer].astype(BF16), ds_ref[...]),
        )
        g_ext = nn(w_in[layer, width : 2 * width, :], table)
        g_own = nn(w_in[layer, :width, :], sums)
        return g_ext, g_own

    def node_back(layer, meanwhile=lambda: None):
        counts = cnt_ref[...]
        grad = dcur[...]
        hat, rstd = norm_parts(joined_c[layer])
        put_vec(layer, GN2, grad * hat)
        put_vec(layer, SH2, grad)
        dc = norm_back(hat, rstd, vec(layer, GN2), grad)
        dy = dc.astype(BF16)
        put_vec(layer, B5, dy.astype(F32))
        df = (tn(f_outt[layer], dy) * slope_f[layer].astype(F32)).astype(BF16)
        put_vec(layer, FB, df.astype(F32))
        part = nn(f_in[layer], df)
        meanwhile()
        total = all_reduce(part, short=True)
        emit_ffn(layer, nt(h1b[layer], df), nt(dy, act[layer]))
        grad = dc + total[...]
        hat, rstd = norm_parts(joined_a[layer])
        put_vec(layer, GN1, grad * hat)
        put_vec(layer, SH1, grad)
        da = norm_back(hat, rstd, vec(layer, GN1), grad)
        dcur[...] = da
        ds = (da * (1.0 / counts)).astype(BF16)
        ds_ref[...] = ds
        put_vec(layer, B3, ds.astype(F32) * counts)
        vrow[...] = nn(w_out[layer], ds)

    if fast:
        own_rows = refs.nodes.shape[0]
        mine = pl.multiple_of(n * own_rows, own_rows)
        k_mid = plan.k_mid

        def pack_in(layer):
            pool[pl.ds(my_shard(IN[layer]), plan.k_in)] = refs.msg_in[layer].astype(BF16)

        def pack_mo(layer):
            at = my_shard(MO[layer])
            pool[pl.ds(at, k_mid)] = refs.msg_mid[layer].astype(BF16)
            pool[pl.ds(aligned(at + k_mid), k_mid)] = refs.msg_out[layer].astype(BF16)

        def pack_ffn(layer):
            at = my_shard(FF[layer])
            for m, ref in enumerate((refs.ffn_in, refs.ffn_outt)):
                for j in range(ff // LANES):
                    to = aligned(at + (m * (ff // LANES) + j) * k_mid)
                    pool[pl.ds(to, k_mid)] = ref[layer, :, j * LANES : (j + 1) * LANES].astype(BF16)

        def pack_edge():
            cols = ew // 4
            for layer in range(2):
                wide[layer * cols : (layer + 1) * cols, : plan.k_in] = refs.edge_in_t[layer]
            turned = wide[:LANES, : 2 * LANES].T
            at = my_shard(ED)
            pool[pl.ds(at, plan.k_in)] = turned[: plan.k_in].astype(BF16)
            for layer in range(2):
                for m in range(2):
                    wide[: plan.k_hid, m * cols : (m + 1) * cols] = refs.edge_hidden[layer, m]
                to = aligned(at + plan.in_pad + layer * plan.hid_pad)
                pool[pl.ds(to, plan.k_hid)] = wide[: plan.k_hid, :LANES].astype(BF16)

        pack_in(0)
        pool[pl.ds(my_shard(TB), plan.tb_rows)] = refs.time_table[...].astype(BF16)
        refs.all_nodes[pl.ds(mine, own_rows)] = refs.nodes[...]
        refs.all_dnodes[pl.ds(mine, own_rows)] = refs.d_nodes[...]
        steps = jnp.zeros((1, own_rows), jnp.int32)
        for p in range(refs.time_index.shape[0]):
            steps += jnp.where(refs.protein_ids[...] == p, refs.time_index[p], 0)
        refs.all_misc[n, 0:1, :] = jnp.sum(refs.mask[...].astype(F32), axis=0, keepdims=True)
        refs.all_misc[n, 1:2, :own_rows] = steps.astype(F32)
        pl.semaphore_wait(barrier, greetings)

        node_copies, late_copies = [], []
        for k in (1, 2, 3):
            peer = (r, lax.rem(n + k, 4))
            for ref, group in (
                (refs.all_nodes.at[pl.ds(mine, own_rows)], node_copies),
                (refs.all_misc.at[n], node_copies),
                (refs.all_dnodes.at[pl.ds(mine, own_rows)], late_copies),
            ):
                group.append(remote(ref, ref, peer))
        every = range(FF1 + 1)
        gz = {item: gather_z(item) for item in every}
        gy = {item: gather_y(item) for item in every}
        gx = {item: gather_x(item) for item in FULL}
        gc = {item: gather_c(item) for item in FULL}

        def pass_on(before, after, *items):
            for item in items:
                wait(before[item])
                start(after[item])

        def first(stage, *items):
            for item in items:
                start(stage[item])

        first(gz, IN0, TB)
        start(node_copies)
        pack_mo(0)
        pack_edge()
        make_vectors()
        pass_on(gz, gy, IN0, TB)
        first(gz, MO0, ED)
        pack_ffn(0)
        pack_in(1)
        pack_mo(1)
        pack_ffn(1)
        make_onehot()
        pass_on(gy, gx, IN0, TB)
        pass_on(gz, gy, MO0, ED)
        first(gz, FF0, IN1, MO1)
        wait(node_copies)
        misc = refs.all_misc[0]
        for k in range(1, 4):
            misc += refs.all_misc[k]
        cnt_ref[...] = misc[0:1]
        steps = jnp.concatenate([refs.all_misc[k, 1:2, :own_rows] for k in range(4)], axis=1)
        times = lax.broadcasted_iota(jnp.int32, (8 * plan.k_time, LANES), 0).astype(F32)
        refs.time_hot[...] = jnp.where(times == steps, 1.0, 0.0).astype(BF16)
        nodes_t = refs.all_nodes[...].T
        pass_on(gx, gc, IN0, TB)
        pass_on(gy, gx, MO0)
        wait(gc[TB])
        for k, rr, nn_ in blocks():
            at = plan.stage[TB] + k * plan.tb_rows
            refs.time_rows[rr * plan.k_time : (rr + 1) * plan.k_time, nn_ * LANES : (nn_ + 1) * LANES] = pool[
                at : at + plan.tb_rows
            ]
        state[0] = nodes_t + tn(refs.time_rows[...], refs.time_hot[...])
        finish = halo(0, state[0].astype(BF16))
        wait(gc[IN0])
        assemble_in(0)
        pass_on(gx, gc, MO0)
        pass_on(gy, gx, ED)
        finish()
        wait(gc[MO0])
        assemble_mo(0)
    else:
        make_vectors()
        make_onehot()
        pl.semaphore_wait(barrier, greetings)
        state[0] = refs.h0[...]
        halo(0, state[0].astype(BF16))()

    prepare_message(0)

    def loop_a(i, _):
        message_forward(0, i * CHUNK)
        if fast:

            @pl.when(i == 1)
            def _():
                pass_on(gz, gy, FF0)

            @pl.when(i == 2)
            def _():
                pass_on(gz, gy, IN1, MO1)
                first(gz, FF1)
                start(late_copies)

        return 0

    lax.fori_loop(0, chunks, loop_a, 0)

    def need_ffn0():
        if fast:
            pass_on(gx, gc, ED)
            pass_on(gy, gx, IN1, MO1)
            wait(gy[FF0])
            assemble_ffn(0)

    finish = node_update(0, need_ffn0)
    if fast:
        pass_on(gz, gy, FF1)
        wait(gc[ED])
        assemble_edge()
        pass_on(gx, gc, IN1, MO1)
        wait(gc[IN1])
        assemble_in(1)
        wait(gc[MO1])
        assemble_mo(1)
        wait(gy[FF1])
        assemble_ffn(1)
        wait(late_copies)
    finish()
    prepare_edge(0)
    prepare_message(1)

    def loop_b(i, _):
        base = i * CHUNK

        def save(j, hat, rstd, p, value):
            psum[base + j] = p
            edges_out[base + j] = value
            eb[1, base + j] = value.astype(BF16)

        edge_forward(0, base, g_edges, save)
        message_forward(1, base)
        return 0

    lax.fori_loop(0, chunks, loop_b, 0)
    load_grads = pltpu.make_async_copy(refs.d_edges, g_edges, refs.local_sem.at[1])
    load_grads.start()
    finish = node_update(1)
    if fast:
        refs.all_nodes[...] = state[2].T
        nodes_out[...] = refs.all_nodes[pl.ds(mine, own_rows)]
    else:
        nodes_out[...] = state[2].T
    clear_edge()
    load_grads.wait()
    finish()
    prepare_edge(1)

    def loop_c(i, _):
        base = i * CHUNK
        kept = {}

        def save(j, hat, rstd, p, value):
            edges_out[base + j] = value
            kept[j] = (hat, rstd)

        edge_forward(1, base, edges_out, save)
        edge_backward(1, base, lambda j: (*kept[j], g_edges[base + j]))
        return 0

    lax.fori_loop(0, chunks, loop_c, 0)
    g_ext, g_own = edge_finish(1)
    dh = refs.all_dnodes[...].T if fast else refs.dh[...]
    dcur[...] = dh + halo_back(0, g_ext, g_own)[...]
    node_back(1)
    clear_message()
    clear_edge()
    reduce_c, reduce_x, reduce_y, reduce_last = {}, {}, {}, {}
    if fast:
        for item in range(FF1 + 1):
            if item in FULL:
                reduce_c[item] = reduce_pairs(item, BY_CORE)
                reduce_x[item] = reduce_pairs(item, BY_X)
            reduce_y[item] = reduce_pairs(item, BY_Y)
            reduce_last[item] = reduce_z(item)

    def reduce_on(before, after, *items):
        for item in items:
            wait(before[item][0])
            before[item][1]()
            start(after[item][0])

    def put_ffn(layer):
        copies, total = reduce_last[FF[layer]]
        wait(copies)
        k_mid, parts = plan.k_mid, ff // LANES
        for m, ref in enumerate((refs.o_fin, refs.o_foutt)):
            for j in range(parts):
                ref[layer, :, j * LANES : (j + 1) * LANES] = total((m * parts + j) * k_mid, k_mid)

    def put_message(layer):
        copies, total = reduce_last[IN[layer]]
        wait(copies)
        refs.o_in[layer] = total(0, plan.k_in)
        copies, total = reduce_last[MO[layer]]
        wait(copies)
        refs.o_mid[layer] = total(0, plan.k_mid)
        refs.o_out[layer] = total(plan.k_mid, plan.k_mid)

    def put_edge():
        copies, total = reduce_last[ED]
        wait(copies)
        cols = ew // 4
        wide[: plan.in_pad, :LANES] = total(0, plan.in_pad)
        turned = wide[: 2 * LANES, :LANES].T
        hidden = total(plan.in_pad, 2 * plan.hid_pad)
        for layer in range(2):
            refs.o_edge[layer] = turned[layer * cols : (layer + 1) * cols, : plan.k_in]
            first = layer * plan.hid_pad
            for m in range(2):
                refs.o_hid[layer, m] = hidden[first : first + plan.k_hid, m * cols : (m + 1) * cols]

    if fast:
        start(reduce_y[FF1][0])

    def loop_d1(i, _):
        base = i * CHUNK

        def add_edge(s, value):
            g_edges[s] += value

        message_backward(1, base, add_edge)
        return 0

    lax.fori_loop(0, chunks, loop_d1, 0)
    m_ext, m_own = message_finish(1)
    acc_z[...] = m_ext
    acc_zs[...] = m_own
    if fast:
        start(reduce_c[IN1][0])
        start(reduce_c[MO1][0])
        reduce_on(reduce_y, reduce_last, FF1)

    def loop_d2(i, _):
        base = i * CHUNK
        edge_backward(0, base, lambda j: (*norm_parts(psum[base + j]), g_edges[base + j]))
        if fast:

            @pl.when(i == 0)
            def _():
                reduce_on(reduce_c, reduce_x, IN1, MO1)

        return 0

    lax.fori_loop(0, chunks, loop_d2, 0)
    e_ext, e_own = edge_finish(0)
    if fast:
        emit_edge_all()
        start(reduce_c[ED][0])
    dcur[...] += halo_back(1, acc_z[...] + e_ext, acc_zs[...] + e_own)[...]
    if fast:
        put_ffn(1)
        reduce_on(reduce_x, reduce_y, IN1, MO1)
    node_back(0)
    clear_message()
    if fast:
        reduce_on(reduce_c, reduce_x, ED)
        start(reduce_y[FF0][0])

    def loop_e(i, _):
        base = i * CHUNK

        def add_edge(s, value):
            g_edges[s] += value

        message_backward(0, base, add_edge)
        if fast:

            @pl.when(i == 2)
            def _():
                reduce_on(reduce_y, reduce_last, IN1, MO1)

        return 0

    lax.fori_loop(0, chunks, loop_e, 0)
    m_ext, m_own = message_finish(0)
    if fast:
        start(reduce_c[IN0][0])
        start(reduce_c[MO0][0])
        reduce_on(reduce_x, reduce_y, ED)
        reduce_on(reduce_c, reduce_x, IN0)
        reduce_on(reduce_y, reduce_last, FF0)
    final = dcur[...] + halo_back(2, m_ext, m_own)[...]
    if not fast:
        g_nodes[...] = final.T
        return
    refs.all_dnodes[...] = final.T
    g_nodes[...] = refs.all_dnodes[pl.ds(mine, own_rows)]

    high = final.astype(BF16)
    low = (final - high.astype(F32)).astype(BF16)
    g_times = (nt(refs.time_hot[...], high) + nt(refs.time_hot[...], low)) * (1.0 / plan.nbr_total)
    for k, rr, nn_ in blocks():
        at = plan.source[TB] + k * plan.tb_rows
        pool[at : at + plan.tb_rows] = g_times[
            rr * plan.k_time : (rr + 1) * plan.k_time, nn_ * LANES : (nn_ + 1) * LANES
        ].astype(BF16)
    start(reduce_c[TB][0])
    table = refs.g_vec[...].T
    sums = refs.vec_sums
    sums[0] = jnp.zeros_like(sums[0])
    for layer in range(2):
        for which, row in VEC_ROWS.items():
            value = table[layer * VECTORS + which : layer * VECTORS + which + 1]
            at = layer * VEC_PER_LAYER + row
            if which == FB:
                sums[0, pl.ds(at + n, 1)] = value
            else:
                scale = 1.0 / plan.nbr_total if B3 <= which <= GN2 else 1.0
                sums[0, at : at + 1] = value * scale
    partners = [(r, buddy), (r, across), y_peer]
    partners += [(2 * (zz + 1 - 2 * lax.rem(zz, 2)) + yy, n), (2 * lax.rem(zz + 2, 4) + yy, n)]
    rounds = [remote(sums.at[2 * k], sums.at[2 * k + 1], partners[k]) for k in range(5)]

    def vec_round(k):
        rounds[k].wait()
        sums[2 * k + 2] = sums[2 * k] + sums[2 * k + 1]
        if k < 4:
            rounds[k + 1].start()

    rounds[0].start()
    reduce_on(reduce_x, reduce_y, IN0)
    reduce_on(reduce_c, reduce_x, MO0, TB)
    vec_round(0)
    reduce_on(reduce_y, reduce_last, ED)
    put_message(1)
    vec_round(1)
    reduce_on(reduce_y, reduce_last, IN0)
    reduce_on(reduce_x, reduce_y, TB, MO0)
    vec_round(2)
    reduce_on(reduce_y, reduce_last, TB, MO0)
    vec_round(3)
    put_ffn(0)
    put_edge()
    vec_round(4)
    for layer in range(2):
        at = layer * VEC_PER_LAYER
        for k in range(6):
            refs.o_node_biases[k, layer : layer + 1] = sums[10, at + k : at + k + 1]
        refs.o_node_gains[layer] = sums[10, at + VEC_ROWS[GN1] : at + VEC_ROWS[GN2] + 1]
        for k in range(4):
            first = at + VEC_ROWS[FB] + k
            refs.o_ffn_bias[layer : layer + 1, k * ff : (k + 1) * ff] = sums[10, first : first + 1, :ff]
        first = at + VEC_ROWS[C1]
        refs.o_edge_biases[layer] = sums[10, first : first + 4, :ew]
        refs.o_edge_gains[layer : layer + 1] = sums[10, first + 4 : first + 5, :ew]
    put_message(0)
    copies, total = reduce_last[TB]
    wait(copies)
    refs.o_time[...] = total(0, plan.tb_rows)


def vmem(shape, dtype):
    return pltpu.VMEM(shape, dtype)


def run_whole(plan, operands):
    lanes, slots, width, ew, ff, layers = LANES, plan.slots, plan.width, plan.ew, plan.ff, plan.layers
    rows_in = 2 * width + ew
    node_rows = lanes // plan.nbr_total if plan.fast else lanes
    outs = dict(
        nodes_out=((node_rows, width), F32),
        edges_out=((slots, ew, lanes), F32),
        g_nodes=((node_rows, width), F32),
        g_edges=((slots, ew, lanes), F32),
    )
    scratch = dict(
        onehot=vmem((slots, 3 * lanes, lanes), BF16),
        eb=vmem((layers, slots, ew, lanes), BF16),
        pool=vmem((plan.pool_rows, lanes), BF16),
        psum=vmem((slots, ew, lanes), F32),
        proj=vmem((width, 3 * lanes + ew), BF16),
        proj_e=vmem((ew, 3 * lanes + ew), BF16),
        own=vmem((width, lanes), F32),
        own_e=vmem((ew, lanes), F32),
        state=vmem((3, width, lanes), F32),
        ext=vmem((3, 3, width, lanes), BF16),
        joined_a=vmem((layers, width, lanes), F32),
        joined_c=vmem((layers, width, lanes), F32),
        h1b=vmem((layers, width, lanes), BF16),
        act=vmem((layers, ff, lanes), BF16),
        slope_f=vmem((layers, ff, lanes), BF16),
        ubar=vmem((layers, width, lanes), F32),
        ds=vmem((width, lanes), BF16),
        acc_mid=vmem((width, width), F32),
        acc_e=vmem((ew, width), F32),
        acc_z=vmem((width, 3 * lanes), F32),
        acc_zs=vmem((width, lanes), F32),
        acc_b2=vmem((width, lanes), F32),
        acc_h2=vmem((ew, ew), F32),
        acc_h3=vmem((ew, ew), F32),
        acc_ee=vmem((ew, ew), F32),
        acc_t=vmem((ew, 3 * lanes), F32),
        acc_ts=vmem((ew, lanes), F32),
        acc_c=vmem((4, ew, lanes), F32),
        wide=vmem((up_to(rows_in, lanes), CHUNK * lanes), F32),
        vrow=vmem((width, lanes), F32),
        dcur=vmem((width, lanes), F32),
        g_part=vmem((width, lanes), F32),
        halo_send=vmem((2, width, lanes), BF16),
        halo_recv=vmem((3, 2, width, lanes), BF16),
        ar_part=vmem((2, width, lanes), F32),
        ar_one=vmem((2, width // 2, lanes), F32),
        ar_two=vmem((2, width // 2, lanes), F32),
        ar_three=vmem((2, width // 2, lanes), F32),
        ar_two_low=vmem((2, width // 2, lanes), BF16),
        ar_three_low=vmem((2, width // 2, lanes), BF16),
        mask_rows=vmem((slots, lanes), F32),
        vectors=vmem((width, lanes), F32),
        ar_tot=vmem((2, width, lanes), F32),
        send_sem=pltpu.SemaphoreType.DMA((160,)),
        recv_sem=pltpu.SemaphoreType.DMA((160,)),
        local_sem=pltpu.SemaphoreType.DMA((2,)),
    )
    kept = dict(
        g_eint=((layers, ew, up_to(rows_in, lanes)), BF16),
        g_ehid=((layers, 2, ew, 2 * lanes), BF16),
        g_vec=((width, lanes), F32),
    )
    if plan.fast:
        scratch.update({name: vmem(*spec) for name, spec in kept.items()})
        own_rows = lanes // plan.nbr_total
        scratch.update(
            dict(
                counts=vmem((1, lanes), F32),
                all_nodes=vmem((lanes, width), F32),
                all_dnodes=vmem((lanes, width), F32),
                all_misc=vmem((plan.nbr_total, 8, lanes), F32),
                time_hot=vmem((8 * plan.k_time, lanes), BF16),
                time_rows=vmem((8 * plan.k_time, width), BF16),
                vec_sums=vmem((11, layers * VEC_PER_LAYER, width), F32),
                w_in=vmem((layers, rows_in, width), BF16),
                w_et=vmem((layers, width, ew), BF16),
                w_mid=vmem((layers, width, width), BF16),
                w_midt=vmem((layers, width, width), BF16),
                w_out=vmem((layers, width, width), BF16),
                f_in=vmem((layers, width, ff), BF16),
                f_outt=vmem((layers, width, ff), BF16),
                e_int=vmem((layers, ew, rows_in), BF16),
                e_e=vmem((layers, ew, ew), BF16),
                e_hid=vmem((layers, 2, ew, ew), BF16),
                e_hidt=vmem((layers, 2, ew, ew), BF16),
            )
        )
        outs.update(
            dict(
                o_in=((layers, plan.k_in, lanes), F32),
                o_mid=((layers, plan.k_mid, lanes), F32),
                o_out=((layers, plan.k_mid, lanes), F32),
                o_fin=((layers, plan.k_mid, ff), F32),
                o_foutt=((layers, plan.k_mid, ff), F32),
                o_edge=((layers, ew // 4, plan.k_in), F32),
                o_hid=((layers, 2, plan.k_hid, ew // 4), F32),
                o_time=((plan.tb_rows, lanes), F32),
                o_node_biases=((6, layers, width), F32),
                o_node_gains=((layers, 2, width), F32),
                o_ffn_bias=((layers, 4 * ff), F32),
                o_edge_gains=((layers, ew), F32),
                o_edge_biases=((layers, 4, ew), F32),
            )
        )
    else:
        outs.update(
            dict(
                g_in=((layers, rows_in, width), BF16),
                g_mid=((layers, width, width), BF16),
                g_out=((layers, width, width), BF16),
                g_fin=((layers, width, ff), BF16),
                g_foutt=((layers, width, ff), BF16),
                **kept,
            )
        )
    names = (*operands, *outs, *scratch)
    in_hbm, in_smem = dict(edges=1, d_edges=1), dict(time_index=1)
    place = lambda name: pl.BlockSpec(
        memory_space=pl.ANY if name in in_hbm else pltpu.SMEM if name in in_smem else pltpu.VMEM
    )
    results = pl.pallas_call(
        functools.partial(whole_kernel, plan, names),
        out_shape=tuple(jax.ShapeDtypeStruct(*spec) for spec in outs.values()),
        in_specs=[place(name) for name in operands],
        out_specs=[pl.BlockSpec(memory_space=pltpu.VMEM)] * len(outs),
        scratch_shapes=list(scratch.values()),
        compiler_params=pltpu.CompilerParams(
            collective_id=1, has_side_effects=True, vmem_limit_bytes=62 * 1024 * 1024
        ),
    )(*operands.values())
    return Refs(outs, results)


def hand_over(values):
    def kernel(*refs):
        for source, result in zip(refs[: len(values)], refs[len(values) :], strict=True):
            result[...] = source[...]

    return pl.pallas_call(
        kernel,
        out_shape=[jax.ShapeDtypeStruct(value.shape, value.dtype) for value in values],
        in_specs=[pl.BlockSpec(memory_space=pltpu.VMEM)] * len(values),
        out_specs=[pl.BlockSpec(memory_space=pltpu.VMEM)] * len(values),
    )(*values)


def gather_all(value, res_dim, nbr_dim):
    value = lax.all_gather(value, "res", axis=res_dim, tiled=True)
    return lax.all_gather(value, "nbr", axis=nbr_dim, tiled=True)


def scatter_sum(value, res_dim, nbr_dim):
    value = lax.psum_scatter(value, "res", scatter_dimension=res_dim, tiled=True)
    return lax.psum_scatter(value, "nbr", scatter_dimension=nbr_dim, tiled=True).astype(F32)


def low(value):
    return value.astype(BF16)


def per_device(
    nodes,
    edges,
    protein_ids,
    time_index,
    neighbors,
    edge_mask,
    time_table,
    msg_in,
    msg_mid,
    msg_out,
    ffn_in,
    ffn_out,
    edge_in,
    edge_hidden,
    node_gains,
    node_biases,
    ffn_bias,
    edge_gains,
    edge_biases,
    d_nodes,
    d_edges,
):
    res_total, nbr_total = lax.axis_size("res"), lax.axis_size("nbr")
    own_rows, width = nodes.shape
    ew = edges.shape[2]
    row_count, slot_count = neighbors.shape
    layers = msg_in.shape[0]
    n_at = lax.axis_index("nbr")
    ff = ffn_bias.shape[1] // nbr_total
    shards = (msg_in.shape[1], msg_mid.shape[1], edge_hidden.shape[2], time_table.shape[0])
    plan = Plan(res_total, nbr_total, slot_count, width, ew, ff, layers, shards)

    operands = dict(
        neighbors=neighbors.T,
        mask=edge_mask.T,
        edges=jnp.transpose(edges, (1, 2, 0)),
        d_edges=jnp.transpose(d_edges, (1, 2, 0)),
        node_biases=jnp.swapaxes(node_biases, 0, 1),
        node_gains=node_gains,
        ffn_bias=ffn_bias,
        edge_gains=edge_gains,
        edge_biases=edge_biases,
    )
    if plan.fast:
        operands.update(
            nodes=nodes,
            d_nodes=d_nodes,
            protein_ids=protein_ids[None, :],
            time_index=time_index,
            msg_in=msg_in,
            msg_mid=msg_mid,
            msg_out=msg_out,
            ffn_in=ffn_in,
            ffn_outt=jnp.swapaxes(ffn_out, 1, 2),
            edge_in_t=jnp.swapaxes(edge_in, 1, 2),
            edge_hidden=edge_hidden,
            time_table=time_table,
        )
        out = run_whole(plan, operands)
        (
            nodes_out, edges_out, g_nodes, g_edges, g_time, g_in, g_mid, g_out, g_fin, g_foutt, g_edge_t,
            g_hid, g_gains, g_biases, g_ffn_bias, g_edge_gains, g_edge_biases,
        ) = hand_over(
            [
                out.nodes_out, out.edges_out, out.g_nodes, out.g_edges, out.o_time, out.o_in, out.o_mid,
                out.o_out, out.o_fin, out.o_foutt, out.o_edge, out.o_hid, out.o_node_gains,
                out.o_node_biases, out.o_ffn_bias, out.o_edge_gains, out.o_edge_biases,
            ]
        )
        return (
            nodes_out,
            jnp.transpose(edges_out, (2, 0, 1)),
            g_nodes,
            jnp.transpose(g_edges, (2, 0, 1)),
            g_time,
            g_in,
            g_mid,
            g_out,
            g_fin,
            jnp.swapaxes(g_foutt, 1, 2),
            jnp.swapaxes(g_edge_t, 1, 2),
            g_hid,
            g_gains,
            jnp.swapaxes(g_biases, 0, 1),
            g_ffn_bias,
            g_edge_gains,
            g_edge_biases,
        )

    count_row = jnp.sum(edge_mask.astype(F32), axis=1)
    matches = protein_ids[:, None] == jnp.arange(time_index.shape[0], dtype=jnp.int32)[None, :]
    step_rows = jnp.sum(jnp.where(matches, time_index[None, :], 0), axis=1)
    mine = lambda a: lax.dynamic_slice_in_dim(a, n_at * own_rows, own_rows, axis=0)
    node_vectors = lambda rows: (rows[:, : SH2 + 1], rows[:, GN1 : GN2 + 1])
    table_low = gather_all(low(time_table), 0, 1)
    w_in = gather_all(low(msg_in), 1, 2)
    w_mid = gather_all(low(msg_mid), 1, 2)
    e_in = gather_all(low(edge_in), 1, 2)
    e_hid = gather_all(low(edge_hidden), 2, 3)
    step_onehot = (
        step_rows[:, None] == jnp.arange(table_low.shape[0], dtype=jnp.int32)[None, :]
    ).astype(BF16)
    state = nodes + jnp.dot(step_onehot, table_low, preferred_element_type=F32)
    count_block = jnp.zeros((8, width), F32).at[0, :row_count].set(count_row)
    packed = lax.all_gather(jnp.concatenate([state, d_nodes, count_block], axis=0), "nbr", axis=0)
    operands.update(
        dict(
            h0=packed[:, :own_rows].reshape(row_count, width).T,
            dh=packed[:, own_rows : 2 * own_rows].reshape(row_count, width).T,
            counts=jnp.sum(packed[:, 2 * own_rows, :row_count], axis=0)[None, :],
            w_in=w_in,
            w_et=jnp.swapaxes(w_in[:, 2 * width :], 1, 2),
            w_mid=w_mid,
            w_midt=jnp.swapaxes(w_mid, 1, 2),
            w_out=gather_all(low(msg_out), 1, 2),
            f_in=lax.all_gather(low(ffn_in), "res", axis=1, tiled=True),
            f_outt=lax.all_gather(jnp.swapaxes(low(ffn_out), 1, 2), "res", axis=1, tiled=True),
            e_int=jnp.swapaxes(e_in, 1, 2),
            e_e=e_in[:, 2 * width :],
            e_hid=e_hid,
            e_hidt=jnp.swapaxes(e_hid, 2, 3),
        )
    )
    out = run_whole(plan, operands)
    g_nodes = mine(out.g_nodes)
    g_table_full = lax.dot_general(
        step_onehot.astype(F32),
        g_nodes,
        (((0,), (0,)), ((), ())),
        precision=lax.Precision.HIGHEST,
        preferred_element_type=F32,
    )
    rows = out.g_vec.T[: layers * VECTORS].reshape(layers, VECTORS, width)
    shared = rows[:, B3 : GN2 + 1] * (1.0 / nbr_total)
    g_bias_ffn = lax.dynamic_update_slice_in_dim(
        jnp.zeros_like(ffn_bias), rows[:, FB, :ff], n_at * ff, axis=1
    )
    vectors, g_ffn_bias, g_edge_biases, g_edge_gains = lax.psum(
        (
            jnp.concatenate([rows[:, :B3], shared], axis=1),
            g_bias_ffn,
            rows[:, C1 : C4 + 1, :ew],
            rows[:, GE, :ew],
        ),
        ("res", "nbr"),
    )
    g_node_biases, g_node_gains = node_vectors(vectors)
    scatter_res = lambda a: lax.psum_scatter(a, "res", scatter_dimension=1, tiled=True).astype(F32)
    return (
        mine(out.nodes_out),
        jnp.transpose(out.edges_out, (2, 0, 1)),
        g_nodes,
        jnp.transpose(out.g_edges, (2, 0, 1)),
        scatter_sum(low(g_table_full), 0, 1),
        scatter_sum(out.g_in, 1, 2),
        scatter_sum(out.g_mid, 1, 2),
        scatter_sum(out.g_out, 1, 2),
        scatter_res(out.g_fin),
        jnp.swapaxes(scatter_res(out.g_foutt), 1, 2),
        jnp.swapaxes(scatter_sum(out.g_eint[:, :, : 2 * width + ew], 2, 1), 1, 2),
        scatter_sum(jnp.swapaxes(out.g_ehid[..., :ew], 2, 3), 2, 3),
        g_node_gains,
        g_node_biases,
        g_ffn_bias,
        g_edge_gains,
        g_edge_biases,
    )


def solution(mesh):
    return jax.shard_map(
        per_device,
        mesh=mesh,
        in_specs=(
            P(("res", "nbr"), None),
            P("res", "nbr", None),
            P(("res", "nbr")),
            P(),
            P("res", "nbr"),
            P("res", "nbr"),
            P("res", "nbr"),
            P(None, "res", "nbr"),
            P(None, "res", "nbr"),
            P(None, "res", "nbr"),
            P(None, "res", "nbr"),
            P(None, "nbr", "res"),
            P(None, "res", "nbr"),
            P(None, None, "res", "nbr"),
            P(),
            P(),
            P(),
            P(),
            P(),
            P(("res", "nbr"), None),
            P("res", "nbr", None),
        ),
        out_specs=(
            P(("res", "nbr"), None),
            P("res", "nbr", None),
            P(("res", "nbr"), None),
            P("res", "nbr", None),
            P("res", "nbr"),
            P(None, "res", "nbr"),
            P(None, "res", "nbr"),
            P(None, "res", "nbr"),
            P(None, "res", "nbr"),
            P(None, "nbr", "res"),
            P(None, "res", "nbr"),
            P(None, None, "res", "nbr"),
            P(),
            P(),
            P(),
            P(),
            P(),
        ),
        check_vma=False,
    )
```

time: 1120 us -> 269 us (0.24)
  waiting for transfers between devices: 607 us -> 0 us
  blocking collectives: 260 us -> 0 us
  Pallas kernels: 164 us -> 268 us
  local copies, waits for them, and re-layouts: 62.6 us -> 0 us
  between operations: 15.9 us -> 0.85 us
    unnamed x28 -> x0, waiting for transfers between devices: 306 us -> none
    reduce_scatter x5 -> x0, waiting for transfers between devices: 301 us -> none  [the longest x3 172 us: scatter_sum(): lax.psum_scatter(value, 'res', scatter_dimension=res_dim, tiled=True)]
    all_gather x10 -> x0, blocking collectives: 219 us -> none  [the longest x6 190 us: gather_all(): value = lax.all_gather(value, 'res', axis=res_dim, tiled=True)]
    pallas_call x1 -> x2, Pallas kernels: 164 us -> 268 us  [the longest x1 263 us: run_whole(): pl.pallas_call(functools.partial(whole_kernel, plan, names), out_shape=tu...]
    psum x1 -> x0, blocking collectives: 41.1 us -> none  [per_device(): lax.psum((jnp.concatenate([g_rows[:, :B3], shared[:, :SH2 + 1 - B3]], axi...]
    unnamed x93 -> x0, local copies, waits for them, and re-layouts: 39.6 us -> none
    all_gather x8 -> x0, local copies, waits for them, and re-layouts: 12.4 us -> none  [the longest x4 8.67 us: gather_all(): return lax.all_gather(value, 'nbr', axis=nbr_dim, tiled=True)]
  transfers between devices with their start and end apart: 19 -> 0, of which waited for: 12 -> 0; matrix products, arithmetic and copies ran while one was open for 6% -> 0% of each run, Pallas kernels for 0% -> 0%
where the time goes in v2:
time: 269 us; the launch traced here: 268 us
  Pallas kernels  268 us (100%)
    pallas_call x1, Pallas kernels, run_whole(): pl.pallas_call(functools.partial(whole_kernel, plan, names), out_shape=tu...  263 us

profile of v2, /device:TPU:0, one launch (start us, length us, event | category | flops | bytes accessed | tf_op | source)
XLA Modules:
  0.0 268.5 jit_solution(5646927759811951278)
XLA Ops:
  0.7 263.4 %shard_map.332 = (f32[32,512]{1,0:T(8,128)}, f32[15,192,128]{2,1,0:T(8,128)}, f32[32,512]{1,0:T(8,128)}, f32[15,192,128]{2,1,0:T(8,128)}, f32[2,152,128]{2,1,0:T...) custom-call(s32[15,128]{1,0:T(8,128)} %bitcast.18, ...), custom_call_target="tpu_custom_call" | custom-call | tf_op jit(solution)/shard_map/pallas_call | solution.py:1279
  264.1 4.2 %shard_map.333 = (f32[32,512]{1,0:T(8,128)}, f32[15,192,128]{2,1,0:T(8,128)}, f32[32,512]{1,0:T(8,128)}, f32[15,192,128]{2,1,0:T(8,128)}, f32[16,128]{1,0:T(8,12...) custom-call(f32[32,512]{1,0:T(8,128)} %get-tuple-element.51.refs_0_,, ...), custom_call_target="tpu_custom_call" | custom-call | tf_op jit(solution)/shard_map/pallas_call | solution.py:1297

commit v3 on v2

--- a/solution.py
+++ b/solution.py
@@ -105,13 +105,15 @@
         for item in (IN1, MO1, ED):
             self.stage[item] = at
             at += 32 * sizes[item]
+        top = at
+        at = 2 * one
         for item in (FF0, FF1):
             self.stage[item] = at
             at += 8 * sizes[item]
-        top = at
+        top = max(top, at)
         self.source, self.recv = {}, {}
         at = 0
-        for item in (IN0, MO0):
+        for item in (MO0, IN0):
             self.source[item] = at
             at += 32 * sizes[item]
         at = one
@@ -126,14 +128,20 @@
         self.recv[FF1, BY_Y] = at + 8 * sizes[FF1]
         at += 12 * sizes[FF1]
         for stage, count in ((BY_CORE, 16), (BY_X, 8), (BY_Y, 4)):
-            for item, twin in ((IN1, IN0), (MO1, MO0)):
-                self.recv[item, stage] = self.recv[twin, stage] = at
+            for item in (IN1, MO1):
+                self.recv[item, stage] = at
                 at += count * sizes[item]
+        self.recv[IN0, BY_CORE], self.recv[MO0, BY_CORE] = self.recv[IN1, BY_CORE], self.recv[MO1, BY_CORE]
         top = max(top, at)
         self.edge_at = top
         self.source[FF0] = top
         self.recv[FF0, BY_Y] = top + 8 * sizes[FF0]
-        at = top + max(4 * edge_rows, 12 * sizes[FF0])
+        at = top + 12 * sizes[FF0]
+        for stage, count in ((BY_X, 8), (BY_Y, 4)):
+            for item in (IN0, MO0):
+                self.recv[item, stage] = at
+                at += count * sizes[item]
+        at = max(at, top + 4 * edge_rows)
         self.source[TB] = at
         at += 32 * sizes[TB]
         for stage, count in ((BY_CORE, 16), (BY_X, 8), (BY_Y, 4)):
@@ -197,15 +205,16 @@
     for device in greeted:
         pl.semaphore_signal(barrier, inc=1, device_id=device, device_id_type=MESH)
 
-    @pl.when(up_too)
-    def _():
-        pl.semaphore_signal(barrier, inc=1, device_id=(r - 1, n), device_id_type=MESH)
-
-    @pl.when(down_too)
-    def _():
-        pl.semaphore_signal(barrier, inc=1, device_id=(r + 1, n), device_id_type=MESH)
-
-    greetings = (len(greeted) + up_too.astype(jnp.int32) + down_too.astype(jnp.int32))
+    def greet(device):
+        pl.semaphore_signal(barrier, inc=1, device_id=device, device_id_type=MESH)
+
+    pl.when(up_too)(lambda: greet((r - 1, n)))
+    pl.when(down_too)(lambda: greet((r + 1, n)))
+    pl.when(has_prev)(lambda: greet((r - 1, across)))
+    pl.when(has_next)(lambda: greet((r + 1, across)))
+    greetings = len(greeted)
+    for there in (up_too, down_too, has_prev, has_next):
+        greetings += there.astype(jnp.int32)
 
     zero_tile = jnp.zeros((width, LANES), BF16)
 
@@ -213,13 +222,13 @@
     def _():
         for b in range(3):
             ext[b, 0] = zero_tile
-            halo_recv[b, 0] = zero_tile
+            halo_recv[b, 0:2] = jnp.zeros_like(halo_recv[b, 0:2])
 
     @pl.when(jnp.logical_not(has_next))
     def _():
         for b in range(3):
             ext[b, 2] = zero_tile
-            halo_recv[b, 1] = zero_tile
+            halo_recv[b, 2:4] = jnp.zeros_like(halo_recv[b, 2:4])
 
     def next_sem():
         at = sem_at[0]
@@ -257,28 +266,30 @@
     load_edges = pltpu.make_async_copy(refs.edges, g_edges, refs.local_sem.at[0])
     load_edges.start()
 
-    def two_way(to_prev, at_prev, to_next, at_next):
-        up = remote(to_prev, at_prev, (r - 1, n))
-        down = remote(to_next, at_next, (r + 1, n))
+    def two_way(pairs):
+        ups = [remote(a, b, (r - 1, col)) for col, a, b, _, _ in pairs]
+        downs = [remote(a, b, (r + 1, col)) for col, _, _, a, b in pairs]
 
         def begin():
-            pl.when(has_prev)(up.start)
-            pl.when(has_next)(down.start)
+            pl.when(has_prev)(lambda: start(ups))
+            pl.when(has_next)(lambda: start(downs))
 
         def finish():
             @pl.when(has_prev)
             def _():
-                up.wait_send()
-                down.wait_recv()
+                for up, down in zip(ups, downs, strict=True):
+                    up.wait_send()
+                    down.wait_recv()
 
             @pl.when(has_next)
             def _():
-                down.wait_send()
-                up.wait_recv()
+                for up, down in zip(ups, downs, strict=True):
+                    down.wait_send()
+                    up.wait_recv()
 
         return begin, finish
 
-    def all_reduce(value, short=False):
+    def all_reduce(value, meanwhile=lambda: None):
         at = ar_at[0] % 2
         ar_at[0] += 1
         mine = pl.multiple_of(core * half_rows, half_rows)
@@ -287,12 +298,12 @@
         one = remote(ar_part.at[at, pl.ds(theirs, half_rows)], ar_one.at[at], (r, buddy))
         one.start()
         one.wait()
-        sent, got = (refs.ar_two_low, refs.ar_three_low) if short else (ar_two, ar_three)
-        sent[at] = (ar_part[at, pl.ds(mine, half_rows)] + ar_one[at]).astype(sent.dtype)
-        two = remote(sent.at[at], got.at[at], (r, across))
+        ar_two[at] = (ar_part[at, pl.ds(mine, half_rows)] + ar_one[at]).astype(BF16)
+        two = remote(ar_two.at[at], ar_three.at[at], (r, across))
         two.start()
+        meanwhile()
         two.wait()
-        ar_tot[at, pl.ds(mine, half_rows)] = sent[at].astype(F32) + got[at].astype(F32)
+        ar_tot[at, pl.ds(mine, half_rows)] = ar_two[at].astype(F32) + ar_three[at].astype(F32)
         span = ar_tot.at[at, pl.ds(mine, half_rows)]
         three = remote(span, span, (r, buddy))
         three.start()
@@ -304,19 +315,46 @@
 
     def halo(b, value):
         ext[b, 1] = value
-        begin, finish = two_way(ext.at[b, 1], ext.at[b, 2], ext.at[b, 1], ext.at[b, 0])
+        begin, finish = two_way([(n, ext.at[b, 1], ext.at[b, 2], ext.at[b, 1], ext.at[b, 0])])
         begin()
         return finish
 
-    def halo_back(b, g_ext, g_own):
-        halo_send[0] = g_ext[:, :LANES].astype(BF16)
-        halo_send[1] = g_ext[:, 2 * LANES :].astype(BF16)
-        g_part[...] = g_ext[:, LANES : 2 * LANES] + g_own
-        begin, finish = two_way(halo_send.at[0], halo_recv.at[b, 1], halo_send.at[1], halo_recv.at[b, 0])
+    def halo_back(b, g_ext, g_own, beside_core=lambda: None, beside_far=lambda: None):
+        at = ar_at[0] % 2
+        ar_at[0] += 1
+        my_half = pl.ds(pl.multiple_of(core * half_rows, half_rows), half_rows)
+        their_half = pl.ds(pl.multiple_of(half_rows - core * half_rows, half_rows), half_rows)
+        for k in range(3):
+            part = g_ext[:, k * LANES : (k + 1) * LANES]
+            g_part[k] = part + g_own if k == 1 else part
+        halo_send[...] = g_part[:, their_half].astype(BF16)
+        one = remote(halo_send, refs.halo_core, (r, buddy))
+        one.start()
+        beside_core()
+        one.wait()
+        half = refs.halo_half
+        half[...] = (g_part[:, my_half] + refs.halo_core[...].astype(F32)).astype(BF16)
+        two = remote(half.at[1], refs.halo_x, (r, across))
+        begin, finish = two_way(
+            [
+                (n, half.at[0], halo_recv.at[b, 2], half.at[2], halo_recv.at[b, 0]),
+                (across, half.at[0], halo_recv.at[b, 3], half.at[2], halo_recv.at[b, 1]),
+            ]
+        )
         begin()
+        two.start()
+        beside_far()
+        two.wait()
         finish()
-        total = g_part[...] + halo_recv[b, 0].astype(F32) + halo_recv[b, 1].astype(F32)
-        return all_reduce(total, short=True)
+        total = half[1].astype(F32) + refs.halo_x[...].astype(F32)
+        for k in (0, 2):
+            total += halo_recv[b, k].astype(F32) + halo_recv[b, k + 1].astype(F32)
+        ar_tot[at, my_half] = total
+        span = ar_tot.at[at, my_half]
+        three = remote(span, span, (r, buddy))
+        three.start()
+        three.wait()
+        return ar_tot.at[at]
 
     FULL = (IN0, MO0, TB, ED, IN1, MO1)
     shard_at = ((core * 2 + xx) * 2 + yy) * 4 + zz
@@ -339,6 +377,25 @@
 
     def gather_y(item):
         return gather_span(item, 4, y_peer)
+
+    def edge_shard(x):
+        at = ((core * 2 + x) * 2 + yy) * 4 + zz
+        return rows_of(aligned(plan.stage[ED] + at * plan.ed_rows), plan.ed_rows)
+
+    def edge_x():
+        span = edge_shard(xx)
+        return [remote(span, span, (r, across))]
+
+    def edge_z():
+        return [remote(edge_shard(x), edge_shard(x), peer) for x in range(2) for peer in z_peers]
+
+    def edge_y():
+        copies = []
+        for x in range(2):
+            at = ((core * 2 + x) * 2 + yy) * 4
+            span = rows_of(aligned(plan.stage[ED] + at * plan.ed_rows), 4 * plan.ed_rows)
+            copies.append(remote(span, span, y_peer))
+        return copies
 
     def gather_x(item):
         return gather_span(item, 8, (r, across))
@@ -483,13 +540,24 @@
                             rr * k_mid : (rr + 1) * k_mid, j * LANES : (j + 1) * LANES
                         ]
 
-    def emit_message(layer, g_own_rows, g_other_rows, g_edge_rows, g_mid, g_out):
+    def emit_middle(layer, g_mid, g_out):
+        if not fast:
+            refs.g_mid[layer] = g_mid.astype(BF16)
+            refs.g_out[layer] = g_out.astype(BF16)
+            return
+        at, k_mid = plan.source[MO[layer]], plan.k_mid
+        for m, value in enumerate((g_mid.astype(BF16), g_out.astype(BF16))):
+            for k, rr, nn_ in blocks():
+                first = at + k * plan.mo_rows + m * k_mid
+                pool[first : first + k_mid] = value[
+                    rr * k_mid : (rr + 1) * k_mid, nn_ * LANES : (nn_ + 1) * LANES
+                ]
+
+    def emit_input(layer, g_own_rows, g_other_rows, g_edge_rows):
         if not fast:
             refs.g_in[layer, :width] = g_own_rows.astype(BF16)
             refs.g_in[layer, width : 2 * width] = g_other_rows.astype(BF16)
             refs.g_in[layer, 2 * width :] = g_edge_rows.astype(BF16)
-            refs.g_mid[layer] = g_mid.astype(BF16)
-            refs.g_out[layer] = g_out.astype(BF16)
             return
         wide[:width, :width] = g_own_rows
         wide[width : 2 * width, :width] = g_other_rows
@@ -500,13 +568,6 @@
             pool[first : first + plan.k_in] = wide[
                 rr * plan.k_in : (rr + 1) * plan.k_in, nn_ * LANES : (nn_ + 1) * LANES
             ].astype(BF16)
-        at, k_mid = plan.source[MO[layer]], plan.k_mid
-        for m, value in enumerate((g_mid.astype(BF16), g_out.astype(BF16))):
-            for k, rr, nn_ in blocks():
-                first = at + k * plan.mo_rows + m * k_mid
-                pool[first : first + k_mid] = value[
-                    rr * k_mid : (rr + 1) * k_mid, nn_ * LANES : (nn_ + 1) * LANES
-                ]
 
     def emit_edge_all():
         at, cols = plan.source[ED], ew // 4
@@ -622,7 +683,7 @@
             hat, rstd = norm_parts(p)
             save(j, hat, rstd, p, hat * vec(layer, GE, ew) + vec(layer, C4, ew))
 
-    def node_update(layer, before_ffn=lambda: None):
+    def node_update(layer, before_ffn=lambda: None, beside_branch=lambda: None):
         total = all_reduce(ubar[layer])[...]
         high = total.astype(BF16)
         low = (total - high.astype(F32)).astype(BF16)
@@ -636,7 +697,7 @@
         before_ffn()
         pre = tn(f_in[layer], h1b[layer]) + vec(layer, FB)
         act[layer], slope_f[layer] = gelu_pair(pre)
-        branch = all_reduce(nn(f_outt[layer], act[layer]))[...]
+        branch = all_reduce(nn(f_outt[layer], act[layer]), beside_branch)[...]
         joined = hidden + (branch + vec(layer, B5))
         joined_c[layer] = joined
         hat, _ = norm_parts(joined)
@@ -677,6 +738,13 @@
         for j in range(CHUNK):
             g_edges[base + j] += back[:, j * LANES : (j + 1) * LANES]
 
+    def edge_terms(layer):
+        table = acc_t[...].astype(BF16)
+        sums = acc_ts[...].astype(BF16)
+        g_ext = tn(e_int[layer, :, width : 2 * width], table)
+        g_own = tn(e_int[layer, :, :width], sums)
+        return g_ext, g_own
+
     def edge_finish(layer):
         put_vec(layer, GE, acc_c[0])
         put_vec(layer, C4, acc_c[1])
@@ -690,21 +758,20 @@
         refs.g_eint[layer, :, :width] = nt(sums, ext[layer + 1, 1]).astype(BF16)
         refs.g_eint[layer, :, width : 2 * width] = nt(table, extended(layer + 1)).astype(BF16)
         refs.g_eint[layer, :, 2 * width : 2 * width + ew] = acc_ee[...].astype(BF16)
-        g_ext = tn(e_int[layer, :, width : 2 * width], table)
-        g_own = tn(e_int[layer, :, :width], sums)
-        return g_ext, g_own
-
-    def message_backward(layer, base, add_edge):
+
+    def message_back_two(layer, base):
         grads = []
         for j in range(CHUNK):
             s = base + j
             slope = pool[act_at(S2, layer, s)].astype(F32)
             dz = (vrow[...] * mask_ref[pl.ds(s, 1), :] * slope).astype(BF16)
             acc_b2[...] += dz.astype(F32)
+            pool[act_at(S2, layer, s)] = dz
             grads.append(dz)
-        grad_two = jnp.concatenate(grads, axis=1)
-        acc_mid[...] += nt(acts(U1, layer, base), grad_two)
-        wide[:width, :] = nn(w_mid[layer], grad_two)
+        acc_mid[...] += nt(acts(U1, layer, base), jnp.concatenate(grads, axis=1))
+
+    def message_back_one(layer, base, add_edge):
+        wide[:width, :] = nn(w_mid[layer], acts(S2, layer, base))
         grads = []
         for j in range(CHUNK):
             slope = pool[act_at(S1, layer, base + j)].astype(F32)
@@ -718,22 +785,22 @@
         for j in range(CHUNK):
             add_edge(base + j, back[:, j * LANES : (j + 1) * LANES])
 
-    def message_finish(layer):
+    def middle_finish(layer):
         put_vec(layer, B2, acc_b2[...])
-        put_vec(layer, B1, acc_zs[...])
+        emit_middle(layer, acc_mid[...], nt(ubar[layer].astype(BF16), ds_ref[...]))
+
+    def message_terms(layer):
         table = acc_z[...].astype(BF16)
         sums = acc_zs[...].astype(BF16)
-        emit_message(
-            layer,
-            nt(ext[layer, 1], sums),
-            nt(extended(layer), table),
-            acc_e[...],
-            acc_mid[...],
-            nt(ubar[layer].astype(BF16), ds_ref[...]),
-        )
         g_ext = nn(w_in[layer, width : 2 * width, :], table)
         g_own = nn(w_in[layer, :width, :], sums)
         return g_ext, g_own
+
+    def message_finish(layer):
+        table = acc_z[...].astype(BF16)
+        sums = acc_zs[...].astype(BF16)
+        emit_input(layer, nt(ext[layer, 1], sums), nt(extended(layer), table), acc_e[...])
+        put_vec(layer, B1, acc_zs[...])
 
     def node_back(layer, meanwhile=lambda: None):
         counts = cnt_ref[...]
@@ -747,8 +814,7 @@
         df = (tn(f_outt[layer], dy) * slope_f[layer].astype(F32)).astype(BF16)
         put_vec(layer, FB, df.astype(F32))
         part = nn(f_in[layer], df)
-        meanwhile()
-        total = all_reduce(part, short=True)
+        total = all_reduce(part, meanwhile)
         emit_ffn(layer, nt(h1b[layer], df), nt(dy, act[layer]))
         grad = dc + total[...]
         hat, rstd = norm_parts(joined_a[layer])
@@ -815,10 +881,11 @@
             ):
                 group.append(remote(ref, ref, peer))
         every = range(FF1 + 1)
-        gz = {item: gather_z(item) for item in every}
-        gy = {item: gather_y(item) for item in every}
-        gx = {item: gather_x(item) for item in FULL}
+        gz = {item: gather_z(item) for item in every if item != ED}
+        gy = {item: gather_y(item) for item in every if item != ED}
+        gx = {item: gather_x(item) for item in FULL if item != ED}
         gc = {item: gather_c(item) for item in FULL}
+        gx[ED], gz[ED], gy[ED] = edge_x(), edge_z(), edge_y()
 
         def pass_on(before, after, *items):
             for item in items:
@@ -829,21 +896,17 @@
             for item in items:
                 start(stage[item])
 
-        first(gz, IN0, TB)
+        first(gz, TB, IN0)
         start(node_copies)
         pack_mo(0)
+        first(gz, MO0)
         pack_edge()
-        make_vectors()
-        pass_on(gz, gy, IN0, TB)
-        first(gz, MO0, ED)
-        pack_ffn(0)
+        first(gx, ED)
+        pass_on(gz, gy, TB, IN0)
         pack_in(1)
         pack_mo(1)
-        pack_ffn(1)
-        make_onehot()
-        pass_on(gy, gx, IN0, TB)
-        pass_on(gz, gy, MO0, ED)
-        first(gz, FF0, IN1, MO1)
+        pass_on(gy, gx, TB)
+        make_vectors()
         wait(node_copies)
         misc = refs.all_misc[0]
         for k in range(1, 4):
@@ -853,8 +916,8 @@
         times = lax.broadcasted_iota(jnp.int32, (8 * plan.k_time, LANES), 0).astype(F32)
         refs.time_hot[...] = jnp.where(times == steps, 1.0, 0.0).astype(BF16)
         nodes_t = refs.all_nodes[...].T
-        pass_on(gx, gc, IN0, TB)
-        pass_on(gy, gx, MO0)
+        pass_on(gx, gc, TB)
+        pass_on(gy, gx, IN0)
         wait(gc[TB])
         for k, rr, nn_ in blocks():
             at = plan.stage[TB] + k * plan.tb_rows
@@ -863,11 +926,23 @@
             ]
         state[0] = nodes_t + tn(refs.time_rows[...], refs.time_hot[...])
         finish = halo(0, state[0].astype(BF16))
+        pass_on(gz, gy, MO0)
+        first(gz, IN1, MO1)
+        pack_ffn(0)
+        first(gz, FF0)
+        pass_on(gx, gz, ED)
+        make_onehot()
+        pack_ffn(1)
+        pass_on(gy, gx, MO0)
+        finish()
+        pass_on(gz, gy, IN1, MO1)
+        pass_on(gx, gc, IN0)
         wait(gc[IN0])
         assemble_in(0)
         pass_on(gx, gc, MO0)
-        pass_on(gy, gx, ED)
-        finish()
+        pass_on(gy, gx, IN1, MO1)
+        pass_on(gz, gy, FF0)
+        first(gz, FF1)
         wait(gc[MO0])
         assemble_mo(0)
     else:
@@ -885,13 +960,7 @@
 
             @pl.when(i == 1)
             def _():
-                pass_on(gz, gy, FF0)
-
-            @pl.when(i == 2)
-            def _():
-                pass_on(gz, gy, IN1, MO1)
-                first(gz, FF1)
-                start(late_copies)
+                pass_on(gz, gy, ED)
 
         return 0
 
@@ -899,26 +968,27 @@
 
     def need_ffn0():
         if fast:
-            pass_on(gx, gc, ED)
-            pass_on(gy, gx, IN1, MO1)
             wait(gy[FF0])
             assemble_ffn(0)
 
-    finish = node_update(0, need_ffn0)
+    def beside_branch():
+        if fast:
+            pass_on(gx, gc, IN1, MO1)
+            pass_on(gy, gc, ED)
+
+    finish = node_update(0, need_ffn0, beside_branch)
     if fast:
-        pass_on(gz, gy, FF1)
-        wait(gc[ED])
-        assemble_edge()
-        pass_on(gx, gc, IN1, MO1)
+        start(late_copies)
         wait(gc[IN1])
         assemble_in(1)
         wait(gc[MO1])
         assemble_mo(1)
-        wait(gy[FF1])
-        assemble_ffn(1)
-        wait(late_copies)
+        wait(gc[ED])
+        assemble_edge()
     finish()
     prepare_edge(0)
+    if fast:
+        pass_on(gz, gy, FF1)
     prepare_message(1)
 
     def loop_b(i, _):
@@ -936,7 +1006,14 @@
     lax.fori_loop(0, chunks, loop_b, 0)
     load_grads = pltpu.make_async_copy(refs.d_edges, g_edges, refs.local_sem.at[1])
     load_grads.start()
-    finish = node_update(1)
+
+    def need_ffn1():
+        if fast:
+            wait(late_copies)
+            wait(gy[FF1])
+            assemble_ffn(1)
+
+    finish = node_update(1, need_ffn1)
     if fast:
         refs.all_nodes[...] = state[2].T
         nodes_out[...] = refs.all_nodes[pl.ds(mine, own_rows)]
@@ -960,9 +1037,9 @@
         return 0
 
     lax.fori_loop(0, chunks, loop_c, 0)
-    g_ext, g_own = edge_finish(1)
+    g_ext, g_own = edge_terms(1)
     dh = refs.all_dnodes[...].T if fast else refs.dh[...]
-    dcur[...] = dh + halo_back(0, g_ext, g_own)[...]
+    dcur[...] = dh + halo_back(0, g_ext, g_own, beside_far=lambda: edge_finish(1))[...]
     node_back(1)
     clear_message()
     clear_edge()
@@ -1020,52 +1097,70 @@
         def add_edge(s, value):
             g_edges[s] += value
 
-        message_backward(1, base, add_edge)
+        message_back_two(1, base)
+        message_back_one(1, base, add_edge)
         return 0
 
     lax.fori_loop(0, chunks, loop_d1, 0)
-    m_ext, m_own = message_finish(1)
+    middle_finish(1)
+    message_finish(1)
+    m_ext, m_own = message_terms(1)
     acc_z[...] = m_ext
     acc_zs[...] = m_own
     if fast:
         start(reduce_c[IN1][0])
         start(reduce_c[MO1][0])
-        reduce_on(reduce_y, reduce_last, FF1)
 
     def loop_d2(i, _):
         base = i * CHUNK
         edge_backward(0, base, lambda j: (*norm_parts(psum[base + j]), g_edges[base + j]))
+        return 0
+
+    lax.fori_loop(0, chunks, loop_d2, 0)
+    e_ext, e_own = edge_terms(0)
+
+    def beside_edge():
+        if fast:
+            reduce_on(reduce_c, reduce_x, IN1, MO1)
+            reduce_on(reduce_y, reduce_last, FF1)
+        edge_finish(0)
+        if fast:
+            emit_edge_all()
+
+    dcur[...] += halo_back(1, acc_z[...] + e_ext, acc_zs[...] + e_own, beside_far=beside_edge)[...]
+
+    def beside_node():
+        if fast:
+            start(reduce_c[ED][0])
+
+    node_back(0, beside_node)
+    clear_message()
+    if fast:
+        reduce_on(reduce_x, reduce_y, IN1, MO1)
+        start(reduce_y[FF0][0])
+        reduce_on(reduce_c, reduce_x, ED)
+
+    def loop_e1(i, _):
+        message_back_two(0, i * CHUNK)
+        return 0
+
+    lax.fori_loop(0, chunks, loop_e1, 0)
+    middle_finish(0)
+    if fast:
+        start(reduce_c[MO0][0])
+
+    def loop_e2(i, _):
+        base = i * CHUNK
+
+        def add_edge(s, value):
+            g_edges[s] += value
+
+        message_back_one(0, base, add_edge)
         if fast:
 
             @pl.when(i == 0)
             def _():
-                reduce_on(reduce_c, reduce_x, IN1, MO1)
-
-        return 0
-
-    lax.fori_loop(0, chunks, loop_d2, 0)
-    e_ext, e_own = edge_finish(0)
-    if fast:
-        emit_edge_all()
-        start(reduce_c[ED][0])
-    dcur[...] += halo_back(1, acc_z[...] + e_ext, acc_zs[...] + e_own)[...]
-    if fast:
-        put_ffn(1)
-        reduce_on(reduce_x, reduce_y, IN1, MO1)
-    node_back(0)
-    clear_message()
-    if fast:
-        reduce_on(reduce_c, reduce_x, ED)
-        start(reduce_y[FF0][0])
-
-    def loop_e(i, _):
-        base = i * CHUNK
-
-        def add_edge(s, value):
-            g_edges[s] += value
-
-        message_backward(0, base, add_edge)
-        if fast:
+                reduce_on(reduce_c, reduce_x, MO0)
 
             @pl.when(i == 2)
             def _():
@@ -1073,21 +1168,50 @@
 
         return 0
 
-    lax.fori_loop(0, chunks, loop_e, 0)
-    m_ext, m_own = message_finish(0)
-    if fast:
+    lax.fori_loop(0, chunks, loop_e2, 0)
+    m_ext, m_own = message_terms(0)
+    if not fast:
+        message_finish(0)
+        final = dcur[...] + halo_back(2, m_ext, m_own)[...]
+        g_nodes[...] = final.T
+        return
+
+    def beside_last_core():
+        message_finish(0)
         start(reduce_c[IN0][0])
-        start(reduce_c[MO0][0])
-        reduce_on(reduce_x, reduce_y, ED)
+
+    sums = refs.vec_sums
+    partners = [(r, buddy), (r, across), y_peer]
+    partners += [(2 * (zz + 1 - 2 * lax.rem(zz, 2)) + yy, n), (2 * lax.rem(zz + 2, 4) + yy, n)]
+    rounds = [remote(sums.at[2 * k], sums.at[2 * k + 1], partners[k]) for k in range(5)]
+
+    def vec_round(k):
+        rounds[k].wait()
+        sums[2 * k + 2] = sums[2 * k] + sums[2 * k + 1]
+        if k < 4:
+            rounds[k + 1].start()
+
+    def beside_last_far():
+        table = refs.g_vec[...].T
+        sums[0] = jnp.zeros_like(sums[0])
+        for layer in range(2):
+            for which, row in VEC_ROWS.items():
+                value = table[layer * VECTORS + which : layer * VECTORS + which + 1]
+                at = layer * VEC_PER_LAYER + row
+                if which == FB:
+                    sums[0, pl.ds(at + n, 1)] = value
+                else:
+                    scale = 1.0 / plan.nbr_total if B3 <= which <= GN2 else 1.0
+                    sums[0, at : at + 1] = value * scale
+        rounds[0].start()
         reduce_on(reduce_c, reduce_x, IN0)
         reduce_on(reduce_y, reduce_last, FF0)
-    final = dcur[...] + halo_back(2, m_ext, m_own)[...]
-    if not fast:
-        g_nodes[...] = final.T
-        return
-    refs.all_dnodes[...] = final.T
-    g_nodes[...] = refs.all_dnodes[pl.ds(mine, own_rows)]
-
+        reduce_on(reduce_x, reduce_y, MO0, ED)
+        vec_round(0)
+        put_ffn(1)
+        put_message(1)
+
+    final = dcur[...] + halo_back(2, m_ext, m_own, beside_last_core, beside_last_far)[...]
     high = final.astype(BF16)
     low = (final - high.astype(F32)).astype(BF16)
     g_times = (nt(refs.time_hot[...], high) + nt(refs.time_hot[...], low)) * (1.0 / plan.nbr_total)
@@ -1097,42 +1221,18 @@
             rr * plan.k_time : (rr + 1) * plan.k_time, nn_ * LANES : (nn_ + 1) * LANES
         ].astype(BF16)
     start(reduce_c[TB][0])
-    table = refs.g_vec[...].T
-    sums = refs.vec_sums
-    sums[0] = jnp.zeros_like(sums[0])
-    for layer in range(2):
-        for which, row in VEC_ROWS.items():
-            value = table[layer * VECTORS + which : layer * VECTORS + which + 1]
-            at = layer * VEC_PER_LAYER + row
-            if which == FB:
-                sums[0, pl.ds(at + n, 1)] = value
-            else:
-                scale = 1.0 / plan.nbr_total if B3 <= which <= GN2 else 1.0
-                sums[0, at : at + 1] = value * scale
-    partners = [(r, buddy), (r, across), y_peer]
-    partners += [(2 * (zz + 1 - 2 * lax.rem(zz, 2)) + yy, n), (2 * lax.rem(zz + 2, 4) + yy, n)]
-    rounds = [remote(sums.at[2 * k], sums.at[2 * k + 1], partners[k]) for k in range(5)]
-
-    def vec_round(k):
-        rounds[k].wait()
-        sums[2 * k + 2] = sums[2 * k] + sums[2 * k + 1]
-        if k < 4:
-            rounds[k + 1].start()
-
-    rounds[0].start()
+    vec_round(1)
     reduce_on(reduce_x, reduce_y, IN0)
-    reduce_on(reduce_c, reduce_x, MO0, TB)
-    vec_round(0)
-    reduce_on(reduce_y, reduce_last, ED)
-    put_message(1)
-    vec_round(1)
-    reduce_on(reduce_y, reduce_last, IN0)
-    reduce_on(reduce_x, reduce_y, TB, MO0)
+    reduce_on(reduce_c, reduce_x, TB)
+    refs.all_dnodes[...] = final.T
+    g_nodes[...] = refs.all_dnodes[pl.ds(mine, own_rows)]
+    reduce_on(reduce_y, reduce_last, MO0)
     vec_round(2)
-    reduce_on(reduce_y, reduce_last, TB, MO0)
+    reduce_on(reduce_x, reduce_y, TB)
+    reduce_on(reduce_y, reduce_last, IN0, ED)
     vec_round(3)
     put_ffn(0)
-    put_edge()
+    reduce_on(reduce_y, reduce_last, TB)
     vec_round(4)
     for layer in range(2):
         at = layer * VEC_PER_LAYER
@@ -1146,6 +1246,7 @@
         refs.o_edge_biases[layer] = sums[10, first : first + 4, :ew]
         refs.o_edge_gains[layer : layer + 1] = sums[10, first + 4 : first + 5, :ew]
     put_message(0)
+    put_edge()
     copies, total = reduce_last[TB]
     wait(copies)
     refs.o_time[...] = total(0, plan.tb_rows)
@@ -1197,15 +1298,16 @@
         wide=vmem((up_to(rows_in, lanes), CHUNK * lanes), F32),
         vrow=vmem((width, lanes), F32),
         dcur=vmem((width, lanes), F32),
-        g_part=vmem((width, lanes), F32),
-        halo_send=vmem((2, width, lanes), BF16),
-        halo_recv=vmem((3, 2, width, lanes), BF16),
+        g_part=vmem((3, width, lanes), F32),
+        halo_send=vmem((3, width // 2, lanes), BF16),
+        halo_core=vmem((3, width // 2, lanes), BF16),
+        halo_half=vmem((3, width // 2, lanes), BF16),
+        halo_x=vmem((width // 2, lanes), BF16),
+        halo_recv=vmem((3, 4, width // 2, lanes), BF16),
         ar_part=vmem((2, width, lanes), F32),
         ar_one=vmem((2, width // 2, lanes), F32),
-        ar_two=vmem((2, width // 2, lanes), F32),
-        ar_three=vmem((2, width // 2, lanes), F32),
-        ar_two_low=vmem((2, width // 2, lanes), BF16),
-        ar_three_low=vmem((2, width // 2, lanes), BF16),
+        ar_two=vmem((2, width // 2, lanes), BF16),
+        ar_three=vmem((2, width // 2, lanes), BF16),
         mask_rows=vmem((slots, lanes), F32),
         vectors=vmem((width, lanes), F32),
         ar_tot=vmem((2, width, lanes), F32),
@@ -1283,7 +1385,7 @@
         out_specs=[pl.BlockSpec(memory_space=pltpu.VMEM)] * len(outs),
         scratch_shapes=list(scratch.values()),
         compiler_params=pltpu.CompilerParams(
-            collective_id=1, has_side_effects=True, vmem_limit_bytes=62 * 1024 * 1024
+            collective_id=1, has_side_effects=True, vmem_limit_bytes=63 * 1024 * 1024
         ),
     )(*operands.values())
     return Refs(outs, results)

time: 269 us -> 232 us (0.86)
  Pallas kernels: 268 us -> 231 us
    pallas_call x1, Pallas kernels: 263 us -> 227 us  [run_whole(): pl.pallas_call(functools.partial(whole_kernel, plan, names), out_shape=tu...]
where the time goes in v3:
time: 232 us
  Pallas kernels  231 us (100%)
    pallas_call x1, Pallas kernels, run_whole(): pl.pallas_call(functools.partial(whole_kernel, plan, names), out_shape=tu...  227 us

profile of v3, /device:TPU:0, one launch (start us, length us, event | category | flops | bytes accessed | tf_op | source)
XLA Modules:
  0.0 232.2 jit_solution(17600181410033377593)
XLA Ops:
  0.7 227.1 %shard_map.332 = (f32[32,512]{1,0:T(8,128)}, f32[15,192,128]{2,1,0:T(8,128)}, f32[32,512]{1,0:T(8,128)}, f32[15,192,128]{2,1,0:T(8,128)}, f32[2,152,128]{2,1,0:T...) custom-call(s32[15,128]{1,0:T(8,128)} %bitcast.18, ...), custom_call_target="tpu_custom_call" | custom-call | tf_op jit(solution)/shard_map/pallas_call | solution.py:1381
  227.8 4.2 %shard_map.333 = (f32[32,512]{1,0:T(8,128)}, f32[15,192,128]{2,1,0:T(8,128)}, f32[32,512]{1,0:T(8,128)}, f32[15,192,128]{2,1,0:T(8,128)}, f32[16,128]{1,0:T(8,12...) custom-call(f32[32,512]{1,0:T(8,128)} %get-tuple-element.51.refs_0_,, ...), custom_call_target="tpu_custom_call" | custom-call | tf_op jit(solution)/shard_map/pallas_call | solution.py:1399

commit v4 on v3

--- a/solution.py
+++ b/solution.py
@@ -171,7 +171,8 @@
     w_in, w_et, w_mid, w_midt, w_out = refs.w_in, refs.w_et, refs.w_mid, refs.w_midt, refs.w_out
     f_in, f_outt, e_int, e_e = refs.f_in, refs.f_outt, refs.e_int, refs.e_e
     e_hid, e_hidt = refs.e_hid, refs.e_hidt
-    nodes_out, edges_out, g_nodes, g_edges = refs.nodes_out, refs.edges_out, refs.g_nodes, refs.g_edges
+    nodes_out, g_nodes = refs.nodes_out, refs.g_nodes
+    edges_out, g_edges = refs.edge_state, refs.edge_grad
     cnt_ref = refs.counts
     res_total = plan.res_total
     slots, width, ew, ff = plan.slots, plan.width, plan.ew, plan.ff
@@ -378,25 +379,6 @@
     def gather_y(item):
         return gather_span(item, 4, y_peer)
 
-    def edge_shard(x):
-        at = ((core * 2 + x) * 2 + yy) * 4 + zz
-        return rows_of(aligned(plan.stage[ED] + at * plan.ed_rows), plan.ed_rows)
-
-    def edge_x():
-        span = edge_shard(xx)
-        return [remote(span, span, (r, across))]
-
-    def edge_z():
-        return [remote(edge_shard(x), edge_shard(x), peer) for x in range(2) for peer in z_peers]
-
-    def edge_y():
-        copies = []
-        for x in range(2):
-            at = ((core * 2 + x) * 2 + yy) * 4
-            span = rows_of(aligned(plan.stage[ED] + at * plan.ed_rows), 4 * plan.ed_rows)
-            copies.append(remote(span, span, y_peer))
-        return copies
-
     def gather_x(item):
         return gather_span(item, 8, (r, across))
 
@@ -881,11 +863,10 @@
             ):
                 group.append(remote(ref, ref, peer))
         every = range(FF1 + 1)
-        gz = {item: gather_z(item) for item in every if item != ED}
-        gy = {item: gather_y(item) for item in every if item != ED}
-        gx = {item: gather_x(item) for item in FULL if item != ED}
+        gz = {item: gather_z(item) for item in every}
+        gy = {item: gather_y(item) for item in every}
+        gx = {item: gather_x(item) for item in FULL}
         gc = {item: gather_c(item) for item in FULL}
-        gx[ED], gz[ED], gy[ED] = edge_x(), edge_z(), edge_y()
 
         def pass_on(before, after, *items):
             for item in items:
@@ -900,11 +881,13 @@
         start(node_copies)
         pack_mo(0)
         first(gz, MO0)
-        pack_edge()
-        first(gx, ED)
-        pass_on(gz, gy, TB, IN0)
         pack_in(1)
         pack_mo(1)
+        first(gz, IN1, MO1)
+        pack_edge()
+        first(gz, ED)
+        pass_on(gz, gy, TB, IN0)
+        pack_ffn(0)
         pass_on(gy, gx, TB)
         make_vectors()
         wait(node_copies)
@@ -927,24 +910,22 @@
         state[0] = nodes_t + tn(refs.time_rows[...], refs.time_hot[...])
         finish = halo(0, state[0].astype(BF16))
         pass_on(gz, gy, MO0)
-        first(gz, IN1, MO1)
-        pack_ffn(0)
         first(gz, FF0)
-        pass_on(gx, gz, ED)
         make_onehot()
+        pass_on(gy, gx, MO0)
+        pass_on(gz, gy, IN1, MO1)
         pack_ffn(1)
-        pass_on(gy, gx, MO0)
-        finish()
-        pass_on(gz, gy, IN1, MO1)
         pass_on(gx, gc, IN0)
         wait(gc[IN0])
         assemble_in(0)
         pass_on(gx, gc, MO0)
         pass_on(gy, gx, IN1, MO1)
-        pass_on(gz, gy, FF0)
+        pass_on(gz, gy, ED)
         first(gz, FF1)
         wait(gc[MO0])
         assemble_mo(0)
+        finish()
+        pass_on(gy, gx, ED)
     else:
         make_vectors()
         make_onehot()
@@ -960,7 +941,7 @@
 
             @pl.when(i == 1)
             def _():
-                pass_on(gz, gy, ED)
+                pass_on(gz, gy, FF0)
 
         return 0
 
@@ -968,19 +949,19 @@
 
     def need_ffn0():
         if fast:
+            pass_on(gx, gc, IN1, MO1)
             wait(gy[FF0])
             assemble_ffn(0)
 
     def beside_branch():
         if fast:
-            pass_on(gx, gc, IN1, MO1)
-            pass_on(gy, gc, ED)
+            wait(gc[IN1])
+            assemble_in(1)
 
     finish = node_update(0, need_ffn0, beside_branch)
     if fast:
         start(late_copies)
-        wait(gc[IN1])
-        assemble_in(1)
+        pass_on(gx, gc, ED)
         wait(gc[MO1])
         assemble_mo(1)
         wait(gc[ED])
@@ -1037,6 +1018,8 @@
         return 0
 
     lax.fori_loop(0, chunks, loop_c, 0)
+    save_edges = pltpu.make_async_copy(edges_out, refs.edges_out, refs.local_sem.at[2])
+    save_edges.start()
     g_ext, g_own = edge_terms(1)
     dh = refs.all_dnodes[...].T if fast else refs.dh[...]
     dcur[...] = dh + halo_back(0, g_ext, g_own, beside_far=lambda: edge_finish(1))[...]
@@ -1114,6 +1097,12 @@
     def loop_d2(i, _):
         base = i * CHUNK
         edge_backward(0, base, lambda j: (*norm_parts(psum[base + j]), g_edges[base + j]))
+        if fast:
+
+            @pl.when(i == 1)
+            def _():
+                reduce_on(reduce_c, reduce_x, IN1)
+
         return 0
 
     lax.fori_loop(0, chunks, loop_d2, 0)
@@ -1121,22 +1110,24 @@
 
     def beside_edge():
         if fast:
-            reduce_on(reduce_c, reduce_x, IN1, MO1)
+            reduce_on(reduce_c, reduce_x, MO1)
             reduce_on(reduce_y, reduce_last, FF1)
         edge_finish(0)
         if fast:
             emit_edge_all()
+            reduce_on(reduce_x, reduce_y, IN1)
 
     dcur[...] += halo_back(1, acc_z[...] + e_ext, acc_zs[...] + e_own, beside_far=beside_edge)[...]
 
     def beside_node():
         if fast:
             start(reduce_c[ED][0])
+            reduce_on(reduce_x, reduce_y, MO1)
+            reduce_on(reduce_y, reduce_last, IN1)
 
     node_back(0, beside_node)
     clear_message()
     if fast:
-        reduce_on(reduce_x, reduce_y, IN1, MO1)
         start(reduce_y[FF0][0])
         reduce_on(reduce_c, reduce_x, ED)
 
@@ -1148,6 +1139,7 @@
     middle_finish(0)
     if fast:
         start(reduce_c[MO0][0])
+        reduce_on(reduce_y, reduce_last, MO1)
 
     def loop_e2(i, _):
         base = i * CHUNK
@@ -1162,18 +1154,18 @@
             def _():
                 reduce_on(reduce_c, reduce_x, MO0)
 
-            @pl.when(i == 2)
-            def _():
-                reduce_on(reduce_y, reduce_last, IN1, MO1)
-
         return 0
 
     lax.fori_loop(0, chunks, loop_e2, 0)
+    save_grads = pltpu.make_async_copy(g_edges, refs.g_edges, refs.local_sem.at[3])
+    save_grads.start()
     m_ext, m_own = message_terms(0)
     if not fast:
         message_finish(0)
         final = dcur[...] + halo_back(2, m_ext, m_own)[...]
         g_nodes[...] = final.T
+        save_edges.wait()
+        save_grads.wait()
         return
 
     def beside_last_core():
@@ -1250,6 +1242,8 @@
     copies, total = reduce_last[TB]
     wait(copies)
     refs.o_time[...] = total(0, plan.tb_rows)
+    save_edges.wait()
+    save_grads.wait()
 
 
 def vmem(shape, dtype):
@@ -1313,7 +1307,9 @@
         ar_tot=vmem((2, width, lanes), F32),
         send_sem=pltpu.SemaphoreType.DMA((160,)),
         recv_sem=pltpu.SemaphoreType.DMA((160,)),
-        local_sem=pltpu.SemaphoreType.DMA((2,)),
+        local_sem=pltpu.SemaphoreType.DMA((4,)),
+        edge_state=vmem((slots, ew, lanes), F32),
+        edge_grad=vmem((slots, ew, lanes), F32),
     )
     kept = dict(
         g_eint=((layers, ew, up_to(rows_in, lanes)), BF16),
@@ -1374,7 +1370,7 @@
             )
         )
     names = (*operands, *outs, *scratch)
-    in_hbm, in_smem = dict(edges=1, d_edges=1), dict(time_index=1)
+    in_hbm, in_smem = dict(edges=1, d_edges=1, edges_out=1, g_edges=1), dict(time_index=1)
     place = lambda name: pl.BlockSpec(
         memory_space=pl.ANY if name in in_hbm else pltpu.SMEM if name in in_smem else pltpu.VMEM
     )
@@ -1382,7 +1378,7 @@
         functools.partial(whole_kernel, plan, names),
         out_shape=tuple(jax.ShapeDtypeStruct(*spec) for spec in outs.values()),
         in_specs=[place(name) for name in operands],
-        out_specs=[pl.BlockSpec(memory_space=pltpu.VMEM)] * len(outs),
+        out_specs=[place(name) for name in outs],
         scratch_shapes=list(scratch.values()),
         compiler_params=pltpu.CompilerParams(
             collective_id=1, has_side_effects=True, vmem_limit_bytes=63 * 1024 * 1024
@@ -1392,15 +1388,32 @@
 
 
 def hand_over(values):
+    count = len(values)
+
     def kernel(*refs):
-        for source, result in zip(refs[: len(values)], refs[len(values) :], strict=True):
-            result[...] = source[...]
-
+        sources, results, held = refs[:count], refs[count : 2 * count], refs[2 * count : 3 * count]
+        come, go = refs[3 * count :]
+        arriving = [pltpu.make_async_copy(sources[k], held[k], come.at[k]) for k in range(count)]
+        leaving = [pltpu.make_async_copy(held[k], results[k], go.at[k]) for k in range(count)]
+        for copy in arriving:
+            copy.start()
+        for first, second in zip(arriving, leaving, strict=True):
+            first.wait()
+            second.start()
+        for copy in leaving:
+            copy.wait()
+
+    specs = [pl.BlockSpec(memory_space=pl.ANY)] * count
     return pl.pallas_call(
         kernel,
         out_shape=[jax.ShapeDtypeStruct(value.shape, value.dtype) for value in values],
-        in_specs=[pl.BlockSpec(memory_space=pltpu.VMEM)] * len(values),
-        out_specs=[pl.BlockSpec(memory_space=pltpu.VMEM)] * len(values),
+        in_specs=specs,
+        out_specs=specs,
+        scratch_shapes=[
+            *(pltpu.VMEM(value.shape, value.dtype) for value in values),
+            pltpu.SemaphoreType.DMA((count,)),
+            pltpu.SemaphoreType.DMA((count,)),
+        ],
     )(*values)
 
 

time: 232 us -> 225 us (0.970)
  Pallas kernels: 231 us -> 224 us
    pallas_call x1, Pallas kernels: 227 us -> 220 us  [run_whole(): pl.pallas_call(functools.partial(whole_kernel, plan, names), out_shape=tu...]
where the time goes in v4:
time: 225 us
  Pallas kernels  224 us (100%)
    pallas_call x1, Pallas kernels, run_whole(): pl.pallas_call(functools.partial(whole_kernel, plan, names), out_shape=tu...  220 us

profile of v4, /device:TPU:0, one launch (start us, length us, event | category | flops | bytes accessed | tf_op | source)
XLA Modules:
  0.0 224.6 jit_solution(7939691173914793533)
XLA Ops:
  0.7 220.1 %shard_map.332 = (f32[32,512]{1,0:T(8,128)}, f32[15,192,128]{2,1,0:T(8,128)}, f32[32,512]{1,0:T(8,128)}, f32[15,192,128]{2,1,0:T(8,128)}, f32[2,152,128]{2,1,0:T...) custom-call(s32[15,128]{1,0:T(8,128)} %bitcast.18, ...), custom_call_target="tpu_custom_call" | custom-call | tf_op jit(solution)/shard_map/pallas_call | solution.py:1377
  220.8 3.7 %shard_map.333 = (f32[32,512]{1,0:T(8,128)}, f32[15,192,128]{2,1,0:T(8,128)}, f32[32,512]{1,0:T(8,128)}, f32[15,192,128]{2,1,0:T(8,128)}, f32[16,128]{1,0:T(8,12...) custom-call(f32[32,512]{1,0:T(8,128)} %get-tuple-element.51.refs_0_,, ...), custom_call_target="tpu_custom_call" | custom-call | tf_op jit(solution)/shard_map/pallas_call | solution.py:1407

commit v5 on v4

--- a/solution.py
+++ b/solution.py
@@ -1168,10 +1168,6 @@
         save_grads.wait()
         return
 
-    def beside_last_core():
-        message_finish(0)
-        start(reduce_c[IN0][0])
-
     sums = refs.vec_sums
     partners = [(r, buddy), (r, across), y_peer]
     partners += [(2 * (zz + 1 - 2 * lax.rem(zz, 2)) + yy, n), (2 * lax.rem(zz + 2, 4) + yy, n)]
@@ -1184,6 +1180,10 @@
             rounds[k + 1].start()
 
     def beside_last_far():
+        reduce_on(reduce_y, reduce_last, FF0)
+        message_finish(0)
+        start(reduce_c[IN0][0])
+        reduce_on(reduce_x, reduce_y, MO0, ED)
         table = refs.g_vec[...].T
         sums[0] = jnp.zeros_like(sums[0])
         for layer in range(2):
@@ -1197,13 +1197,11 @@
                     sums[0, at : at + 1] = value * scale
         rounds[0].start()
         reduce_on(reduce_c, reduce_x, IN0)
-        reduce_on(reduce_y, reduce_last, FF0)
-        reduce_on(reduce_x, reduce_y, MO0, ED)
         vec_round(0)
         put_ffn(1)
         put_message(1)
 
-    final = dcur[...] + halo_back(2, m_ext, m_own, beside_last_core, beside_last_far)[...]
+    final = dcur[...] + halo_back(2, m_ext, m_own, beside_far=beside_last_far)[...]
     high = final.astype(BF16)
     low = (final - high.astype(F32)).astype(BF16)
     g_times = (nt(refs.time_hot[...], high) + nt(refs.time_hot[...], low)) * (1.0 / plan.nbr_total)
@@ -1214,14 +1212,14 @@
         ].astype(BF16)
     start(reduce_c[TB][0])
     vec_round(1)
+    reduce_on(reduce_y, reduce_last, MO0, ED)
     reduce_on(reduce_x, reduce_y, IN0)
     reduce_on(reduce_c, reduce_x, TB)
     refs.all_dnodes[...] = final.T
     g_nodes[...] = refs.all_dnodes[pl.ds(mine, own_rows)]
-    reduce_on(reduce_y, reduce_last, MO0)
     vec_round(2)
     reduce_on(reduce_x, reduce_y, TB)
-    reduce_on(reduce_y, reduce_last, IN0, ED)
+    reduce_on(reduce_y, reduce_last, IN0)
     vec_round(3)
     put_ffn(0)
     reduce_on(reduce_y, reduce_last, TB)

time: 225 us -> 221 us (0.982)
  Pallas kernels: 224 us -> 220 us
    pallas_call x1, Pallas kernels: 220 us -> 217 us  [run_whole(): pl.pallas_call(functools.partial(whole_kernel, plan, names), out_shape=tu...]
where the time goes in v5:
time: 221 us
  Pallas kernels  220 us (100%)
    pallas_call x1, Pallas kernels, run_whole(): pl.pallas_call(functools.partial(whole_kernel, plan, names), out_shape=tu...  217 us

profile of v5, /device:TPU:0, one launch (start us, length us, event | category | flops | bytes accessed | tf_op | source)
XLA Modules:
  0.0 221.2 jit_solution(8539529870710943159)
XLA Ops:
  0.7 216.7 %shard_map.332 = (f32[32,512]{1,0:T(8,128)}, f32[15,192,128]{2,1,0:T(8,128)}, f32[32,512]{1,0:T(8,128)}, f32[15,192,128]{2,1,0:T(8,128)}, f32[2,152,128]{2,1,0:T...) custom-call(s32[15,128]{1,0:T(8,128)} %bitcast.18, ...), custom_call_target="tpu_custom_call" | custom-call | tf_op jit(solution)/shard_map/pallas_call | solution.py:1375
  217.3 3.7 %shard_map.333 = (f32[32,512]{1,0:T(8,128)}, f32[15,192,128]{2,1,0:T(8,128)}, f32[32,512]{1,0:T(8,128)}, f32[15,192,128]{2,1,0:T(8,128)}, f32[16,128]{1,0:T(8,12...) custom-call(f32[32,512]{1,0:T(8,128)} %get-tuple-element.51.refs_0_,, ...), custom_call_target="tpu_custom_call" | custom-call | tf_op jit(solution)/shard_map/pallas_call | solution.py:1405
